TPU v7x, 32 devices: a whole 2x2x4 slice. The times are simulated.
32 devices in a mesh: wide: 8 (over z, y), narrow: 4 (over x, core).
Axes of the slice: x: 2, y: 2, z: 4, core: 2. Of those that a mesh axis runs over, the one named last changes fastest.
Arguments:
- features: float32 [8192, 602], P(('wide', 'narrow')), may hold values from -6 to 6
- adjacency: int32 [8192, 8192], P('wide', 'narrow'), may hold values from 0 to 1, as said below
- labels: int32 [8192, 121], P(('wide', 'narrow')), may hold values 0 or 1
- labelled: int32 [8192], P(('wide', 'narrow')), may hold values from 0 to 1, as said below
- node_count: int32 [8192], P(('wide', 'narrow')), may hold values from 1 to 8
- w_in: float32 [602, 512], P(None, ('wide', 'narrow')), may hold values from -0.25 to 0.25
- w_side: float32 [3, 1024, 512], P(None, ('wide', 'narrow')), may hold values from -0.25 to 0.25
- w_proj: float32 [3, 1024, 512], P(None, ('wide', 'narrow')), may hold values from -0.1875 to 0.1875
- w_out: float32 [512, 121], P(('wide', 'narrow')), may hold values from -0.25 to 0.25
- row_in: float32 [602], replicated, may hold values from 8.5449216e-08 to 3.4179686e-07
- col_in: float32 [512], P(('wide', 'narrow')), may hold values from 8.5449216e-08 to 3.4179686e-07
- row_side: float32 [3, 1024], P(None, ('wide', 'narrow')), may hold values from 1.8310547e-07 to 7.324219e-07
- col_side: float32 [3, 512], replicated, may hold values from 1.8310547e-07 to 7.324219e-07
- row_proj: float32 [3, 1024], P(None, ('wide', 'narrow')), may hold values from 6.1035155e-07 to 2.4414062e-06
- col_proj: float32 [3, 512], replicated, may hold values from 6.1035155e-07 to 2.4414062e-06
- row_out: float32 [512], P(('wide', 'narrow')), may hold values from 2.4414063e-05 to 9.765625e-05
- col_out: float32 [121], replicated, may hold values from 2.4414063e-05 to 9.765625e-05
Outputs:
- loss_sum: float32 [], replicated
- label_count: float32 [], replicated
- grad_in: float32 [602, 512], P(None, ('wide', 'narrow'))
- grad_side: float32 [3, 1024, 512], P(None, ('wide', 'narrow'))
- grad_proj: float32 [3, 1024, 512], P(None, ('wide', 'narrow'))
- grad_out: float32 [512, 121], P(('wide', 'narrow'))
- new_in: float32 [602, 512], P(None, ('wide', 'narrow'))
- new_side: float32 [3, 1024, 512], P(None, ('wide', 'narrow'))
- new_proj: float32 [3, 1024, 512], P(None, ('wide', 'narrow'))
- new_out: float32 [512, 121], P(('wide', 'narrow'))
- new_row_in: float32 [602], replicated
- new_col_in: float32 [512], P(('wide', 'narrow'))
- new_row_side: float32 [3, 1024], P(None, ('wide', 'narrow'))
- new_col_side: float32 [3, 512], replicated
- new_row_proj: float32 [3, 1024], P(None, ('wide', 'narrow'))
- new_col_proj: float32 [3, 512], replicated
- new_row_out: float32 [512], P(('wide', 'narrow'))
- new_col_out: float32 [121], replicated
Inputs may be any that keep to these rules, and one draw needn't show every extreme that they name: `adjacency`: each row has a drawn edge density; every row and column of a block may hold edges. The last node is labelled.
All inputs are finite; a program needn't handle non-finite values. No bound on the sum of `labels` on one device may be relied on, other than what follows from the above.
Results may differ from a plain program's by a relative error of at most 0.0003.
Values sent between devices are 32-bit elements; how exact they have to be, the bound alone decides.
A program may use at most 192 MiB of HBM per device.

v0:
```python
import jax
import jax.numpy as jnp
from jax import lax
from jax.sharding import PartitionSpec as P

norm_eps = 1e-06
stat_eps = 1e-30
clip_level = 0.5
step_rate = 0.04


def matmul(left, right):
    return jnp.dot(left, right, precision=lax.Precision.HIGHEST, preferred_element_type=jnp.float32)


def left_t(left, right):
    return lax.dot_general(
        left,
        right,
        (((0,), (0,)), ((), ())),
        precision=lax.Precision.HIGHEST,
        preferred_element_type=jnp.float32,
    )


def right_t(left, right):
    return lax.dot_general(
        left,
        right,
        (((1,), (1,)), ((), ())),
        precision=lax.Precision.HIGHEST,
        preferred_element_type=jnp.float32,
    )


def forward_layer(hidden, side, proj, adj_float, degree, alpha):
    width = side.shape[1]
    sent = alpha[:, None] * hidden
    gathered = lax.all_gather(sent, "wide", axis=0, tiled=True)
    summed = lax.psum_scatter(
        matmul(adj_float, gathered), "narrow", scatter_dimension=0, tiled=True
    )
    agg = summed / degree[:, None]
    joined = jnp.concatenate([matmul(hidden, side[:width]), matmul(agg, side[width:])], 1)
    pre_act = matmul(joined, proj)
    act = jax.nn.silu(pre_act)
    scaled = act * lax.rsqrt(jnp.mean(act * act, -1, keepdims=True) + norm_eps)
    return (scaled, (hidden, agg, joined, pre_act))


def backward_layer(d_out, kept, side, proj, adj_float, degree, alpha):
    hidden, agg, joined, pre_act = kept
    width = side.shape[1]
    sig = jax.nn.sigmoid(pre_act)
    act = pre_act * sig
    scale = lax.rsqrt(jnp.mean(act * act, -1, keepdims=True) + norm_eps)
    normed = act * scale
    d_act = scale * (d_out - normed * jnp.mean(d_out * normed, -1, keepdims=True))
    d_pre = d_act * sig * (1.0 + pre_act * (1.0 - sig))
    g_proj = left_t(joined, d_pre)
    d_joined = right_t(d_pre, proj)
    d_self = d_joined[:, :width]
    d_neigh = d_joined[:, width:]
    g_side = jnp.concatenate([left_t(hidden, d_self), left_t(agg, d_neigh)], 0)
    d_hidden = right_t(d_self, side[:width])
    d_summed = right_t(d_neigh, side[width:]) / degree[:, None]
    every_row = lax.all_gather(d_summed, "narrow", axis=0, tiled=True)
    d_sent = lax.psum_scatter(left_t(adj_float, every_row), "wide", scatter_dimension=0, tiled=True)
    return (d_hidden + alpha[:, None] * d_sent, g_side, g_proj)


def shards(
    features,
    adjacency,
    labels,
    labelled,
    node_count,
    w_in,
    w_side,
    w_proj,
    w_out,
    row_in,
    col_in,
    row_side,
    col_side,
    row_proj,
    col_proj,
    row_out,
    col_out,
):
    layers = w_side.shape[0]
    width = w_side.shape[2]
    in_width = features.shape[1]
    classes = w_out.shape[1]
    adj_float = adjacency.astype(jnp.float32)
    degree = 1.0 + lax.psum_scatter(
        jnp.sum(adj_float, 1), "narrow", scatter_dimension=0, tiled=True
    )
    counts = node_count.astype(jnp.float32)
    alpha = 2.0 / (1.0 + counts)
    lam = lax.rsqrt(counts)
    target = labels.astype(jnp.float32)
    weight_mask = labelled.astype(jnp.float32)
    full_in, full_side, full_proj, full_out = (
        lax.all_gather(w_in, ("wide", "narrow"), axis=1, tiled=True),
        lax.all_gather(w_side, ("wide", "narrow"), axis=1, tiled=True),
        lax.all_gather(w_proj, ("wide", "narrow"), axis=1, tiled=True),
        lax.all_gather(w_out, ("wide", "narrow"), axis=0, tiled=True),
    )
    hidden = matmul(features, full_in)
    kept_all = []
    for layer in range(layers):
        hidden, kept = forward_layer(
            hidden, full_side[layer], full_proj[layer], adj_float, degree, alpha
        )
        kept_all.append(kept)
    logits = matmul(hidden, full_out)
    per = jnp.sum(jax.nn.softplus(logits) - target * logits, -1)
    loss_sum, label_count = lax.psum(
        (jnp.sum(weight_mask * lam * per), jnp.sum(weight_mask)), ("wide", "narrow")
    )
    d_logits = (weight_mask * lam / label_count)[:, None] * (jax.nn.sigmoid(logits) - target)
    g_out = left_t(hidden, d_logits)
    d_hidden = right_t(d_logits, full_out)
    side_grads = [None] * layers
    proj_grads = [None] * layers
    for layer in reversed(range(layers)):
        d_hidden, g_side, g_proj = backward_layer(
            d_hidden, kept_all[layer], full_side[layer], full_proj[layer], adj_float, degree, alpha
        )
        side_grads[layer], proj_grads[layer] = (g_side, g_proj)
    g_in = left_t(features, d_hidden)
    red_in, red_side, red_proj, red_out = (
        lax.psum_scatter(g_in, ("wide", "narrow"), scatter_dimension=1, tiled=True),
        lax.psum_scatter(
            jnp.stack(side_grads), ("wide", "narrow"), scatter_dimension=1, tiled=True
        ),
        lax.psum_scatter(
            jnp.stack(proj_grads), ("wide", "narrow"), scatter_dimension=1, tiled=True
        ),
        lax.psum_scatter(g_out, ("wide", "narrow"), scatter_dimension=0, tiled=True),
    )
    sq_in = red_in * red_in
    sq_side = red_side * red_side
    sq_proj = red_proj * red_proj
    sq_out = red_out * red_out
    new_col_in = 0.5 * col_in + 0.5 * (jnp.mean(sq_in, 0) + stat_eps)
    new_row_side = 0.5 * row_side + 0.5 * (jnp.mean(sq_side, 2) + stat_eps)
    new_row_proj = 0.5 * row_proj + 0.5 * (jnp.mean(sq_proj, 2) + stat_eps)
    new_row_out = 0.5 * row_out + 0.5 * (jnp.mean(sq_out, 1) + stat_eps)
    sum_row_in, sum_col_side, sum_col_proj, sum_col_out, total_side, total_proj, total_out = (
        lax.psum(
            (
                jnp.sum(sq_in, 1),
                jnp.sum(sq_side, 1),
                jnp.sum(sq_proj, 1),
                jnp.sum(sq_out, 0),
                jnp.sum(new_row_side, 1),
                jnp.sum(new_row_proj, 1),
                jnp.sum(new_row_out),
            ),
            ("wide", "narrow"),
        )
    )
    new_row_in = 0.5 * row_in + 0.5 * (sum_row_in / width + stat_eps)
    new_col_side = 0.5 * col_side + 0.5 * (sum_col_side / (2 * width) + stat_eps)
    new_col_proj = 0.5 * col_proj + 0.5 * (sum_col_proj / (2 * width) + stat_eps)
    new_col_out = 0.5 * col_out + 0.5 * (sum_col_out / width + stat_eps)
    mean_in = jnp.mean(new_row_in)
    mean_side = total_side / (2 * width)
    mean_proj = total_proj / (2 * width)
    mean_out = total_out / width
    up_in = red_in * lax.rsqrt(new_row_in[:, None] * new_col_in[None, :] / mean_in)
    up_side = red_side * lax.rsqrt(
        new_row_side[:, :, None] * new_col_side[:, None, :] / mean_side[:, None, None]
    )
    up_proj = red_proj * lax.rsqrt(
        new_row_proj[:, :, None] * new_col_proj[:, None, :] / mean_proj[:, None, None]
    )
    up_out = red_out * lax.rsqrt(new_row_out[:, None] * new_col_out[None, :] / mean_out)
    sq_up_in, sq_up_side, sq_up_proj, sq_up_out = lax.psum(
        (
            jnp.sum(up_in * up_in),
            jnp.sum(up_side * up_side, (1, 2)),
            jnp.sum(up_proj * up_proj, (1, 2)),
            jnp.sum(up_out * up_out),
        ),
        ("wide", "narrow"),
    )
    fac_in = 1.0 / jnp.maximum(1.0, jnp.sqrt(sq_up_in / (in_width * width)) / clip_level)
    fac_side = 1.0 / jnp.maximum(1.0, jnp.sqrt(sq_up_side / (2 * width * width)) / clip_level)
    fac_proj = 1.0 / jnp.maximum(1.0, jnp.sqrt(sq_up_proj / (2 * width * width)) / clip_level)
    fac_out = 1.0 / jnp.maximum(1.0, jnp.sqrt(sq_up_out / (width * classes)) / clip_level)
    new_in = w_in - step_rate * (up_in * fac_in)
    new_side = w_side - step_rate * (up_side * fac_side[:, None, None])
    new_proj = w_proj - step_rate * (up_proj * fac_proj[:, None, None])
    new_out = w_out - step_rate * (up_out * fac_out)
    return (
        loss_sum,
        label_count,
        red_in,
        red_side,
        red_proj,
        red_out,
        new_in,
        new_side,
        new_proj,
        new_out,
        new_row_in,
        new_col_in,
        new_row_side,
        new_col_side,
        new_row_proj,
        new_col_proj,
        new_row_out,
        new_col_out,
    )


def solution(mesh):
    in_specs = (
        P(("wide", "narrow"), None),
        P("wide", "narrow"),
        P(("wide", "narrow"), None),
        P(("wide", "narrow")),
        P(("wide", "narrow")),
        P(None, ("wide", "narrow")),
        P(None, ("wide", "narrow"), None),
        P(None, ("wide", "narrow"), None),
        P(("wide", "narrow"), None),
        P(),
        P(("wide", "narrow")),
        P(None, ("wide", "narrow")),
        P(),
        P(None, ("wide", "narrow")),
        P(),
        P(("wide", "narrow")),
        P(),
    )
    out_specs = (
        P(),
        P(),
        P(None, ("wide", "narrow")),
        P(None, ("wide", "narrow"), None),
        P(None, ("wide", "narrow"), None),
        P(("wide", "narrow"), None),
        P(None, ("wide", "narrow")),
        P(None, ("wide", "narrow"), None),
        P(None, ("wide", "narrow"), None),
        P(("wide", "narrow"), None),
        P(),
        P(("wide", "narrow")),
        P(None, ("wide", "narrow")),
        P(),
        P(None, ("wide", "narrow")),
        P(),
        P(("wide", "narrow")),
        P(),
    )
    return jax.shard_map(shards, mesh=mesh, in_specs=in_specs, out_specs=out_specs, check_vma=False)
```

profile of v0, /device:TPU:0, one launch (start us, length us, event | category | flops | bytes accessed | tf_op | source)
XLA Modules:
  0.0 1736.8 jit_solution(7089782297140739265)
XLA Ops:
  8.7 59.2 %all-gather.10.cloned.1.call-done = f32[602,512]{0,1:T(8,128)} async-done(((f32[602,16]{0,1:T(8,128)}), f32[602,512]{0,1:T(8,128)}) %all-gather.10.cloned.1.call-update) | async-done | bytes 1232912 | tf_op jit(solution)/shard_map/all_gather | solution.py:105
  67.9 4.4 broadcast_multiply_fusion
  73.2 71.7 %all-gather.14.cloned.1.call-done = f32[2048,512]{1,0:T(8,128)} async-done(((f32[256,512]{1,0:T(8,128)}), f32[2048,512]{1,0:T(8,128)}) %all-gather.14.cloned.1.call-update) | async-done | bytes 4194320 | tf_op jit(solution)/shard_map/all_gather | solution.py:39
  144.9 31.4 %fusion.27 = f32[1024,512]{0,1:T(8,128)} fusion(f32[2048,512]{1,0:T(8,128)} %all-gather.14.cloned.1.call-done, s32[1024,2048]{1,0:T(8,128)} %param.18), kind=kOutput, calls=%fused_computation.33 | convolution fusion | flops 12886999040 | bytes 14680064 | tf_op jit(solution)/shard_map/dot_general | solution.py:13
  178.2 4.0 convert_reduce_fusion
  182.2 6.1 all-reduce
  188.4 26.8 %all-gather.12.cloned.1.call-done = f32[3,1024,512]{2,1,0:T(8,128)} async-done(((f32[3,32,512]{2,1,0:T(8,128)}), f32[3,1024,512]{2,1,0:T(8,128)}) %all-gather.12.cloned.1.call-update) | async-done | bytes 6291472 | tf_op jit(solution)/shard_map/all_gather | solution.py:106
  217.5 30.5 %reduce-scatter.13.cloned.1.call-done = f32[256,512]{0,1:T(8,128)} async-done(((f32[1024,512]{0,1:T(8,128)}), f32[256,512]{0,1:T(8,128)}) %reduce-scatter.13.cloned.1.call-update) | async-done | bytes 524304 | tf_op jit(solution)/shard_map/reduce_scatter | solution.py:40
  247.9 2.5 fusion.37
  250.4 69.8 %all-gather.16.cloned.1.call-done = f32[3,1024,512]{2,1,0:T(8,128)} async-done(((f32[3,32,512]{2,1,0:T(8,128)}), f32[3,1024,512]{2,1,0:T(8,128)}) %all-gather.16.cloned.1.call-update) | async-done | bytes 6291472 | tf_op jit(solution)/shard_map/all_gather | solution.py:107
  320.2 3.7 multiply_reduce_fusion.5
  325.0 72.4 %all-gather.18.cloned.1.call-done = f32[2048,512]{1,0:T(8,128)} async-done(((f32[256,512]{1,0:T(8,128)}), f32[2048,512]{1,0:T(8,128)}) %all-gather.18.cloned.1.call-update) | async-done | bytes 4194320 | tf_op jit(solution)/shard_map/all_gather | solution.py:39
  397.4 31.0 %fusion.30 = f32[1024,512]{0,1:T(8,128)} fusion(f32[2048,512]{1,0:T(8,128)} %all-gather.18.cloned.1.call-done, s32[1024,2048]{1,0:T(8,128)} %param.18), kind=kOutput, calls=%fused_computation.34 | convolution fusion | flops 12886999040 | bytes 14680064 | tf_op jit(solution)/shard_map/dot_general | solution.py:13
  430.9 27.4 %reduce-scatter.15.cloned.1.call-done = f32[256,512]{0,1:T(8,128)} async-done(((f32[1024,512]{0,1:T(8,128)}), f32[256,512]{0,1:T(8,128)}) %reduce-scatter.15.cloned.1.call-update) | async-done | bytes 524304 | tf_op jit(solution)/shard_map/reduce_scatter | solution.py:40
  460.7 3.9 multiply_reduce_fusion.4
  465.8 73.5 %all-gather.20.cloned.1.call-done = f32[2048,512]{1,0:T(8,128)} async-done(((f32[256,512]{1,0:T(8,128)}), f32[2048,512]{1,0:T(8,128)}) %all-gather.20.cloned.1.call-update) | async-done | bytes 4194320 | tf_op jit(solution)/shard_map/all_gather | solution.py:39
  539.3 31.2 %fusion.33 = f32[1024,512]{0,1:T(8,128)} fusion(f32[2048,512]{1,0:T(8,128)} %all-gather.20.cloned.1.call-done, s32[1024,2048]{1,0:T(8,128)} %param.18), kind=kOutput, calls=%fused_computation.35 | convolution fusion | flops 12886999040 | bytes 14680064 | tf_op jit(solution)/shard_map/dot_general | solution.py:13
  570.7 39.8 %all_gather.36 = f32[512,121]{1,0:T(8,128)S(1)} all-gather(f32[16,121]{1,0:T(8,128)S(1)} %copy-done.17), channel_id=1, replica_groups=mesh['wide'=8,'narrow'=4] {'wide','narrow'}, dimensions={0}, use_global_device_ids=true | all-gather | bytes 255552 | tf_op jit(solution)/shard_map/all_gather | solution.py:108
  610.5 3.2 fusion.40
  613.7 2.5 fusion.41
  616.2 4.0 multiply_reduce_fusion.3
  621.8 37.1 %psum.92 = f32[]{:T(128)} all-reduce(f32[]{:T(128)} %get-tuple-element.80), channel_id=1, replica_groups=mesh['wide'=8,'narrow'=4] {'wide','narrow'}, use_global_device_ids=true, to_apply=%region_12.13 | all-reduce | flops 1 | bytes 8 | tf_op jit(solution)/shard_map/psum | solution.py:119
  662.2 3.9 fusion.25
  666.1 3.4 convolution_divide_fusion.2
  669.5 23.3 %all-gather.22.cloned.1.call-done = f32[1024,512]{0,1:T(8,128)} async-done(((f32[256,512]{0,1:T(8,128)}), f32[1024,512]{0,1:T(8,128)}) %all-gather.22.cloned.1.call-update) | async-done | bytes 2097168 | tf_op jit(solution)/shard_map/all_gather | solution.py:67
  692.9 17.8 %fusion.12 = f32[2048,512]{1,0:T(8,128)} fusion(f32[1024,512]{0,1:T(8,128)} %all-gather.22.cloned.1.call-done, s32[1024,2048]{1,0:T(8,128)} %param.18), kind=kOutput, calls=%fused_computation.15 | convolution fusion | flops 12886999040 | bytes 14680064 | tf_op jit(solution)/shard_map/dot_general | solution.py:17
  710.7 88.0 %reduce-scatter.19.cloned.1.call-done = f32[256,512]{1,0:T(8,128)} async-done(((f32[2048,512]{1,0:T(8,128)}), f32[256,512]{1,0:T(8,128)}) %reduce-scatter.19.cloned.1.call-update) | async-done | bytes 524304 | tf_op jit(solution)/shard_map/reduce_scatter | solution.py:68
  798.8 2.7 multiply_reduce_fusion.1
  802.3 3.7 fusion.23
  806.0 3.4 convolution_divide_fusion.1
  809.5 22.4 %all-gather.24.cloned.1.call-done = f32[1024,512]{0,1:T(8,128)} async-done(((f32[256,512]{0,1:T(8,128)}), f32[1024,512]{0,1:T(8,128)}) %all-gather.24.cloned.1.call-update) | async-done | bytes 2097168 | tf_op jit(solution)/shard_map/all_gather | solution.py:67
  832.0 18.0 %fusion.15 = f32[2048,512]{1,0:T(8,128)} fusion(f32[1024,512]{0,1:T(8,128)} %all-gather.24.cloned.1.call-done, s32[1024,2048]{1,0:T(8,128)} %param.18), kind=kOutput, calls=%fused_computation.16 | convolution fusion | flops 12886999040 | bytes 14680064 | tf_op jit(solution)/shard_map/dot_general | solution.py:17
  850.1 88.2 %reduce-scatter.21.cloned.1.call-done = f32[256,512]{1,0:T(8,128)} async-done(((f32[2048,512]{1,0:T(8,128)}), f32[256,512]{1,0:T(8,128)}) %reduce-scatter.21.cloned.1.call-update) | async-done | bytes 524304 | tf_op jit(solution)/shard_map/reduce_scatter | solution.py:68
  938.2 2.7 multiply_reduce_fusion
  941.0 3.9 fusion.21
  945.9 3.1 convolution_divide_fusion
  949.0 22.5 %all-gather.26.cloned.1.call-done = f32[1024,512]{0,1:T(8,128)} async-done(((f32[256,512]{0,1:T(8,128)}), f32[1024,512]{0,1:T(8,128)}) %all-gather.26.cloned.1.call-update) | async-done | bytes 2097168 | tf_op jit(solution)/shard_map/all_gather | solution.py:67
  971.5 17.8 %fusion.18 = f32[2048,512]{1,0:T(8,128)} fusion(f32[1024,512]{0,1:T(8,128)} %all-gather.26.cloned.1.call-done, s32[1024,2048]{1,0:T(8,128)} %param.18), kind=kOutput, calls=%fused_computation.17 | convolution fusion | flops 12886999040 | bytes 14680064 | tf_op jit(solution)/shard_map/dot_general | solution.py:17
  1002.0 3.4 pad_maximum_fusion
  1005.8 3.8 convolution_bitcast_fusion
  1014.0 3.3 pad_maximum_fusion.1
  1017.4 60.2 %reduce-scatter.23.cloned.1.call-done = f32[256,512]{1,0:T(8,128)} async-done(((f32[2048,512]{1,0:T(8,128)}), f32[256,512]{1,0:T(8,128)}) %reduce-scatter.23.cloned.1.call-update) | async-done | bytes 524304 | tf_op jit(solution)/shard_map/reduce_scatter | solution.py:68
  1082.8 131.0 %reduce-scatter.29.cloned.1.call-done = f32[16,121]{1,0:T(8,128)} async-done(((f32[512,121]{1,0:T(8,128)}), f32[16,121]{1,0:T(8,128)}) %reduce-scatter.29.cloned.1.call-update) | async-done | bytes 7760 | tf_op jit(solution)/shard_map/reduce_scatter | solution.py:141
  1215.3 142.2 %reduce-scatter.25.cloned.1.call-done = f32[3,32,512]{2,1,0:T(8,128)} async-done(((f32[3,1024,512]{2,1,0:T(8,128)}), f32[3,32,512]{2,1,0:T(8,128)}) %reduce-scatter.25.cloned.1.call-update) | async-done | bytes 196624 | tf_op jit(solution)/shard_map/reduce_scatter | solution.py:135
  1358.5 142.6 %reduce-scatter.27.cloned.1.call-done = f32[3,32,512]{2,1,0:T(8,128)} async-done(((f32[3,1024,512]{2,1,0:T(8,128)}), f32[3,32,512]{2,1,0:T(8,128)}) %reduce-scatter.27.cloned.1.call-update) | async-done | bytes 196624 | tf_op jit(solution)/shard_map/reduce_scatter | solution.py:138
  1502.5 132.7 %reduce-scatter.31.cloned.1.call-done = f32[16,602]{1,0:T(8,128)} async-done(((f32[512,602]{1,0:T(8,128)}), f32[16,602]{1,0:T(8,128)}) %reduce-scatter.31.cloned.1.call-update) | async-done | bytes 38544
  1636.3 37.5 %all-reduce.2 = (f32[602]{0:T(1024)S(1)}, f32[3]{0:T(128)S(1)}, f32[3,512]{1,0:T(4,128)S(1)}, f32[3]{0:T(128)S(1)}, f32[3,512]{1,0:T(4,128)S(1)}, /*index=5*/f32[]{:T(128)}, f32[121]{0:T(128)S(1)}) all-reduce(f32[602]{0:T(1024)S(1)} %get-tuple-element.73, ...), channel_id=1, replica_groups=mesh['wide'=8,'narrow'=4] {'wide','narrow'}, use_global_device_ids=true, to_apply=%region_24.25 | all-reduce | flops 3802 | bytes 30416 | tf_op jit(solution)/shard_map/psum | solution.py:152
  1680.9 41.2 %all-reduce.1 = (f32[]{:T(128)}, f32[]{:T(128)}, f32[3]{0:T(128)S(1)}, f32[3]{0:T(128)S(1)}, f32[]{:T(128)}) all-reduce(f32[]{:T(128)} %get-tuple-element.81, f32[]{:T(128)} %multiply_reduce_fusion.14, f32[3]{0:T(128)S(1)} %multiply_reduce_fusion.9, ...), channel_id=1, replica_groups=mesh['wide'=8,'narrow'=4] {'wide','narrow'}, use_global_device_ids=true, to_apply=%region_10.11 | all-reduce | flops 9 | bytes 72 | tf_op jit(solution)/shard_map/psum | solution.py:119
  (202 shorter events, 59.4 us)
Async XLA Ops:
  7.2 60.7 %copy-start = (f32[256,602]{0,1:T(8,128)S(1)}, f32[256,602]{0,1:T(8,128)}, u32[]{:S(2)}) copy-start(f32[256,602]{0,1:T(8,128)} %param.17) | copy-start | bytes 1849348
  7.2 60.7 %all-gather.10.cloned.1.call-start = ((), (), s32[]{:S(2)}) async-start(), calls=%async_computation.10 | async-start | bytes 1351680 | tf_op jit(solution)/shard_map/all_gather | solution.py:105
  7.9 137.0 %all-gather.14.cloned.1.call-start = ((), (), s32[]{:S(2)}) async-start(), calls=%async_computation.12 | async-start | bytes 4718592 | tf_op jit(solution)/shard_map/all_gather | solution.py:39
  72.4 142.8 %all-gather.12.cloned.1.call-start = ((), (), s32[]{:S(2)}) async-start(), calls=%async_computation.11 | async-start | bytes 6488064 | tf_op jit(solution)/shard_map/all_gather | solution.py:106
  73.1 103.9 %copy-start.38 = (u32[32]{0:T(128)S(1)}, u32[32]{0:T(128)}, u32[]{:S(2)}) copy-start(u32[32]{0:T(128)} %constant.88) | copy-start | bytes 388
  73.1 174.8 %reduce-scatter.13.cloned.1.call-start = ((), (), s32[]{:S(2)}) async-start(), calls=%async_computation.13 | async-start | bytes 2621440 | tf_op jit(solution)/shard_map/reduce_scatter | solution.py:40
  176.3 143.9 %all-gather.16.cloned.1.call-start = ((), (), s32[]{:S(2)}) async-start(), calls=%async_computation.14 | async-start | bytes 6488064 | tf_op jit(solution)/shard_map/all_gather | solution.py:107
  176.9 220.5 %all-gather.18.cloned.1.call-start = ((), (), s32[]{:S(2)}) async-start(), calls=%async_computation.15 | async-start | bytes 4718592 | tf_op jit(solution)/shard_map/all_gather | solution.py:39
  217.5 107.5 %copy-start.10 = (f32[256,512]{1,0:T(8,128)}, f32[256,512]{1,0:T(8,128)S(1)}, u32[]{:S(2)}) copy-start(f32[256,512]{1,0:T(8,128)S(1)} %fusion.36) | copy-start | bytes 1572868
  250.4 178.0 %copy-start.39 = (f32[256,512]{1,0:T(8,128)}, f32[256,512]{1,0:T(8,128)S(1)}, u32[]{:S(2)}) copy-start(f32[256,512]{1,0:T(8,128)S(1)} %fusion.37) | copy-start | bytes 1572868
  323.9 617.1 %copy-start.6 = (f32[256,512]{1,0:T(8,128)}, f32[256,512]{1,0:T(8,128)S(1)}, u32[]{:S(2)}) copy-start(f32[256,512]{1,0:T(8,128)S(1)} %get-tuple-element.105) | copy-start | bytes 1572868
  324.9 133.3 %reduce-scatter.15.cloned.1.call-start = ((), (), s32[]{:S(2)}) async-start(), calls=%async_computation.16 | async-start | bytes 2621440 | tf_op jit(solution)/shard_map/reduce_scatter | solution.py:40
  428.4 110.9 %all-gather.20.cloned.1.call-start = ((), (), s32[]{:S(2)}) async-start(), calls=%async_computation.17 | async-start | bytes 4718592 | tf_op jit(solution)/shard_map/all_gather | solution.py:39
  464.6 524.8 %copy-start.8 = (f32[256,512]{1,0:T(8,128)}, f32[256,512]{1,0:T(8,128)S(1)}, u32[]{:S(2)}) copy-start(f32[256,512]{1,0:T(8,128)S(1)} %get-tuple-element.107) | copy-start | bytes 1572868
  465.7 104.9 %copy-start.13 = (s32[256,121]{1,0:T(8,128)S(1)}, s32[256,121]{1,0:T(8,128)}, u32[]{:S(2)}) copy-start(s32[256,121]{1,0:T(8,128)} %param.19) | copy-start | bytes 371716
  465.7 105.0 %copy-start.17 = (f32[16,121]{1,0:T(8,128)S(1)}, f32[16,121]{1,0:T(8,128)}, u32[]{:S(2)}) copy-start(f32[16,121]{1,0:T(8,128)} %param.25) | copy-start | bytes 23236
  465.7 147.9 %reduce-scatter.17.cloned.1.call-start = ((), (), s32[]{:S(2)}) async-start(), calls=%async_computation.18 | async-start | bytes 2621440 | tf_op jit(solution)/shard_map/reduce_scatter | solution.py:40
  570.5 122.3 %all-gather.22.cloned.1.call-start = ((), (), s32[]{:S(2)}) async-start(), calls=%async_computation.19 | async-start | bytes 2621440 | tf_op jit(solution)/shard_map/all_gather | solution.py:67
  616.1 45.2 %copy-start.43 = (f32[256,512]{1,0:T(8,128)}, f32[256,512]{1,0:T(8,128)S(1)}, u32[]{:S(2)}) copy-start(f32[256,512]{1,0:T(8,128)S(1)} %fusion.41) | copy-start | bytes 1572868
  669.5 129.3 %reduce-scatter.19.cloned.1.call-start = ((), (), s32[]{:S(2)}) async-start(), calls=%async_computation.20 | async-start | bytes 4718592 | tf_op jit(solution)/shard_map/reduce_scatter | solution.py:68
  710.7 121.3 %all-gather.24.cloned.1.call-start = ((), (), s32[]{:S(2)}) async-start(), calls=%async_computation.21 | async-start | bytes 2621440 | tf_op jit(solution)/shard_map/all_gather | solution.py:67
  809.5 128.8 %reduce-scatter.21.cloned.1.call-start = ((), (), s32[]{:S(2)}) async-start(), calls=%async_computation.22 | async-start | bytes 4718592 | tf_op jit(solution)/shard_map/reduce_scatter | solution.py:68
  850.0 121.5 %all-gather.26.cloned.1.call-start = ((), (), s32[]{:S(2)}) async-start(), calls=%async_computation.23 | async-start | bytes 2621440 | tf_op jit(solution)/shard_map/all_gather | solution.py:67
  949.0 128.6 %reduce-scatter.23.cloned.1.call-start = ((), (), s32[]{:S(2)}) async-start(), calls=%async_computation.24 | async-start | bytes 4718592 | tf_op jit(solution)/shard_map/reduce_scatter | solution.py:68
  989.4 224.5 %reduce-scatter.29.cloned.1.call-start = ((), (), s32[]{:S(2)}) async-start(), calls=%async_computation.27 | async-start | bytes 270336 | tf_op jit(solution)/shard_map/reduce_scatter | solution.py:141
  994.8 362.7 %reduce-scatter.25.cloned.1.call-start = ((), (), s32[]{:S(2)}) async-start(), calls=%async_computation.25 | async-start | bytes 6488064 | tf_op jit(solution)/shard_map/reduce_scatter | solution.py:135
  1005.5 495.7 %reduce-scatter.27.cloned.1.call-start = ((), (), s32[]{:S(2)}) async-start(), calls=%async_computation.26 | async-start | bytes 6488064 | tf_op jit(solution)/shard_map/reduce_scatter | solution.py:138
  1017.3 60.3 %copy-start.3 = (f32[256,1024]{1,0:T(8,128)S(1)}, f32[256,1024]{1,0:T(8,128)}, u32[]{:S(2)}) copy-start(f32[256,1024]{1,0:T(8,128)} %copy-done.1) | copy-start | bytes 3145732
  1017.3 197.4 %copy-start.30 = (f32[16]{0:T(128)S(1)}, f32[16]{0:T(128)}, u32[]{:S(2)}) copy-start(f32[16]{0:T(128)} %param.32) | copy-start | bytes 196
  1017.3 484.9 %copy-start.27 = (f32[3,32]{1,0:T(4,128)S(1)}, f32[3,32]{1,0:T(4,128)}, u32[]{:S(2)}) copy-start(f32[3,32]{1,0:T(4,128)} %param.28) | copy-start | bytes 1156
  1017.3 485.0 %copy-start.28 = (f32[3,32]{1,0:T(4,128)S(1)}, f32[3,32]{1,0:T(4,128)}, u32[]{:S(2)}) copy-start(f32[3,32]{1,0:T(4,128)} %param.30) | copy-start | bytes 1156
  1017.3 617.8 %reduce-scatter.31.cloned.1.call-start = ((), (), s32[]{:S(2)}) async-start(), calls=%async_computation.28 | async-start | bytes 1351680
  1080.0 593.8 %copy-start.24 = (f32[602]{0:T(1024)S(1)}, f32[602]{0:T(1024)}, u32[]{:S(2)}) copy-start(f32[602]{0:T(1024)} %param.26) | copy-start | bytes 7228
  1080.0 595.0 %copy-start.33 = (f32[16]{0:T(128)S(1)}, f32[16]{0:T(128)}, u32[]{:S(2)}) copy-start(f32[16]{0:T(128)} %param.27) | copy-start | bytes 196
  1080.0 595.7 %copy-start.34 = (f32[121]{0:T(128)S(1)}, f32[121]{0:T(128)}, u32[]{:S(2)}) copy-start(f32[121]{0:T(128)} %param.33) | copy-start | bytes 1456
  1080.0 595.7 %copy-start.21 = (f32[3,512]{1,0:T(4,128)S(1)}, f32[3,512]{1,0:T(4,128)}, u32[]{:S(2)}) copy-start(f32[3,512]{1,0:T(4,128)} %param.31) | copy-start | bytes 18436
  1080.0 595.7 %copy-start.22 = (f32[3,512]{1,0:T(4,128)S(1)}, f32[3,512]{1,0:T(4,128)}, u32[]{:S(2)}) copy-start(f32[3,512]{1,0:T(4,128)} %param.29) | copy-start | bytes 18436
  1080.1 643.6 %copy-start.12 = (f32[602,16]{0,1:T(8,128)S(1)}, f32[602,16]{0,1:T(8,128)}, u32[]{:S(2)}) copy-start(f32[602,16]{0,1:T(8,128)} %param.22) | copy-start | bytes 115588
  1080.1 645.1 %copy-start.4 = (f32[3,32,512]{2,1,0:T(8,128)S(1)}, f32[3,32,512]{2,1,0:T(8,128)}, u32[]{:S(2)}) copy-start(f32[3,32,512]{2,1,0:T(8,128)} %param.23) | copy-start | bytes 589828
  1080.1 646.8 %copy-start.5 = (f32[3,32,512]{2,1,0:T(8,128)S(1)}, f32[3,32,512]{2,1,0:T(8,128)}, u32[]{:S(2)}) copy-start(f32[3,32,512]{2,1,0:T(8,128)} %param.24) | copy-start | bytes 589828
  1215.3 514.7 %copy-start.23 = (f32[16]{0:T(128)}, f32[16]{0:T(128)S(1)}, u32[]{:S(2)}) copy-start(f32[16]{0:T(128)S(1)} %get-tuple-element.97) | copy-start | bytes 196
  1502.3 227.7 %copy-start.18 = (f32[3,32]{1,0:T(4,128)}, f32[3,32]{1,0:T(4,128)S(1)}, u32[]{:S(2)}) copy-start(f32[3,32]{1,0:T(4,128)S(1)} %get-tuple-element.101) | copy-start | bytes 1156
  1502.5 227.6 %copy-start.19 = (f32[3,32]{1,0:T(4,128)}, f32[3,32]{1,0:T(4,128)S(1)}, u32[]{:S(2)}) copy-start(f32[3,32]{1,0:T(4,128)S(1)} %get-tuple-element.99) | copy-start | bytes 1156
  1674.4 55.7 %copy-start.16 = (f32[602]{0:T(1024)}, f32[602]{0:T(1024)S(1)}, u32[]{:S(2)}) copy-start(f32[602]{0:T(1024)S(1)} %get-tuple-element.95) | copy-start | bytes 7228
  1675.0 55.0 %copy-start.26 = (f32[16]{0:T(128)}, f32[16]{0:T(128)S(1)}, u32[]{:S(2)}) copy-start(f32[16]{0:T(128)S(1)} %add_multiply_fusion.10) | copy-start | bytes 196
  1675.7 54.3 %copy-start.29 = (f32[121]{0:T(128)}, f32[121]{0:T(128)S(1)}, u32[]{:S(2)}) copy-start(f32[121]{0:T(128)S(1)} %add_multiply_fusion.8) | copy-start | bytes 1456
  1675.8 54.3 %copy-start.14 = (f32[3,512]{1,0:T(4,128)}, f32[3,512]{1,0:T(4,128)S(1)}, u32[]{:S(2)}) copy-start(f32[3,512]{1,0:T(4,128)S(1)} %get-tuple-element.118) | copy-start | bytes 18436
  1675.8 54.2 %copy-start.15 = (f32[3,512]{1,0:T(4,128)}, f32[3,512]{1,0:T(4,128)S(1)}, u32[]{:S(2)}) copy-start(f32[3,512]{1,0:T(4,128)S(1)} %get-tuple-element.119) | copy-start | bytes 18436
  (24 other events, 230.4 us)
Sparse Core Ops, SparseCore 0:
  10.9 56.9 all-gather.9
  72.5 72.3 all-gather.13
  147.8 67.3 all-gather.11
  217.6 30.3 reduce-scatter.12
  251.1 69.0 all-gather.15
  325.1 72.2 all-gather.17
  428.5 29.6 reduce-scatter.14
  465.8 73.4 all-gather.19
  570.6 30.5 reduce-scatter.16
  669.6 23.1 all-gather.21
  710.8 87.8 reduce-scatter.18
  809.6 22.3 all-gather.23
  850.1 88.0 reduce-scatter.20
  949.1 22.3 all-gather.25
  989.5 88.0 reduce-scatter.22
  1080.2 133.5 reduce-scatter.28
  1216.7 140.7 reduce-scatter.24
  1360.3 140.7 reduce-scatter.26
  1504.1 131.0 reduce-scatter.30
where the time goes:
time: 1740 us
  waiting for transfers between devices  1290 us (74%)
  matrix products  231 us (13%)
  blocking collectives  162 us (9%)
  other arithmetic  31.3 us (2%)
  between operations  18.7 us (1%)
    reduce_scatter x3, waiting for transfers between devices, backward_layer(): lax.psum_scatter(left_t(adj_float, every_row), 'wide', scatter_dimension=...  236 us
    all_gather x3, waiting for transfers between devices, forward_layer(): gathered = lax.all_gather(sent, 'wide', axis=0, tiled=True)  218 us
    reduce_scatter x1, waiting for transfers between devices, shards(): lax.psum_scatter(jnp.stack(proj_grads), ('wide', 'narrow'), scatter_dimen...  143 us
    reduce_scatter x1, waiting for transfers between devices, shards(): lax.psum_scatter(jnp.stack(side_grads), ('wide', 'narrow'), scatter_dimen...  142 us
    unnamed x20, waiting for transfers between devices  135 us
    reduce_scatter x1, waiting for transfers between devices, shards(): lax.psum_scatter(g_out, ('wide', 'narrow'), scatter_dimension=0, tiled=True)  131 us
    dot_general x14, matrix products, matmul(): jnp.dot(left, right, precision=lax.Precision.HIGHEST, preferred_element_t...  126 us
    psum x2, blocking collectives, shards(): lax.psum((jnp.sum(weight_mask * lam * per), jnp.sum(weight_mask)), ('wide...  78.3 us
  transfers between devices with their start and end apart: 19, of which 18 were waited for; matrix products, arithmetic and copies ran while one was open for 5% of the time, Pallas kernels for 0%

commit v1 on v0

v1 whole, which is shorter than its diff:
```python
import functools
import jax
import jax.numpy as jnp
from jax import lax
from jax.experimental import pallas as pl
from jax.experimental.pallas import tpu as pltpu
from jax.sharding import PartitionSpec as P

MESH = pl.DeviceIdType.MESH
LANES = 128
CORES = 2
f32 = jnp.float32
bf16 = jnp.bfloat16


def grid_of(mesh):
    wide, narrow = mesh.shape["wide"], mesh.shape["narrow"]
    far = 4 if wide % 4 == 0 else wide
    return far, wide // far, narrow // CORES, CORES


def place(dims):
    far, near, across, cores = dims
    wide, narrow = lax.axis_index("wide"), lax.axis_index("narrow")
    return wide // near, lax.rem(wide, near), narrow // cores, lax.rem(narrow, cores)


def device(dims, far_at, near_at, across_at, core_at):
    return (far_at * dims[1] + near_at, across_at * dims[3] + core_at)


def send(src, dst, send_sem, recv_sem, target):
    pltpu.make_async_remote_copy(
        src_ref=src,
        dst_ref=dst,
        send_sem=send_sem,
        recv_sem=recv_sem,
        device_id=target,
        device_id_type=MESH,
    ).start()


def arrived(dst, recv_sem):
    pltpu.make_async_copy(dst, dst, recv_sem).wait()


def left_source(src, send_sem):
    pltpu.make_async_copy(src, src, send_sem).wait()


def halves(value):
    high = value.astype(bf16)
    return high, (value - high.astype(f32)).astype(bf16)


def neighbours(dims, at):
    far, near, across, cores = dims
    p, q, x, c = at
    always = [(p, lax.rem(q + step, near), x, c) for step in range(1, near)]
    always += [(p, q, lax.rem(x + step, across), c) for step in range(1, across)]
    always += [(p, q, x, 1 - c)]
    return always


def entry_barrier(dims, at):
    far, near, across, cores = dims
    p, q, x, c = at
    barrier = pltpu.get_barrier_semaphore()
    steady = neighbours(dims, at)
    for other in steady:
        pl.semaphore_signal(barrier, inc=1, device_id=device(dims, *other), device_id_type=MESH)

    @pl.when(p > 0)
    def _():
        pl.semaphore_signal(barrier, inc=1, device_id=device(dims, p - 1, q, x, c), device_id_type=MESH)

    @pl.when(p < far - 1)
    def _():
        pl.semaphore_signal(barrier, inc=1, device_id=device(dims, p + 1, q, x, c), device_id_type=MESH)

    ends = jnp.where(p > 0, 1, 0) + jnp.where(p < far - 1, 1, 0)
    pl.semaphore_wait(barrier, len(steady) + ends)


def chunk(ref, k):
    return ref.at[:, pl.ds(k * LANES, LANES)]


def forward_kernel(dims, chunks, adj, sent, out, gathered, pair, part, from_core, from_across, to_right, to_left, to_near, came, core_sems, across_out, across_in):
    far, near, across, cores = dims
    p, q, x, c = at = place(dims)
    nodes = sent.shape[0]
    early = chunks - 1
    right, left = device(dims, p + 1, q, x, c), device(dims, p - 1, q, x, c)
    others = [lax.rem(q + step, near) for step in range(1, near)]
    entry_barrier(dims, at)

    def go_right(k, pp, qq, src):
        @pl.when(p < far - 1)
        def _():
            send(src, gathered.at[k, pp, qq], to_right.at[k, pp, qq], came.at[k, pp, qq], right)

    def go_left(k, pp, qq, src):
        @pl.when(p > 0)
        def _():
            send(src, gathered.at[k, pp, qq], to_left.at[k, pp, qq], came.at[k, pp, qq], left)

    def go_near(k, pp, src):
        for step, qq in enumerate(others):
            send(src, gathered.at[k, pp, q], to_near.at[k, pp, step], came.at[k, pp, q], device(dims, p, qq, x, c))

    for k in [early] + list(range(chunks - 1)):
        src = chunk(sent, k)
        go_near(k, p, src)
        go_right(k, p, q, src)
        go_left(k, p, q, src)
    for k in range(chunks):
        gathered[k, p, q] = sent[:, k * LANES : (k + 1) * LANES]
    for qq in others:
        arrived(gathered.at[early, p, qq], came.at[early, p, qq])
        go_right(early, p, qq, gathered.at[early, p, qq])
        go_left(early, p, qq, gathered.at[early, p, qq])
    for step in range(1, far):
        for k in range(chunks):
            for side in range(2):
                pp = p - step if side == 0 else p + step
                onward = go_right if side == 0 else go_left

                @pl.when(pp >= 0 if side == 0 else pp < far)
                def _(k=k, pp=pp, onward=onward):
                    for qq in [q] + (others if k == early else []):
                        block = gathered.at[k, pp, qq]
                        arrived(block, came.at[k, pp, qq])
                        onward(k, pp, qq, block)
                    if k != early:
                        go_near(k, pp, gathered.at[k, pp, q])

    def reduce_across(k):
        arrived(from_core.at[k], core_sems.at[1, k])
        for step in range(1, across):
            xx = lax.rem(x + step, across)
            part[k, c, xx] = part[k, c, xx] + from_core[k, xx]
            send(part.at[k, c, xx], from_across.at[k, x], across_out.at[k, xx], across_in.at[k, x], device(dims, p, q, xx, c))

    def finish(k):
        total = part[k, c, x] + from_core[k, x]
        for step in range(1, across):
            xx = lax.rem(x + step, across)
            arrived(from_across.at[k, xx], across_in.at[k, xx])
            total = total + from_across[k, xx]
        out[:, k * LANES : (k + 1) * LANES] = total

    for k in range(chunks):
        if k != early:
            for pp in range(far):
                for qq in others:
                    arrived(gathered.at[k, pp, qq], came.at[k, pp, qq])
        high, low = halves(gathered[k].reshape(far * near * nodes, LANES))
        pair[:, :LANES] = high
        pair[:, LANES:] = low

        def product(index, carry, k=k):
            cc = lax.rem(index // across + 1 + c, cores)
            xx = lax.rem(index, across)
            rows = pl.multiple_of((xx * cores + cc) * nodes, nodes)
            both = jnp.dot(adj[pl.ds(rows, nodes), :], pair[...], preferred_element_type=f32)
            part[k, cc, xx] = both[:, :LANES] + both[:, LANES:]

            @pl.when(index == across - 1)
            def _():
                send(part.at[k, 1 - c], from_core.at[k], core_sems.at[0, k], core_sems.at[1, k], device(dims, p, q, x, 1 - c))

            return carry

        lax.fori_loop(0, cores * across, product, 0)
        if k >= 1:
            reduce_across(k - 1)
        if k >= 2:
            finish(k - 2)
    reduce_across(chunks - 1)
    if chunks >= 2:
        finish(chunks - 2)
    finish(chunks - 1)

    for k in range(chunks):
        left_source(part.at[k, 1 - c], core_sems.at[0, k])
        for step in range(1, across):
            xx = lax.rem(x + step, across)
            left_source(part.at[k, c, xx], across_out.at[k, xx])
        for pp in range(far):
            for qq in [q] + (others if k == early else []):
                block = gathered.at[k, pp, qq]

                @pl.when(jnp.logical_and(p < far - 1, pp <= p))
                def _(k=k, pp=pp, qq=qq, block=block):
                    left_source(block, to_right.at[k, pp, qq])

                @pl.when(jnp.logical_and(p > 0, pp >= p))
                def _(k=k, pp=pp, qq=qq, block=block):
                    left_source(block, to_left.at[k, pp, qq])

            def near_sent(k=k, pp=pp):
                for step in range(near - 1):
                    left_source(gathered.at[k, pp, q], to_near.at[k, pp, step])

            if k == early:
                pl.when(pp == p)(near_sent)
            else:
                near_sent()


def forward_aggregate(dims, name_id, adj, sent):
    far, near, across, cores = dims
    nodes, width = sent.shape
    chunks = width // LANES
    dma = pltpu.SemaphoreType.DMA
    return pl.pallas_call(
        functools.partial(forward_kernel, dims, chunks),
        out_shape=jax.ShapeDtypeStruct((nodes, width), f32),
        in_specs=[pl.BlockSpec(memory_space=pltpu.VMEM)] * 2,
        out_specs=pl.BlockSpec(memory_space=pltpu.VMEM),
        scratch_shapes=[
            pltpu.VMEM((chunks, far, near, nodes, LANES), f32),
            pltpu.VMEM((far * near * nodes, 2 * LANES), bf16),
            pltpu.VMEM((chunks, cores, across, nodes, LANES), f32),
            pltpu.VMEM((chunks, across, nodes, LANES), f32),
            pltpu.VMEM((chunks, across, nodes, LANES), f32),
            dma((chunks, far, near)),
            dma((chunks, far, near)),
            dma((chunks, far, near)),
            dma((chunks, far, near)),
            dma((2, chunks)),
            dma((chunks, across)),
            dma((chunks, across)),
        ],
        compiler_params=pltpu.CompilerParams(
            collective_id=name_id, has_side_effects=True, vmem_limit_bytes=60 * 2**20
        ),
    )(adj, sent)


def backward_kernel(dims, chunks, adj, sent, out, rows, pair, part, from_near, from_left, from_right, final, row_out, row_in, near_out, near_in, right_out, left_out, left_in, right_in):
    far, near, across, cores = dims
    p, q, x, c = at = place(dims)
    nodes = sent.shape[0]
    early = 0
    right, left = device(dims, p + 1, q, x, c), device(dims, p - 1, q, x, c)
    others = [lax.rem(q + step, near) for step in range(1, near)]
    crossing = [lax.rem(x + step, across) for step in range(1, across)]
    entry_barrier(dims, at)

    for k in range(chunks):
        src = chunk(sent, k)
        for xx in crossing:
            send(src, rows.at[k, x, c], row_out.at[k, xx], row_in.at[k, x, c], device(dims, p, q, xx, c))
        send(src, rows.at[k, x, c], row_out.at[k, across + x], row_in.at[k, x, c], device(dims, p, q, x, 1 - c))
    for k in range(chunks):
        rows[k, x, c] = sent[:, k * LANES : (k + 1) * LANES]

    def dest(i):
        rights = far - 1 - p
        low = jnp.where(i < rights, far - 1 - i, jnp.where(i < far - 1, i - rights, p))
        high = jnp.where(i < p, i, jnp.where(i < far - 1, far - 1 - (i - p), p))
        return jnp.where(p < far // 2, low, high)

    def along(k, pp, qq):
        @pl.when(pp > p)
        def _():
            @pl.when(p > 0)
            def _():
                arrived(from_left.at[k, pp, qq], left_in.at[k, pp, qq])
                part[k, pp, qq] = part[k, pp, qq] + from_left[k, pp, qq]

            send(part.at[k, pp, qq], from_left.at[k, pp, qq], right_out.at[k, pp, qq], left_in.at[k, pp, qq], right)

        @pl.when(pp < p)
        def _():
            @pl.when(p < far - 1)
            def _():
                arrived(from_right.at[k, pp, qq], right_in.at[k, pp, qq])
                part[k, pp, qq] = part[k, pp, qq] + from_right[k, pp, qq]

            send(part.at[k, pp, qq], from_right.at[k, pp, qq], left_out.at[k, pp, qq], right_in.at[k, pp, qq], left)

    def settle(k, qq):
        @pl.when(p > 0)
        def _():
            arrived(from_left.at[k, p, qq], left_in.at[k, p, qq])
            part[k, p, qq] = part[k, p, qq] + from_left[k, p, qq]

        @pl.when(p < far - 1)
        def _():
            arrived(from_right.at[k, p, qq], right_in.at[k, p, qq])
            part[k, p, qq] = part[k, p, qq] + from_right[k, p, qq]

    def line(k):
        def step(i, carry):
            pp = dest(i)
            if k == early:
                for qq in others + [q]:
                    along(k, pp, qq)
            else:
                for qq in others:
                    arrived(from_near.at[k, pp, qq], near_in.at[k, pp, qq])
                    part[k, pp, q] = part[k, pp, q] + from_near[k, pp, qq]
                along(k, pp, q)
            return carry

        lax.fori_loop(0, far, step, 0)

    def early_end():
        for step, qq in enumerate(others):
            settle(early, qq)
            send(part.at[early, p, qq], from_near.at[early, p, q], near_out.at[early, p, step], near_in.at[early, p, q], device(dims, p, qq, x, c))

    for k in range(chunks):
        for xx in crossing:
            arrived(rows.at[k, xx, c], row_in.at[k, xx, c])
            send(rows.at[k, xx, c], rows.at[k, xx, c], row_out.at[k, across + xx], row_in.at[k, xx, c], device(dims, p, q, x, 1 - c))
        for xx in range(across):
            arrived(rows.at[k, xx, 1 - c], row_in.at[k, xx, 1 - c])
        high, low = halves(rows[k].reshape(across * cores * nodes, LANES))
        pair[:, :LANES] = high
        pair[:, LANES:] = low

        def product(i, carry, k=k):
            pp = dest(i // near)
            qq = lax.rem(q + 1 + lax.rem(i, near), near)
            start = pl.multiple_of((pp * near + qq) * nodes, nodes)
            both = lax.dot_general(adj[:, pl.ds(start, nodes)], pair[...], (((0,), (0,)), ((), ())), preferred_element_type=f32)
            part[k, pp, qq] = both[:, :LANES] + both[:, LANES:]
            if k != early:
                @pl.when(qq != q)
                def _():
                    send(part.at[k, pp, qq], from_near.at[k, pp, q], near_out.at[k, pp, lax.rem(qq - q - 1 + near, near)], near_in.at[k, pp, q], device(dims, p, qq, x, c))

            return carry

        lax.fori_loop(0, far * near, product, 0)
        if k >= 1:
            line(k - 1)
    early_end()
    line(chunks - 1)
    for k in range(chunks):
        settle(k, q)
        total = part[k, p, q]
        if k == early:
            for qq in others:
                arrived(from_near.at[k, p, qq], near_in.at[k, p, qq])
                total = total + from_near[k, p, qq]
        out[:, k * LANES : (k + 1) * LANES] = total

    for k in range(chunks):
        for xx in crossing:
            left_source(rows.at[k, x, c], row_out.at[k, xx])
        for xx in range(across):
            left_source(rows.at[k, xx, c], row_out.at[k, across + xx])
        for pp in range(far):
            for qq in [q] + (others if k == early else []):
                @pl.when(pp > p)
                def _(k=k, pp=pp, qq=qq):
                    left_source(part.at[k, pp, qq], right_out.at[k, pp, qq])

                @pl.when(pp < p)
                def _(k=k, pp=pp, qq=qq):
                    left_source(part.at[k, pp, qq], left_out.at[k, pp, qq])

            def near_sent(k=k, pp=pp):
                for step in range(near - 1):
                    left_source(part.at[k, pp, q], near_out.at[k, pp, step])

            if k == early:
                pl.when(pp == p)(near_sent)
            else:
                near_sent()


def backward_aggregate(dims, name_id, adj, sent):
    far, near, across, cores = dims
    nodes, width = sent.shape
    chunks = width // LANES
    dma = pltpu.SemaphoreType.DMA
    blocks = pltpu.VMEM((chunks, far, near, nodes, LANES), f32)
    return pl.pallas_call(
        functools.partial(backward_kernel, dims, chunks),
        out_shape=jax.ShapeDtypeStruct((nodes, width), f32),
        in_specs=[pl.BlockSpec(memory_space=pltpu.VMEM)] * 2,
        out_specs=pl.BlockSpec(memory_space=pltpu.VMEM),
        scratch_shapes=[
            pltpu.VMEM((chunks, across, cores, nodes, LANES), f32),
            pltpu.VMEM((across * cores * nodes, 2 * LANES), bf16),
            blocks,
            blocks,
            blocks,
            blocks,
            pltpu.VMEM((8, LANES), f32),
            dma((chunks, 2 * across)),
            dma((chunks, across, cores)),
        ]
        + [dma((chunks, far, near))] * 6,
        compiler_params=pltpu.CompilerParams(
            collective_id=name_id, has_side_effects=True, vmem_limit_bytes=60 * 2**20
        ),
    )(adj, sent)


norm_eps = 1e-06
stat_eps = 1e-30
clip_level = 0.5
step_rate = 0.04


def dot(left, right, over=((1,), (0,))):
    return lax.dot_general(
        left, right, (over, ((), ())), precision=lax.Precision.HIGH, preferred_element_type=f32
    )


def left_t(left, right):
    return dot(left, right, ((0,), (0,)))


def right_t(left, right):
    return dot(left, right, ((1,), (1,)))


def step_on_device(
    dims,
    features,
    adjacency,
    labels,
    labelled,
    node_count,
    w_in,
    w_side,
    w_proj,
    w_out,
    row_in,
    col_in,
    row_side,
    col_side,
    row_proj,
    col_proj,
    row_out,
    col_out,
):
    layers = w_side.shape[0]
    width = w_side.shape[2]
    in_width = features.shape[1]
    classes = w_out.shape[1]
    nodes = features.shape[0]
    both = ("wide", "narrow")
    adj = adjacency.astype(bf16)
    counts = node_count.astype(f32)
    alpha = 2.0 / (1.0 + counts)
    lam = lax.rsqrt(counts)
    target = labels.astype(f32)
    weight_mask = labelled.astype(f32)

    spare = -(in_width + 1) % LANES
    sent = jnp.concatenate(
        [alpha[:, None] * features, jnp.ones((nodes, 1), f32), jnp.zeros((nodes, spare), f32)], 1
    )
    summed = forward_aggregate(dims, 1, adj, sent)
    inverse = 1.0 / (1.0 + summed[:, in_width : in_width + 1])
    agg_features = summed[:, :in_width] * inverse

    full_in, full_side, full_proj, full_out = (
        lax.all_gather(w_in, both, axis=1, tiled=True),
        lax.all_gather(w_side, both, axis=1, tiled=True),
        lax.all_gather(w_proj, both, axis=1, tiled=True),
        lax.all_gather(w_out, both, axis=0, tiled=True),
    )
    mix_self = [dot(full_side[l, :width], full_proj[l, :width]) for l in range(layers)]
    mix_neigh = [dot(full_side[l, width:], full_proj[l, width:]) for l in range(layers)]

    kept = []
    hidden = dot(features, full_in)
    agg = dot(agg_features, full_in)
    for layer in range(layers):
        if layer > 0:
            agg = forward_aggregate(dims, 1 + layer, adj, alpha[:, None] * hidden) * inverse
        pre_act = dot(hidden, mix_self[layer]) + dot(agg, mix_neigh[layer])
        kept.append((hidden, agg, pre_act))
        act = jax.nn.silu(pre_act)
        hidden = act * lax.rsqrt(jnp.mean(act * act, -1, keepdims=True) + norm_eps)

    logits = dot(hidden, full_out)
    per = jnp.sum(jax.nn.softplus(logits) - target * logits, -1)
    loss_sum, label_count = lax.psum(
        (jnp.sum(weight_mask * lam * per), jnp.sum(weight_mask)), both
    )
    d_logits = (weight_mask * lam / label_count)[:, None] * (jax.nn.sigmoid(logits) - target)
    g_out = left_t(hidden, d_logits)
    d_out = right_t(d_logits, full_out)
    side_grads = [None] * layers
    proj_grads = [None] * layers
    for layer in reversed(range(layers)):
        hidden, agg, pre_act = kept[layer]
        sig = jax.nn.sigmoid(pre_act)
        act = pre_act * sig
        scale = lax.rsqrt(jnp.mean(act * act, -1, keepdims=True) + norm_eps)
        normed = act * scale
        d_act = scale * (d_out - normed * jnp.mean(d_out * normed, -1, keepdims=True))
        d_pre = d_act * sig * (1.0 + pre_act * (1.0 - sig))
        outer_self = left_t(hidden, d_pre)
        outer_neigh = left_t(agg, d_pre)
        side, proj = full_side[layer], full_proj[layer]
        side_grads[layer] = jnp.concatenate(
            [right_t(outer_self, proj[:width]), right_t(outer_neigh, proj[width:])], 0
        )
        proj_grads[layer] = jnp.concatenate(
            [left_t(side[:width], outer_self), left_t(side[width:], outer_neigh)], 0
        )
        d_self = right_t(d_pre, mix_self[layer])
        if layer > 0:
            back = backward_aggregate(dims, 3 + layer, adj, d_pre * inverse)
            d_out = d_self + right_t(alpha[:, None] * back, mix_neigh[layer])
        else:
            g_in = left_t(features, d_self) + left_t(agg_features, right_t(d_pre, mix_neigh[layer]))
    red_in, red_side, red_proj, red_out = (
        lax.psum_scatter(g_in, both, scatter_dimension=1, tiled=True),
        lax.psum_scatter(jnp.stack(side_grads), both, scatter_dimension=1, tiled=True),
        lax.psum_scatter(jnp.stack(proj_grads), both, scatter_dimension=1, tiled=True),
        lax.psum_scatter(g_out, both, scatter_dimension=0, tiled=True),
    )
    sq_in = red_in * red_in
    sq_side = red_side * red_side
    sq_proj = red_proj * red_proj
    sq_out = red_out * red_out
    new_col_in = 0.5 * col_in + 0.5 * (jnp.mean(sq_in, 0) + stat_eps)
    new_row_side = 0.5 * row_side + 0.5 * (jnp.mean(sq_side, 2) + stat_eps)
    new_row_proj = 0.5 * row_proj + 0.5 * (jnp.mean(sq_proj, 2) + stat_eps)
    new_row_out = 0.5 * row_out + 0.5 * (jnp.mean(sq_out, 1) + stat_eps)
    (
        sum_row_in,
        sum_col_side,
        sum_col_proj,
        sum_col_out,
        total_side,
        total_proj,
        total_out,
        over_in,
        over_side,
        over_proj,
        over_out,
    ) = lax.psum(
        (
            jnp.sum(sq_in, 1),
            jnp.sum(sq_side, 1),
            jnp.sum(sq_proj, 1),
            jnp.sum(sq_out, 0),
            jnp.sum(new_row_side, 1),
            jnp.sum(new_row_proj, 1),
            jnp.sum(new_row_out),
            jnp.sum(sq_in / new_col_in[None, :], 1),
            jnp.sum(sq_side / new_row_side[:, :, None], 1),
            jnp.sum(sq_proj / new_row_proj[:, :, None], 1),
            jnp.sum(sq_out / new_row_out[:, None], 0),
        ),
        both,
    )
    new_row_in = 0.5 * row_in + 0.5 * (sum_row_in / width + stat_eps)
    new_col_side = 0.5 * col_side + 0.5 * (sum_col_side / (2 * width) + stat_eps)
    new_col_proj = 0.5 * col_proj + 0.5 * (sum_col_proj / (2 * width) + stat_eps)
    new_col_out = 0.5 * col_out + 0.5 * (sum_col_out / width + stat_eps)
    mean_in = jnp.mean(new_row_in)
    mean_side = total_side / (2 * width)
    mean_proj = total_proj / (2 * width)
    mean_out = total_out / width
    up_in = red_in * lax.rsqrt(new_row_in[:, None] * new_col_in[None, :] / mean_in)
    up_side = red_side * lax.rsqrt(
        new_row_side[:, :, None] * new_col_side[:, None, :] / mean_side[:, None, None]
    )
    up_proj = red_proj * lax.rsqrt(
        new_row_proj[:, :, None] * new_col_proj[:, None, :] / mean_proj[:, None, None]
    )
    up_out = red_out * lax.rsqrt(new_row_out[:, None] * new_col_out[None, :] / mean_out)
    ms_in = mean_in * jnp.sum(over_in / new_row_in) / (in_width * width)
    ms_side = mean_side * jnp.sum(over_side / new_col_side, 1) / (2 * width * width)
    ms_proj = mean_proj * jnp.sum(over_proj / new_col_proj, 1) / (2 * width * width)
    ms_out = mean_out * jnp.sum(over_out / new_col_out) / (width * classes)
    fac_in = 1.0 / jnp.maximum(1.0, jnp.sqrt(ms_in) / clip_level)
    fac_side = 1.0 / jnp.maximum(1.0, jnp.sqrt(ms_side) / clip_level)
    fac_proj = 1.0 / jnp.maximum(1.0, jnp.sqrt(ms_proj) / clip_level)
    fac_out = 1.0 / jnp.maximum(1.0, jnp.sqrt(ms_out) / clip_level)
    new_in = w_in - step_rate * (up_in * fac_in)
    new_side = w_side - step_rate * (up_side * fac_side[:, None, None])
    new_proj = w_proj - step_rate * (up_proj * fac_proj[:, None, None])
    new_out = w_out - step_rate * (up_out * fac_out)
    return (
        loss_sum,
        label_count,
        red_in,
        red_side,
        red_proj,
        red_out,
        new_in,
        new_side,
        new_proj,
        new_out,
        new_row_in,
        new_col_in,
        new_row_side,
        new_col_side,
        new_row_proj,
        new_col_proj,
        new_row_out,
        new_col_out,
    )


def solution(mesh):
    in_specs = (
        P(("wide", "narrow"), None),
        P("wide", "narrow"),
        P(("wide", "narrow"), None),
        P(("wide", "narrow")),
        P(("wide", "narrow")),
        P(None, ("wide", "narrow")),
        P(None, ("wide", "narrow"), None),
        P(None, ("wide", "narrow"), None),
        P(("wide", "narrow"), None),
        P(),
        P(("wide", "narrow")),
        P(None, ("wide", "narrow")),
        P(),
        P(None, ("wide", "narrow")),
        P(),
        P(("wide", "narrow")),
        P(),
    )
    out_specs = (
        P(),
        P(),
        P(None, ("wide", "narrow")),
        P(None, ("wide", "narrow"), None),
        P(None, ("wide", "narrow"), None),
        P(("wide", "narrow"), None),
        P(None, ("wide", "narrow")),
        P(None, ("wide", "narrow"), None),
        P(None, ("wide", "narrow"), None),
        P(("wide", "narrow"), None),
        P(),
        P(("wide", "narrow")),
        P(None, ("wide", "narrow")),
        P(),
        P(None, ("wide", "narrow")),
        P(),
        P(("wide", "narrow")),
        P(),
    )
    shards = functools.partial(step_on_device, grid_of(mesh))
    return jax.shard_map(shards, mesh=mesh, in_specs=in_specs, out_specs=out_specs, check_vma=False)
```

time: 1740 us -> 1200 us (0.69)
  waiting for transfers between devices: 1290 us -> 564 us
  Pallas kernels: 0 us -> 365 us
  matrix products: 231 us -> 71.9 us
  blocking collectives: 162 us -> 120 us
    all_gather x9 -> x3, waiting for transfers between devices: 442 us -> 54.4 us  [the longest x1 54.3 us: step_on_device(): lax.all_gather(w_proj, both, axis=1, tiled=True)]
    pallas_call x0 -> x5, Pallas kernels: none -> 365 us  [the longest x3 227 us: forward_aggregate(): pl.pallas_call(functools.partial(forward_kernel, dims, chunks), out_shape...]
    reduce_scatter x9 -> x3, waiting for transfers between devices: 710 us -> 376 us  [the longest x1 142 us: step_on_device(): lax.psum_scatter(jnp.stack(proj_grads), both, scatter_dimension=1, tiled=...]
    dot_general x38 -> x43, matrix products: 231 us -> 71.9 us  [dot(): lax.dot_general(left, right, (over, ((), ())), precision=lax.Precision.HI...]
    psum x3 -> x2, blocking collectives: 116 us -> 75.3 us  [step_on_device(): lax.psum((jnp.sum(weight_mask * lam * per), jnp.sum(weight_mask)), both)]
    unnamed x20 -> x8, waiting for transfers between devices: 135 us -> 134 us
  transfers between devices with their start and end apart: 19 -> 7, of which waited for: 18 -> 5; matrix products, arithmetic and copies ran while one was open for 5% -> 5% of each run, Pallas kernels for 0% -> 8%
where the time goes in v1:
time: 1200 us; the launch traced here: 1190 us
  waiting for transfers between devices  564 us (47%)
  Pallas kernels  365 us (30%)
  blocking collectives  120 us (10%)
  matrix products  71.9 us (6%)
  other arithmetic  39.7 us (3%)
  between operations  18.4 us (2%)
    pallas_call x3, Pallas kernels, forward_aggregate(): pl.pallas_call(functools.partial(forward_kernel, dims, chunks), out_shape...  227 us
    reduce_scatter x1, waiting for transfers between devices, step_on_device(): lax.psum_scatter(jnp.stack(proj_grads), both, scatter_dimension=1, tiled=...  142 us
    reduce_scatter x1, waiting for transfers between devices, step_on_device(): lax.psum_scatter(jnp.stack(side_grads), both, scatter_dimension=1, tiled=...  141 us
    pallas_call x2, Pallas kernels, backward_aggregate(): pl.pallas_call(functools.partial(backward_kernel, dims, chunks), out_shap...  139 us
    unnamed x8, waiting for transfers between devices  134 us
    reduce_scatter x1, waiting for transfers between devices, step_on_device(): lax.psum_scatter(g_out, both, scatter_dimension=0, tiled=True)  92.4 us
    psum x2, blocking collectives, step_on_device(): lax.psum((jnp.sum(weight_mask * lam * per), jnp.sum(weight_mask)), both)  75.3 us
    dot_general x43, matrix products, dot(): lax.dot_general(left, right, (over, ((), ())), precision=lax.Precision.HI...  71.9 us
  transfers between devices with their start and end apart: 7, of which 5 were waited for; matrix products, arithmetic and copies ran while one was open for 5% of the time, Pallas kernels for 8%

profile of v1, /device:TPU:0, one launch (start us, length us, event | category | flops | bytes accessed | tf_op | source)
XLA Modules:
  0.0 1187.4 jit_solution(13291500725558068393)
XLA Ops:
  10.5 1.3 copy.54
  11.8 6.5 convert_element_type.14.adj
  19.5 92.1 %shard_map.304 = f32[256,640]{1,0:T(8,128)} custom-call(bf16[1024,2048]{1,0:T(8,128)(2,1)} %convert_element_type.14.adj, f32[256,640]{1,0:T(8,128)} %maximum_maximum_fusion.sent), custom_call_target="tpu_custom_call" | custom-call | tf_op jit(solution)/shard_map/pallas_call | solution.py:217
  111.7 44.6 %all_gather.15 = f32[512,121]{1,0:T(8,128)} all-gather(f32[16,121]{1,0:T(8,128)S(1)} %copy-done.33), channel_id=1, replica_groups=mesh['wide'=8,'narrow'=4] {'wide','narrow'}, dimensions={0}, use_global_device_ids=true | all-gather | bytes 255552 | tf_op jit(solution)/shard_map/all_gather | solution.py:472
  157.4 2.6 fusion.63
  160.0 2.5 fusion.12
  162.6 54.3 %all-gather.8.cloned.1.call-done = f32[3,1024,512]{2,1,0:T(8,128)} async-done(((f32[3,32,512]{2,1,0:T(8,128)}), f32[3,1024,512]{2,1,0:T(8,128)}) %all-gather.8.cloned.1.call-update) | async-done | bytes 6291472 | tf_op jit(solution)/shard_map/all_gather | solution.py:471
  216.9 2.5 fusion
  220.1 2.5 fusion.2
  224.6 68.5 %shard_map.305 = f32[256,512]{1,0:T(8,128)} custom-call(bf16[1024,2048]{1,0:T(8,128)(2,1)} %convert_element_type.14.adj, f32[256,512]{1,0:T(8,128)} %multiply_multiply_fusion.1.sent), custom_call_target="tpu_custom_call" | custom-call | tf_op jit(solution)/shard_map/pallas_call | solution.py:217
  293.2 2.6 fusion.4
  297.5 2.5 fusion.6
  302.0 66.0 %shard_map.306 = f32[256,512]{1,0:T(8,128)} custom-call(bf16[1024,2048]{1,0:T(8,128)(2,1)} %convert_element_type.14.adj, f32[256,512]{1,0:T(8,128)} %multiply_multiply_fusion.sent), custom_call_target="tpu_custom_call" | custom-call | tf_op jit(solution)/shard_map/pallas_call | solution.py:217
  368.0 2.6 fusion.8
  372.3 2.5 fusion.10
  377.1 37.3 %psum.92 = f32[]{:T(128)} all-reduce(f32[]{:T(128)} %get-tuple-element.100), channel_id=1, replica_groups=mesh['wide'=8,'narrow'=4] {'wide','narrow'}, use_global_device_ids=true, to_apply=%region_7.8 | all-reduce | flops 1 | bytes 8 | tf_op jit(solution)/shard_map/psum | solution.py:490
  415.1 1.4 fusion.24
  416.4 1.6 multiply_reduce_fusion.2
  419.2 2.0 fusion.65
  421.2 70.6 %shard_map.307 = f32[256,512]{1,0:T(8,128)} custom-call(bf16[1024,2048]{1,0:T(8,128)(2,1)} %convert_element_type.14.adj, f32[256,512]{1,0:T(8,128)} %get-tuple-element.129.sent), custom_call_target="tpu_custom_call" | custom-call | tf_op jit(solution)/shard_map/pallas_call | solution.py:384
  491.9 2.2 multiply_reduce_fusion.1
  495.2 2.8 fusion.66
  498.0 68.1 %shard_map.308 = f32[256,512]{1,0:T(8,128)} custom-call(bf16[1024,2048]{1,0:T(8,128)(2,1)} %convert_element_type.14.adj, f32[256,512]{1,0:T(8,128)} %get-tuple-element.127.sent), custom_call_target="tpu_custom_call" | custom-call | tf_op jit(solution)/shard_map/pallas_call | solution.py:384
  566.2 2.3 multiply_reduce_fusion
  568.5 1.4 add_multiply_fusion
  569.9 2.7 fusion.68
  572.6 1.5 fusion.67
  574.0 1.7 fusion.28
  575.8 1.7 convolution_bitcast_fusion
  577.5 1.8 convolution_add_fusion
  579.3 1.5 copy.62
  581.5 1.9 fusion.18
  583.7 2.3 fusion.11
  586.1 2.7 fusion.9
  596.3 3.4 pad_maximum_fusion
  600.0 2.7 convolution_bitcast_fusion.1
  602.8 2.7 convolution_bitcast_fusion.2
  605.7 2.4 convolution_bitcast_fusion.6
  611.7 3.4 pad_maximum_fusion.1
  615.2 92.4 %reduce-scatter.11.cloned.1.call-done = f32[16,121]{1,0:T(8,128)} async-done(((f32[512,121]{1,0:T(8,128)}), f32[16,121]{1,0:T(8,128)}) %reduce-scatter.11.cloned.1.call-update) | async-done | bytes 7760 | tf_op jit(solution)/shard_map/reduce_scatter | solution.py:525
  709.8 131.6 %reduce-scatter.13.cloned.1.call-done = f32[16,602]{1,0:T(8,128)} async-done(((f32[512,602]{1,0:T(8,128)}), f32[16,602]{1,0:T(8,128)}) %reduce-scatter.13.cloned.1.call-update) | async-done | bytes 38544
  843.2 141.2 %reduce-scatter.7.cloned.1.call-done = f32[3,32,512]{2,1,0:T(8,128)} async-done(((f32[3,1024,512]{2,1,0:T(8,128)}), f32[3,32,512]{2,1,0:T(8,128)}) %reduce-scatter.7.cloned.1.call-update) | async-done | bytes 196624 | tf_op jit(solution)/shard_map/reduce_scatter | solution.py:523
  985.6 142.5 %reduce-scatter.9.cloned.1.call-done = f32[3,32,512]{2,1,0:T(8,128)} async-done(((f32[3,1024,512]{2,1,0:T(8,128)}), f32[3,32,512]{2,1,0:T(8,128)}) %reduce-scatter.9.cloned.1.call-update) | async-done | bytes 196624 | tf_op jit(solution)/shard_map/reduce_scatter | solution.py:524
  1131.4 38.0 %all-reduce = (f32[]{:T(128)}, f32[602]{0:T(1024)S(1)}, f32[602]{0:T(1024)S(1)}, f32[3,512]{1,0:T(4,128)S(1)}, f32[3,512]{1,0:T(4,128)S(1)}, /*index=5*/f32[3]{0...) all-reduce(f32[]{:T(128)} %get-tuple-element.101, ...), channel_id=1, replica_groups=mesh['wide'=8,'narrow'=4] {'wide','narrow'}, use_global_device_ids=true, to_apply=%region_5.6 | all-reduce | flops 7598 | bytes 60784 | tf_op jit(solution)/shard_map/psum | solution.py:490
  1173.7 1.4 multiply_subtract_fusion.3
  1175.1 1.5 multiply_subtract_fusion.2
  1176.6 1.7 multiply_subtract_fusion
  1178.3 1.7 multiply_subtract_fusion.1
  (188 shorter events, 41.0 us)
Async XLA Ops:
  7.2 150.2 %all-gather.4.cloned.1.call-start = ((), (), s32[]{:S(2)}) async-start(), calls=%async_computation.4 | async-start | bytes 1351680 | tf_op jit(solution)/shard_map/all_gather | solution.py:469
  7.9 154.6 %all-gather.6.cloned.1.call-start = ((), (), s32[]{:S(2)}) async-start(), calls=%async_computation.5 | async-start | bytes 6488064 | tf_op jit(solution)/shard_map/all_gather | solution.py:470
  8.7 208.2 %all-gather.8.cloned.1.call-start = ((), (), s32[]{:S(2)}) async-start(), calls=%async_computation.6 | async-start | bytes 6488064 | tf_op jit(solution)/shard_map/all_gather | solution.py:471
  9.4 698.2 %reduce-scatter.11.cloned.1.call-start = ((), (), s32[]{:S(2)}) async-start(), calls=%async_computation.9 | async-start | bytes 270336 | tf_op jit(solution)/shard_map/reduce_scatter | solution.py:525
  11.8 6.6 copy-start.37
  18.3 93.4 %copy-start.33 = (f32[16,121]{1,0:T(8,128)S(1)}, f32[16,121]{1,0:T(8,128)}, u32[]{:S(2)}) copy-start(f32[16,121]{1,0:T(8,128)} %param.25) | copy-start | bytes 23236
  18.3 139.1 %copy-start.6 = (f32[256,602]{0,1:T(8,128)S(1)}, f32[256,602]{0,1:T(8,128)}, u32[]{:S(2)}) copy-start(f32[256,602]{0,1:T(8,128)} %param.17) | copy-start | bytes 1849348
  160.0 63.4 %copy-start.7 = (f32[256,512]{1,0:T(8,128)}, f32[256,512]{1,0:T(8,128)S(1)}, u32[]{:S(2)}) copy-start(f32[256,512]{1,0:T(8,128)S(1)} %fusion.63) | copy-start | bytes 1572868
  162.5 130.6 %copy-start.23 = (f32[256,512]{1,0:T(8,128)}, f32[256,512]{1,0:T(8,128)S(1)}, u32[]{:S(2)}) copy-start(f32[256,512]{1,0:T(8,128)S(1)} %fusion.12) | copy-start | bytes 1572868
  223.4 76.6 %copy-start.17 = (f32[256,512]{1,0:T(8,128)}, f32[256,512]{1,0:T(8,128)S(1)}, u32[]{:S(2)}) copy-start(f32[256,512]{1,0:T(8,128)S(1)} %get-tuple-element.136) | copy-start | bytes 1572868
  293.2 6.9 copy-start.20
  368.0 6.9 copy-start.22
  368.0 7.9 copy-start.29
  376.5 39.9 %copy-start.50 = (f32[256,121]{0,1:T(8,128)}, f32[256,121]{0,1:T(8,128)S(1)}, u32[]{:S(2)}) copy-start(f32[256,121]{0,1:T(8,128)S(1)} %get-tuple-element.142) | copy-start | bytes 371716
  419.2 154.8 %copy-start.11 = (f32[256,512]{1,0:T(8,128)}, f32[256,512]{1,0:T(8,128)S(1)}, u32[]{:S(2)}) copy-start(f32[256,512]{1,0:T(8,128)S(1)} %get-tuple-element.130) | copy-start | bytes 1572868
  491.9 74.3 %copy-start.18 = (f32[256,512]{1,0:T(8,128)S(1)}, f32[256,512]{1,0:T(8,128)}, u32[]{:S(2)}) copy-start(f32[256,512]{1,0:T(8,128)} %copy-done.17) | copy-start | bytes 1572868
  495.2 71.0 %copy-start.9 = (f32[256,512]{1,0:T(8,128)}, f32[256,512]{1,0:T(8,128)S(1)}, u32[]{:S(2)}) copy-start(f32[256,512]{1,0:T(8,128)S(1)} %get-tuple-element.128) | copy-start | bytes 1572868
  568.5 9.0 copy-start.5
  574.0 6.9 copy-start.24
  575.7 265.7 %reduce-scatter.13.cloned.1.call-start = ((), (), s32[]{:S(2)}) async-start(), calls=%async_computation.10 | async-start | bytes 1351680
  580.9 7.9 copy-start.8
  583.5 401.0 %reduce-scatter.7.cloned.1.call-start = ((), (), s32[]{:S(2)}) async-start(), calls=%async_computation.7 | async-start | bytes 6488064 | tf_op jit(solution)/shard_map/reduce_scatter | solution.py:523
  583.7 6.0 copy-start.10
  583.7 6.0 copy-start.19
  599.7 8.4 slice-start
  599.7 528.4 %reduce-scatter.9.cloned.1.call-start = ((), (), s32[]{:S(2)}) async-start(), calls=%async_computation.8 | async-start | bytes 6488064 | tf_op jit(solution)/shard_map/reduce_scatter | solution.py:524
  600.0 5.7 copy-start.1
  602.8 5.3 slice-start.1
  602.8 6.4 copy-start.4
  615.1 93.4 %copy-start.48 = (f32[16]{0:T(128)S(1)}, f32[16]{0:T(128)}, u32[]{:S(2)}) copy-start(f32[16]{0:T(128)} %param.32) | copy-start | bytes 196
  615.1 227.2 %copy-start.49 = (f32[16]{0:T(128)S(1)}, f32[16]{0:T(128)}, u32[]{:S(2)}) copy-start(f32[16]{0:T(128)} %param.27) | copy-start | bytes 196
  615.1 370.4 %copy-start.44 = (f32[3,32]{1,0:T(4,128)S(1)}, f32[3,32]{1,0:T(4,128)}, u32[]{:S(2)}) copy-start(f32[3,32]{1,0:T(4,128)} %param.28) | copy-start | bytes 1156
  615.1 514.0 %copy-start.45 = (f32[3,32]{1,0:T(4,128)S(1)}, f32[3,32]{1,0:T(4,128)}, u32[]{:S(2)}) copy-start(f32[3,32]{1,0:T(4,128)} %param.30) | copy-start | bytes 1156
  615.1 554.3 %copy-start.41 = (f32[602]{0:T(1024)S(1)}, f32[602]{0:T(1024)}, u32[]{:S(2)}) copy-start(f32[602]{0:T(1024)} %param.26) | copy-start | bytes 7228
  615.1 556.9 %copy-start.47 = (f32[121]{0:T(128)S(1)}, f32[121]{0:T(128)}, u32[]{:S(2)}) copy-start(f32[121]{0:T(128)} %param.33) | copy-start | bytes 1456
  615.1 558.3 %copy-start.38 = (f32[3,512]{1,0:T(4,128)S(1)}, f32[3,512]{1,0:T(4,128)}, u32[]{:S(2)}) copy-start(f32[3,512]{1,0:T(4,128)} %param.29) | copy-start | bytes 18436
  615.1 558.4 %copy-start.39 = (f32[3,512]{1,0:T(4,128)S(1)}, f32[3,512]{1,0:T(4,128)}, u32[]{:S(2)}) copy-start(f32[3,512]{1,0:T(4,128)} %param.31) | copy-start | bytes 18436
  615.2 560.0 %copy-start.30 = (f32[602,16]{0,1:T(8,128)S(1)}, f32[602,16]{0,1:T(8,128)}, u32[]{:S(2)}) copy-start(f32[602,16]{0,1:T(8,128)} %param.22) | copy-start | bytes 115588
  615.2 561.4 %copy-start.27 = (f32[3,32,512]{2,1,0:T(8,128)S(1)}, f32[3,32,512]{2,1,0:T(8,128)}, u32[]{:S(2)}) copy-start(f32[3,32,512]{2,1,0:T(8,128)} %param.24) | copy-start | bytes 589828
  615.2 563.2 %copy-start.28 = (f32[3,32,512]{2,1,0:T(8,128)S(1)}, f32[3,32,512]{2,1,0:T(8,128)}, u32[]{:S(2)}) copy-start(f32[3,32,512]{2,1,0:T(8,128)} %param.23) | copy-start | bytes 589828
  709.1 471.0 %copy-start.40 = (f32[16]{0:T(128)}, f32[16]{0:T(128)S(1)}, u32[]{:S(2)}) copy-start(f32[16]{0:T(128)S(1)} %get-tuple-element.122) | copy-start | bytes 196
  842.4 337.7 %copy-start.43 = (f32[16]{0:T(128)}, f32[16]{0:T(128)S(1)}, u32[]{:S(2)}) copy-start(f32[16]{0:T(128)S(1)} %add_multiply_fusion.10) | copy-start | bytes 196
  985.6 194.4 %copy-start.34 = (f32[3,32]{1,0:T(4,128)}, f32[3,32]{1,0:T(4,128)S(1)}, u32[]{:S(2)}) copy-start(f32[3,32]{1,0:T(4,128)S(1)} %get-tuple-element.126) | copy-start | bytes 1156
  1129.3 50.8 %copy-start.35 = (f32[3,32]{1,0:T(4,128)}, f32[3,32]{1,0:T(4,128)S(1)}, u32[]{:S(2)}) copy-start(f32[3,32]{1,0:T(4,128)S(1)} %get-tuple-element.124) | copy-start | bytes 1156
  1170.0 10.1 copy-start.36
  1172.7 7.4 copy-start.46
  1173.6 6.5 copy-start.31
  1173.7 6.4 copy-start.32
  (14 other events, 40.5 us)
Sparse Core Ops, SparseCore 0:
  10.9 59.6 all-gather.3
  73.5 71.9 all-gather.5
  148.4 68.4 all-gather.7
  575.8 131.7 reduce-scatter.10
  710.4 130.9 reduce-scatter.12
  844.2 140.2 reduce-scatter.6
  987.4 140.7 reduce-scatter.8

commit v2 on v1

v2 whole, which is shorter than its diff:
```python
import functools
import jax
import jax.numpy as jnp
from jax import lax
from jax.experimental import pallas as pl
from jax.experimental.pallas import tpu as pltpu
from jax.sharding import PartitionSpec as P

MESH = pl.DeviceIdType.MESH
LANES = 128
CORES = 2
f32 = jnp.float32
bf16 = jnp.bfloat16


norm_eps = 1e-06
stat_eps = 1e-30
clip_level = 0.5
step_rate = 0.04


def grid_of(mesh):
    wide, narrow = mesh.shape["wide"], mesh.shape["narrow"]
    far = 4 if wide % 4 == 0 else wide
    return far, wide // far, narrow // CORES, CORES


def place(dims):
    far, near, across, cores = dims
    wide, narrow = lax.axis_index("wide"), lax.axis_index("narrow")
    return wide // near, lax.rem(wide, near), narrow // cores, lax.rem(narrow, cores)


def device(dims, far_at, near_at, across_at, core_at):
    return (far_at * dims[1] + near_at, across_at * dims[3] + core_at)


def send(src, dst, send_sem, recv_sem, target):
    pltpu.make_async_remote_copy(
        src_ref=src,
        dst_ref=dst,
        send_sem=send_sem,
        recv_sem=recv_sem,
        device_id=target,
        device_id_type=MESH,
    ).start()


def arrived(dst, recv_sem):
    pltpu.make_async_copy(dst, dst, recv_sem).wait()


def left_source(src, send_sem):
    pltpu.make_async_copy(src, src, send_sem).wait()


def halves(value):
    high = value.astype(bf16)
    return high, (value - high.astype(f32)).astype(bf16)


def neighbours(dims, at):
    far, near, across, cores = dims
    p, q, x, c = at
    always = [(p, lax.rem(q + step, near), x, c) for step in range(1, near)]
    always += [(p, q, lax.rem(x + step, across), c) for step in range(1, across)]
    always += [(p, q, x, 1 - c)]
    return always


def entry_barrier(dims, at):
    barrier = pltpu.get_barrier_semaphore()
    announce(dims, at, barrier)
    await_all(dims, at, barrier)


def chunk(ref, k):
    return ref.at[:, pl.ds(k * LANES, LANES)]


class SpreadAll:
    def __init__(self, dims, at, own, every, right_out, left_out, near_out, across_out, core_out, came):
        self.dims, self.at, self.own, self.every = dims, at, own, every
        self.right_out, self.left_out, self.near_out = right_out, left_out, near_out
        self.across_out, self.core_out, self.came = across_out, core_out, came

    def away(self, distance):
        far, p = self.dims[0], self.at[0]
        if distance == 0:
            return [(p, None)]
        return [(p - distance, p >= distance), (p + distance, p + distance < far)]

    def when(self, flag, act):
        if flag is None:
            act()
        else:
            pl.when(flag)(act)

    def on_line(self, pp, src):
        far, near, across, cores = self.dims
        p, q, x, c = self.at
        dst = self.every.at[pp, q, x, c]
        sem = self.came.at[pp, q, x, c]

        @pl.when(jnp.logical_and(p < far - 1, pp <= p))
        def _():
            send(src, dst, self.right_out.at[pp], sem, device(self.dims, p + 1, q, x, c))

        @pl.when(jnp.logical_and(p > 0, pp >= p))
        def _():
            send(src, dst, self.left_out.at[pp], sem, device(self.dims, p - 1, q, x, c))

        for step in range(1, near):
            send(src, dst, self.near_out.at[pp, step - 1], sem, device(self.dims, p, lax.rem(q + step, near), x, c))

    def on_plane(self, pp, qq, src):
        far, near, across, cores = self.dims
        p, q, x, c = self.at
        dst, sem = self.every.at[pp, qq, x, c], self.came.at[pp, qq, x, c]
        for step in range(1, across):
            send(src, dst, self.across_out.at[pp, qq, step - 1], sem, device(self.dims, p, q, lax.rem(x + step, across), c))
        self.to_core(pp, qq, x, src)

    def to_core(self, pp, qq, xx, src):
        p, q, x, c = self.at
        send(src, self.every.at[pp, qq, xx, c], self.core_out.at[pp, qq, xx], self.came.at[pp, qq, xx, c], device(self.dims, p, q, x, 1 - c))

    def wait(self, *where):
        arrived(self.every.at[where], self.came.at[where])

    def begin(self):
        p, q, x, c = self.at
        self.on_line(p, self.own)
        self.on_plane(p, q, self.own)
        self.every[p, q, x, c] = self.own[...]

    def from_line(self, distance):
        p, q, x, c = self.at
        for pp, flag in self.away(distance):
            def act(pp=pp):
                self.wait(pp, q, x, c)
                self.on_line(pp, self.every.at[pp, q, x, c])
                self.on_plane(pp, q, self.every.at[pp, q, x, c])
            self.when(flag, act)

    def from_near(self, distance):
        far, near, across, cores = self.dims
        p, q, x, c = self.at
        for pp, flag in self.away(distance):
            def act(pp=pp):
                for step in range(1, near):
                    qq = lax.rem(q + step, near)
                    self.wait(pp, qq, x, c)
                    self.on_plane(pp, qq, self.every.at[pp, qq, x, c])
            self.when(flag, act)

    def from_across(self, distance):
        far, near, across, cores = self.dims
        p, q, x, c = self.at
        for pp, flag in self.away(distance):
            def act(pp=pp):
                for qq in range(near):
                    for step in range(1, across):
                        xx = lax.rem(x + step, across)
                        self.wait(pp, qq, xx, c)
                        self.to_core(pp, qq, xx, self.every.at[pp, qq, xx, c])
            self.when(flag, act)

    def step(self, distance):
        self.from_line(distance)
        self.from_near(distance - 1)
        if distance >= 2:
            self.from_across(distance - 2)

    def drain(self):
        far = self.dims[0]
        self.from_near(far - 1)
        if far >= 2:
            self.from_across(far - 2)

    def end(self):
        far, near, across, cores = self.dims
        p, q, x, c = self.at
        self.from_across(far - 1)
        for pp in range(far):
            for qq in range(near):
                for xx in range(across):
                    self.wait(pp, qq, xx, 1 - c)
        for pp in range(far):
            block = self.every.at[pp, q, x, c]

            @pl.when(jnp.logical_and(p < far - 1, pp <= p))
            def _(pp=pp, block=block):
                left_source(block, self.right_out.at[pp])

            @pl.when(jnp.logical_and(p > 0, pp >= p))
            def _(pp=pp, block=block):
                left_source(block, self.left_out.at[pp])

            for step in range(1, near):
                left_source(block, self.near_out.at[pp, step - 1])
            for qq in range(near):
                for step in range(1, across):
                    left_source(block, self.across_out.at[pp, qq, step - 1])
                for xx in range(across):
                    left_source(block, self.core_out.at[pp, qq, xx])


def spread_sems(dims):
    far, near, across, cores = dims
    dma = pltpu.SemaphoreType.DMA
    return [
        dma((far,)),
        dma((far,)),
        dma((far, max(near - 1, 1))),
        dma((far, near, max(across - 1, 1))),
        dma((far, near, across)),
        dma((far, near, across, cores)),
    ]


class Blocks:
    def __init__(self, pool, base, *shape):
        self.pool, self.base, self.shape = pool, base, shape

    @property
    def count(self):
        total = 1
        for size in self.shape:
            total *= size
        return total

    def flat(self, where):
        index = 0
        for size, at in zip(self.shape, where):
            index = index * size + at
        left = 1
        for size in self.shape[len(where) :]:
            left *= size
        return self.base + index * left, left

    def ref(self, *where):
        start, _ = self.flat(where)
        return self.pool.at[start]

    def run(self, *where):
        start, left = self.flat(where)
        return self.pool.at[pl.ds(start, left)]

    def add(self, where, other):
        ref = self.ref(*where)
        ref[...] = ref[...] + other[...]


def take(pool, *shapes):
    base, made = 0, []
    for shape in shapes:
        made.append(Blocks(pool, base, *shape))
        base += made[-1].count
    return made


def forward_blocks(dims, chunks):
    far, near, across, cores = dims
    return (
        (chunks, far, near),
        (chunks, cores, across),
        (chunks, across),
        (chunks, across),
    )


def backward_blocks(dims, chunks):
    far, near, across, cores = dims
    return (
        (chunks, across, cores),
        (chunks, far, near),
        (far, near),
        (chunks, far),
        (near,),
        (chunks,),
        (chunks, far, near),
    )


def blocks_of(shapes):
    total = 0
    for shape in shapes:
        size = 1
        for extent in shape:
            size *= extent
        total += size
    return total


def counted(dims, at):
    p, far = at[0], dims[0]
    ends = jnp.where(p > 0, 1, 0) + jnp.where(p < far - 1, 1, 0)
    return len(neighbours(dims, at)) + ends


def announce(dims, at, sem):
    far = dims[0]
    p, q, x, c = at
    for other in neighbours(dims, at):
        pl.semaphore_signal(sem, inc=1, device_id=device(dims, *other), device_id_type=MESH)

    @pl.when(p > 0)
    def _():
        pl.semaphore_signal(sem, inc=1, device_id=device(dims, p - 1, q, x, c), device_id_type=MESH)

    @pl.when(p < far - 1)
    def _():
        pl.semaphore_signal(sem, inc=1, device_id=device(dims, p + 1, q, x, c), device_id_type=MESH)


def await_all(dims, at, sem):
    pl.semaphore_wait(sem, counted(dims, at))


class Hooks:
    def __init__(self, **acts):
        self.acts = acts

    def run(self, name):
        for act in self.acts.get(name, ()):
            act()


def forward_pass(dims, at, chunks, adj, sent, out, pair, pool, sems, hooks):
    to_right, to_left, to_near, came, core_sems, across_out, across_in = sems
    gathered, part, from_core, from_across = take(pool, *forward_blocks(dims, chunks))
    far, near, across, cores = dims
    p, q, x, c = at
    nodes = sent.shape[0]
    early = chunks - 1
    right, left = device(dims, p + 1, q, x, c), device(dims, p - 1, q, x, c)
    others = [lax.rem(q + step, near) for step in range(1, near)]

    def go_right(k, pp, qq, src):
        @pl.when(p < far - 1)
        def _():
            send(src, gathered.ref(k, pp, qq), to_right.at[k, pp, qq], came.at[k, pp, qq], right)

    def go_left(k, pp, qq, src):
        @pl.when(p > 0)
        def _():
            send(src, gathered.ref(k, pp, qq), to_left.at[k, pp, qq], came.at[k, pp, qq], left)

    def go_near(k, pp, src):
        for step, qq in enumerate(others):
            send(src, gathered.ref(k, pp, q), to_near.at[k, pp, step], came.at[k, pp, q], device(dims, p, qq, x, c))

    hooks.run("begin")
    for k in [early] + list(range(chunks - 1)):
        src = chunk(sent, k)
        go_near(k, p, src)
        go_right(k, p, q, src)
        go_left(k, p, q, src)
    for k in range(chunks):
        gathered.ref(k, p, q)[...] = sent[:, k * LANES : (k + 1) * LANES]
    hooks.run("sent")
    for qq in others:
        arrived(gathered.ref(early, p, qq), came.at[early, p, qq])
        go_right(early, p, qq, gathered.ref(early, p, qq))
        go_left(early, p, qq, gathered.ref(early, p, qq))
    for step in range(1, far):
        hooks.run("step%d" % step)
        for k in range(chunks):
            for side in range(2):
                pp = p - step if side == 0 else p + step
                onward = go_right if side == 0 else go_left

                @pl.when(pp >= 0 if side == 0 else pp < far)
                def _(k=k, pp=pp, onward=onward):
                    for qq in [q] + (others if k == early else []):
                        block = gathered.ref(k, pp, qq)
                        arrived(block, came.at[k, pp, qq])
                        onward(k, pp, qq, block)
                    if k != early:
                        go_near(k, pp, gathered.ref(k, pp, q))

    hooks.run("drain")

    def reduce_across(k):
        arrived(from_core.run(k), core_sems.at[1, k])
        for step in range(1, across):
            xx = lax.rem(x + step, across)
            part.add((k, c, xx), from_core.ref(k, xx))
            send(part.ref(k, c, xx), from_across.ref(k, x), across_out.at[k, xx], across_in.at[k, x], device(dims, p, q, xx, c))

    def finish(k):
        total = part.ref(k, c, x)[...] + from_core.ref(k, x)[...]
        for step in range(1, across):
            xx = lax.rem(x + step, across)
            arrived(from_across.ref(k, xx), across_in.at[k, xx])
            total = total + from_across.ref(k, xx)[...]
        out[:, k * LANES : (k + 1) * LANES] = total

    for k in range(chunks):
        if k != early:
            for pp in range(far):
                for qq in others:
                    arrived(gathered.ref(k, pp, qq), came.at[k, pp, qq])
        high, low = halves(gathered.run(k)[...].reshape(far * near * nodes, LANES))
        pair[: far * near * nodes, :LANES] = high
        pair[: far * near * nodes, LANES:] = low

        def product(index, carry, k=k):
            cc = lax.rem(index // across + 1 + c, cores)
            xx = lax.rem(index, across)
            rows = pl.multiple_of((xx * cores + cc) * nodes, nodes)
            both = jnp.dot(adj[pl.ds(rows, nodes), :], pair[: far * near * nodes, :], preferred_element_type=f32)
            part.ref(k, cc, xx)[...] = both[:, :LANES] + both[:, LANES:]

            @pl.when(index == across - 1)
            def _():
                send(part.run(k, 1 - c), from_core.run(k), core_sems.at[0, k], core_sems.at[1, k], device(dims, p, q, x, 1 - c))

            return carry

        lax.fori_loop(0, cores * across, product, 0)
        if k >= 1:
            reduce_across(k - 1)
        if k >= 2:
            finish(k - 2)
    reduce_across(chunks - 1)
    if chunks >= 2:
        finish(chunks - 2)
    finish(chunks - 1)

    for k in range(chunks):
        left_source(part.run(k, 1 - c), core_sems.at[0, k])
        for step in range(1, across):
            xx = lax.rem(x + step, across)
            left_source(part.ref(k, c, xx), across_out.at[k, xx])
        for pp in range(far):
            for qq in [q] + (others if k == early else []):
                block = gathered.ref(k, pp, qq)

                @pl.when(jnp.logical_and(p < far - 1, pp <= p))
                def _(k=k, pp=pp, qq=qq, block=block):
                    left_source(block, to_right.at[k, pp, qq])

                @pl.when(jnp.logical_and(p > 0, pp >= p))
                def _(k=k, pp=pp, qq=qq, block=block):
                    left_source(block, to_left.at[k, pp, qq])

            def near_sent(k=k, pp=pp):
                for step in range(near - 1):
                    left_source(gathered.ref(k, pp, q), to_near.at[k, pp, step])

            if k == early:
                pl.when(pp == p)(near_sent)
            else:
                near_sent()


def forward_sems(dims, chunks):
    far, near, across, cores = dims
    dma = pltpu.SemaphoreType.DMA
    return [dma((chunks, far, near))] * 4 + [dma((2, chunks)), dma((chunks, across)), dma((chunks, across))]


def backward_pass(dims, at, chunks, adj, sent, out, pair, pool, sems, hooks):
    row_out, row_in, near_out, near_in, right_out, left_out, left_in, right_in = sems
    rows, part, line_early, line_rest, right_early, right_rest, from_near = take(
        pool, *backward_blocks(dims, chunks)
    )
    far, near, across, cores = dims
    p, q, x, c = at
    nodes = sent.shape[0]
    total_rows = across * cores * nodes
    early = 0
    right, left = device(dims, p + 1, q, x, c), device(dims, p - 1, q, x, c)
    others = [lax.rem(q + step, near) for step in range(1, near)]
    crossing = [lax.rem(x + step, across) for step in range(1, across)]

    def on_line(k, pp, qq):
        return line_early.ref(pp, qq) if k == early else line_rest.ref(k, pp)

    def from_right_own(k, qq):
        return right_early.ref(qq) if k == early else right_rest.ref(k)

    for k in range(chunks):
        src = chunk(sent, k)
        for xx in crossing:
            send(src, rows.ref(k, x, c), row_out.at[k, xx], row_in.at[k, x, c], device(dims, p, q, xx, c))
        send(src, rows.ref(k, x, c), row_out.at[k, across + x], row_in.at[k, x, c], device(dims, p, q, x, 1 - c))
    for k in range(chunks):
        rows.ref(k, x, c)[...] = sent[:, k * LANES : (k + 1) * LANES]
    hooks.run("sent")

    def dest(i):
        rights = far - 1 - p
        low = jnp.where(i < rights, far - 1 - i, jnp.where(i < far - 1, i - rights, p))
        high = jnp.where(i < p, i, jnp.where(i < far - 1, far - 1 - (i - p), p))
        return jnp.where(p < far // 2, low, high)

    def along(k, pp, qq):
        @pl.when(pp > p)
        def _():
            @pl.when(p > 0)
            def _():
                arrived(on_line(k, pp, qq), left_in.at[k, pp, qq])
                part.add((k, pp, qq), on_line(k, pp, qq))

            send(part.ref(k, pp, qq), on_line(k, pp, qq), right_out.at[k, pp, qq], left_in.at[k, pp, qq], right)

        @pl.when(pp < p)
        def _():
            @pl.when(p < far - 1)
            def _():
                arrived(on_line(k, pp, qq), right_in.at[k, pp, qq])
                part.add((k, pp, qq), on_line(k, pp, qq))

            @pl.when(pp < p - 1)
            def _():
                send(part.ref(k, pp, qq), on_line(k, pp, qq), left_out.at[k, pp, qq], right_in.at[k, pp, qq], left)

            @pl.when(pp == p - 1)
            def _():
                send(part.ref(k, pp, qq), from_right_own(k, qq), left_out.at[k, pp, qq], right_in.at[k, pp, qq], left)

    def settle(k, qq):
        @pl.when(p > 0)
        def _():
            arrived(on_line(k, p, qq), left_in.at[k, p, qq])
            part.add((k, p, qq), on_line(k, p, qq))

        @pl.when(p < far - 1)
        def _():
            arrived(from_right_own(k, qq), right_in.at[k, p, qq])
            part.add((k, p, qq), from_right_own(k, qq))

    def line(k):
        def step(i, carry):
            pp = dest(i)
            if k == early:
                for qq in others + [q]:
                    along(k, pp, qq)
            else:
                for qq in others:
                    arrived(from_near.ref(k, pp, qq), near_in.at[k, pp, qq])
                    part.add((k, pp, q), from_near.ref(k, pp, qq))
                along(k, pp, q)
            return carry

        lax.fori_loop(0, far, step, 0)

    def early_end():
        for step, qq in enumerate(others):
            settle(early, qq)
            send(part.ref(early, p, qq), from_near.ref(early, p, q), near_out.at[early, p, step], near_in.at[early, p, q], device(dims, p, qq, x, c))

    for k in range(chunks):
        for xx in crossing:
            arrived(rows.ref(k, xx, c), row_in.at[k, xx, c])
            send(rows.ref(k, xx, c), rows.ref(k, xx, c), row_out.at[k, across + xx], row_in.at[k, xx, c], device(dims, p, q, x, 1 - c))
        for xx in range(across):
            arrived(rows.ref(k, xx, 1 - c), row_in.at[k, xx, 1 - c])
        high, low = halves(rows.run(k)[...].reshape(total_rows, LANES))
        pair[:total_rows, :LANES] = high
        pair[:total_rows, LANES:] = low

        def product(i, carry, k=k):
            pp = dest(i // near)
            qq = lax.rem(q + 1 + lax.rem(i, near), near)
            start = pl.multiple_of((pp * near + qq) * nodes, nodes)
            both = lax.dot_general(adj[:, pl.ds(start, nodes)], pair[:total_rows, :], (((0,), (0,)), ((), ())), preferred_element_type=f32)
            part.ref(k, pp, qq)[...] = both[:, :LANES] + both[:, LANES:]
            if k != early:
                @pl.when(qq != q)
                def _():
                    send(part.ref(k, pp, qq), from_near.ref(k, pp, q), near_out.at[k, pp, lax.rem(qq - q - 1 + near, near)], near_in.at[k, pp, q], device(dims, p, qq, x, c))

            return carry

        lax.fori_loop(0, far * near, product, 0)
        if k >= 1:
            line(k - 1)
        hooks.run("chunk%d" % k)
    early_end()
    hooks.run("early")
    line(chunks - 1)
    hooks.run("line")
    for k in range(chunks):
        settle(k, q)
        total = part.ref(k, p, q)[...]
        if k == early:
            for qq in others:
                arrived(from_near.ref(k, p, qq), near_in.at[k, p, qq])
                total = total + from_near.ref(k, p, qq)[...]
        out[:, k * LANES : (k + 1) * LANES] = total

    for k in range(chunks):
        for xx in crossing:
            left_source(rows.ref(k, x, c), row_out.at[k, xx])
        for xx in range(across):
            left_source(rows.ref(k, xx, c), row_out.at[k, across + xx])
        for pp in range(far):
            for qq in [q] + (others if k == early else []):
                @pl.when(pp > p)
                def _(k=k, pp=pp, qq=qq):
                    left_source(part.ref(k, pp, qq), right_out.at[k, pp, qq])

                @pl.when(pp < p)
                def _(k=k, pp=pp, qq=qq):
                    left_source(part.ref(k, pp, qq), left_out.at[k, pp, qq])

            def near_sent(k=k, pp=pp):
                for step in range(near - 1):
                    left_source(part.ref(k, pp, q), near_out.at[k, pp, step])

            if k == early:
                pl.when(pp == p)(near_sent)
            else:
                near_sent()


def backward_sems(dims, chunks):
    far, near, across, cores = dims
    dma = pltpu.SemaphoreType.DMA
    return [dma((chunks, 2 * across)), dma((chunks, across, cores))] + [dma((chunks, far, near))] * 6


class ReduceAll:
    def __init__(self, dims, at, own, first_rows, out, bufs, sems):
        self.dims, self.at, self.own, self.first_rows, self.out = dims, at, own, first_rows, out
        self.halfway, self.from_across, self.from_near, self.from_left, self.from_right = bufs
        self.core_sems, self.across_out, self.across_in, self.near_out, self.near_in = sems[:5]
        self.right_out, self.left_out, self.left_in, self.right_in = sems[5:]
        self.depth = self.halfway.shape[4]

    def rows(self, j):
        return pl.ds(self.first_rows[j], self.depth)

    def core_stage(self, j):
        p, q, x, c = self.at
        send(self.own.at[:, :, :, 1 - c, self.rows(j)], self.halfway.at[j], self.core_sems.at[0, j], self.core_sems.at[1, j], device(self.dims, p, q, x, 1 - c))

    def across_stage(self, j):
        far, near, across, cores = self.dims
        p, q, x, c = self.at
        arrived(self.halfway.at[j], self.core_sems.at[1, j])
        self.halfway[j] = self.halfway[j] + self.own[:, :, :, c, self.rows(j)]
        for step in range(1, across):
            xx = lax.rem(x + step, across)
            send(self.halfway.at[j, :, :, xx], self.from_across.at[j, step - 1], self.across_out.at[j, step - 1], self.across_in.at[j, step - 1], device(self.dims, p, q, xx, c))

    def near_stage(self, j):
        far, near, across, cores = self.dims
        p, q, x, c = self.at
        for step in range(1, across):
            arrived(self.from_across.at[j, step - 1], self.across_in.at[j, step - 1])
            self.halfway[j, :, :, x] = self.halfway[j, :, :, x] + self.from_across[j, step - 1]
        for step in range(1, near):
            qq = lax.rem(q + step, near)
            send(self.halfway.at[j, :, qq, x], self.from_near.at[j, step - 1], self.near_out.at[j, step - 1], self.near_in.at[j, step - 1], device(self.dims, p, qq, x, c))

    def line_stage(self, j):
        far, near, across, cores = self.dims
        p, q, x, c = self.at
        for step in range(1, near):
            arrived(self.from_near.at[j, step - 1], self.near_in.at[j, step - 1])
            self.halfway[j, :, q, x] = self.halfway[j, :, q, x] + self.from_near[j, step - 1]
        for distance in range(far - 1, 0, -1):
            pp = p + distance

            @pl.when(pp < far)
            def _(pp=pp):
                @pl.when(p > 0)
                def _():
                    arrived(self.from_left.at[j, pp], self.left_in.at[j, pp])
                    self.halfway[j, pp, q, x] = self.halfway[j, pp, q, x] + self.from_left[j, pp]

                send(self.halfway.at[j, pp, q, x], self.from_left.at[j, pp], self.right_out.at[j, pp], self.left_in.at[j, pp], device(self.dims, p + 1, q, x, c))

            pm = p - distance

            @pl.when(pm >= 0)
            def _(pm=pm):
                @pl.when(p < far - 1)
                def _():
                    arrived(self.from_right.at[j, pm], self.right_in.at[j, pm])
                    self.halfway[j, pm, q, x] = self.halfway[j, pm, q, x] + self.from_right[j, pm]

                send(self.halfway.at[j, pm, q, x], self.from_right.at[j, pm], self.left_out.at[j, pm], self.right_in.at[j, pm], device(self.dims, p - 1, q, x, c))

    def last_stage(self, j, out_row):
        far, near, across, cores = self.dims
        p, q, x, c = self.at
        into = self.out.at[pl.ds(out_row, self.depth)]
        into[...] = self.halfway[j, p, q, x]

        @pl.when(p > 0)
        def _():
            arrived(self.from_left.at[j, p], self.left_in.at[j, p])
            into[...] = into[...] + self.from_left[j, p]

        @pl.when(p < far - 1)
        def _():
            arrived(self.from_right.at[j, p], self.right_in.at[j, p])
            into[...] = into[...] + self.from_right[j, p]

    def end(self, j):
        far, near, across, cores = self.dims
        p, q, x, c = self.at
        left_source(self.own.at[:, :, :, 1 - c, self.rows(j)], self.core_sems.at[0, j])
        for step in range(1, across):
            left_source(self.from_across.at[j, step - 1], self.across_out.at[j, step - 1])
        for step in range(1, near):
            left_source(self.from_near.at[j, step - 1], self.near_out.at[j, step - 1])
        for pp in range(far):
            @pl.when(pp > p)
            def _(pp=pp):
                left_source(self.from_left.at[j, pp], self.right_out.at[j, pp])

            @pl.when(pp < p)
            def _(pp=pp):
                left_source(self.from_right.at[j, pp], self.left_out.at[j, pp])


def reduce_scratch(dims, pieces, depth, width):
    far, near, across, cores = dims
    dma = pltpu.SemaphoreType.DMA
    bufs = [
        pltpu.VMEM((pieces, far, near, across, depth, width), f32),
        pltpu.VMEM((pieces, max(across - 1, 1), far, near, depth, width), f32),
        pltpu.VMEM((pieces, max(near - 1, 1), far, depth, width), f32),
        pltpu.VMEM((pieces, far, depth, width), f32),
        pltpu.VMEM((pieces, far, depth, width), f32),
    ]
    sems = [
        dma((2, pieces)),
        dma((pieces, max(across - 1, 1))),
        dma((pieces, max(across - 1, 1))),
        dma((pieces, max(near - 1, 1))),
        dma((pieces, max(near - 1, 1))),
    ] + [dma((pieces, far))] * 4
    return bufs, sems


def forward_kernel(dims, chunks, adj, sent, out, pair, pool, *sems):
    at = place(dims)
    entry_barrier(dims, at)
    forward_pass(dims, at, chunks, adj, sent, out, pair, pool, sems, Hooks())


def backward_kernel(dims, chunks, adj, sent, out, pair, pool, *sems):
    at = place(dims)
    entry_barrier(dims, at)
    backward_pass(dims, at, chunks, adj, sent, out, pair, pool, sems, Hooks())


def aggregate(dims, name_id, adj, sent, backward=False):
    far, near, across, cores = dims
    nodes, width = sent.shape
    chunks = width // LANES
    kernel = backward_kernel if backward else forward_kernel
    blocks = backward_blocks if backward else forward_blocks
    sems = backward_sems if backward else forward_sems
    depth = (across * cores if backward else far * near) * nodes
    return pl.pallas_call(
        functools.partial(kernel, dims, chunks),
        out_shape=jax.ShapeDtypeStruct((nodes, width), f32),
        in_specs=[pl.BlockSpec(memory_space=pltpu.VMEM)] * 2,
        out_specs=pl.BlockSpec(memory_space=pltpu.VMEM),
        scratch_shapes=[
            pltpu.VMEM((depth, 2 * LANES), bf16),
            pltpu.VMEM((blocks_of(blocks(dims, chunks)), nodes, LANES), f32),
        ]
        + sems(dims, chunks),
        compiler_params=pltpu.CompilerParams(
            collective_id=name_id, has_side_effects=True, vmem_limit_bytes=60 * 2**20
        ),
    )(adj, sent)


def contract(left, right, over):
    first, second = halves(left), halves(right)

    def go(a, b):
        return lax.dot_general(a, b, (over, ((), ())), preferred_element_type=f32)

    return go(first[0], second[0]) + (go(first[0], second[1]) + go(first[1], second[0]))


def plain(left, right):
    return contract(left, right, ((1,), (0,)))


def left_flip(left, right):
    return contract(left, right, ((0,), (0,)))


def right_flip(left, right):
    return contract(left, right, ((1,), (1,)))


def rows_of(every, half, start, size):
    far = every.shape[0]
    value = every[half * (far // 2) : (half + 1) * (far // 2), :, :, :, start : start + size, :]
    return value.reshape(-1, value.shape[-1])


def put_rows(every, half, start, size, value):
    far = every.shape[0]
    shape = (far // 2,) + every.shape[1:4] + (size, value.shape[-1])
    every[half * (far // 2) : (half + 1) * (far // 2), :, :, :, start : start + size, :] = value.reshape(shape)


def activation(pre_act):
    sig = jax.nn.sigmoid(pre_act)
    act = pre_act * sig
    return sig, act, lax.rsqrt(jnp.mean(act * act, -1, keepdims=True) + norm_eps)


def train_kernel(dims, in_width, classes, adj_hbm, feats, info, target, own0, own1, own2, red, notes, refs):
    far, near, across, cores = dims
    at = place(dims)
    nodes, wide_in = feats.shape
    width = own0.shape[1]
    block = own1.shape[0] // 2
    owns = (own0, own1, own2)
    layers = len(owns)
    every = (refs["every0"], refs["every1"], refs["every2"])
    adj, stage, stage_sems = refs["adj"], refs["stage"], refs["stage_sems"]
    pair, pool, sent = refs["pair"], refs["pool"], refs["sent"]
    raw, inverse, mix, direct, back = refs["raw"], refs["inverse"], refs["mix"], refs["direct"], refs["back"]
    agg, hid, pre, outer, ready = refs["agg"], refs["hid"], refs["pre"], refs["outer"], refs["ready"]
    in_chunks, chunks = wide_in // LANES, width // LANES
    head = 2 * block

    strip = stage.shape[1]

    def strip_copy(i):
        return pltpu.make_async_copy(adj_hbm.at[pl.ds(i * strip, strip)], stage.at[i % 2], stage_sems.at[i % 2])

    strips = adj.shape[0] // strip
    strip_copy(0).start()
    strip_copy(1).start()
    entry_barrier(dims, at)
    alpha = info[:, 0:1]
    weight = info[:, 1:2]
    lane = lax.broadcasted_iota(jnp.int32, (nodes, wide_in), 1)
    sent[...] = jnp.where(lane == in_width, 1.0, feats[...] * alpha)

    def load_adjacency():
        for i in range(strips):
            strip_copy(i).wait()
            adj[i * strip : (i + 1) * strip, :] = stage[i % 2].astype(f32).astype(bf16)
            if i + 2 < strips:
                strip_copy(i + 2).start()

    spreads = [SpreadAll(dims, at, owns[l], every[l], *refs["spread%d" % l]) for l in range(layers)]

    def mixing(layer):
        for half in range(2):
            side = rows_of(every[layer], half, 0, block)
            proj = rows_of(every[layer], half, block, block)
            mix[layer % 2, half] = plain(side, proj)

    def input_weights():
        def both(start):
            return jnp.concatenate([rows_of(every[0], half, start, block // 2) for half in range(2)], 0)

        first, second = both(head), both(head + block // 2)
        return jnp.concatenate([first, second[:, : wide_in - width]], 1)

    def ahead(layer):
        def act():
            spreads[layer].drain()
            spreads[layer].end()
            mixing(layer)
            if layer == 0:
                hid[0] = right_flip(feats[...], input_weights())
            direct[...] = plain(hid[layer], mix[layer % 2, 0])
            if layer + 1 < layers:
                spreads[layer + 1].begin()

        return act

    rounds = iter(range(ready.shape[0]))
    for layer in range(layers):
        acts = {"drain": [ahead(layer)]}
        for step in range(1, far):
            acts["step%d" % step] = [functools.partial(spreads[layer].step, step)]
        if layer == 0:
            acts["begin"] = [spreads[0].begin]
            acts["sent"] = [load_adjacency]
            forward_pass(dims, at, in_chunks, adj, sent, raw, pair, pool, refs["forward"], Hooks(**acts))
            turn = ready.at[next(rounds)]
            announce(dims, at, turn)
            inverse[...] = jnp.broadcast_to(1.0 / (1.0 + raw[:, in_width : in_width + 1]), inverse.shape)
            raw[...] = raw[...] * inverse[:, 0:1]
            agg[0] = right_flip(raw[...], input_weights())
        else:
            forward_pass(dims, at, chunks, adj, sent, agg.at[layer], pair, pool, refs["forward"], Hooks(**acts))
            turn = ready.at[next(rounds)]
            announce(dims, at, turn)
            agg[layer] = agg[layer] * inverse[:, 0:1]
        pre_act = direct[...] + plain(agg[layer], mix[layer % 2, 1])
        pre[layer] = pre_act
        _, act, scale = activation(pre_act)
        after = act * scale
        hid[layer + 1] = after
        if layer + 1 < layers:
            sent[:, :width] = after * alpha
        await_all(dims, at, turn)

    def output_weights():
        at_lane = wide_in - width
        return jnp.concatenate(
            [rows_of(every[0], half, head + block // 2, block // 2)[:, at_lane : at_lane + LANES] for half in range(2)], 0
        )

    tail = wide_in - width + LANES
    labelled = jnp.sum(every[0][:, :, :, :, head + block // 2 : head + block // 2 + 8, tail : tail + LANES].reshape(-1, 8, LANES), 0)[0:1, 0:1]
    notes[...] = jnp.broadcast_to(labelled, notes.shape)
    head_weights = output_weights()
    logits = plain(hid[layers], head_weights)
    column = lax.broadcasted_iota(jnp.int32, logits.shape, 1)
    soft = jnp.maximum(logits, 0.0) + jnp.log(1.0 + jnp.exp(-jnp.abs(logits)))
    each = jnp.where(column < classes, soft - target[...] * logits, 0.0)
    loss = jnp.sum(weight * jnp.sum(each, -1, keepdims=True), 0, keepdims=True)
    d_logits = jnp.where(column < classes, (weight / labelled) * (jax.nn.sigmoid(logits) - target[...]), 0.0)
    g_out = left_flip(hid[layers], d_logits)
    d_out = right_flip(d_logits, head_weights)
    start = head + block // 2
    half_rows = width // 2
    for half in range(2):
        piece = jnp.concatenate(
            [
                jnp.zeros((half_rows, wide_in - width), f32),
                g_out[half * half_rows : (half + 1) * half_rows],
                jnp.broadcast_to(loss, (half_rows, width - tail)),
            ],
            1,
        )
        put_rows(every[0], half, start, block // 2, piece)

    reduces = [
        ReduceAll(dims, at, every[l], [0, block, head], red, refs["reduce_bufs"], refs["reduce_sems"]) for l in range(layers)
    ]

    def slope(layer, d_out):
        pre_act = pre[layer]
        sig, act, scale = activation(pre_act)
        normed = act * scale
        d_act = scale * (d_out - normed * jnp.mean(d_out * normed, -1, keepdims=True))
        return d_act * sig * (1.0 + pre_act * (1.0 - sig))

    def outers(layer, d_pre):
        outer[0] = left_flip(hid[layer], d_pre)
        outer[1] = left_flip(agg[layer], d_pre)

    def weight_grads(layer, half):
        side = rows_of(every[layer], half, 0, block)
        proj = rows_of(every[layer], half, block, block)
        g_side = right_flip(outer[half], proj)
        g_proj = left_flip(side, outer[half])
        put_rows(every[layer], half, 0, block, g_side)
        put_rows(every[layer], half, block, block, g_proj)

    base = [0, 3 * block, 5 * block]

    def finish_reduce(layer, pieces):
        for j in pieces:
            reduces[layer].last_stage(j, base[layer] + j * block)
        for j in pieces:
            reduces[layer].end(j)

    d_pre_ref = refs["d_pre"]
    carried, freed = [], []
    for layer in range(layers - 1, 0, -1):
        d_pre_ref[...] = slope(layer, d_out)
        sent[:, :width] = d_pre_ref[...] * inverse[:, 0:1]

        def grads(layer=layer):
            outers(layer, d_pre_ref[...])
            for half in range(2):
                weight_grads(layer, half)
            if freed:
                await_all(dims, at, freed.pop())
            for j in range(2):
                reduces[layer].core_stage(j)

        def direct_part(layer=layer):
            direct[...] = right_flip(d_pre_ref[...], mix[layer % 2, 0])

        def stage(name, layer=layer):
            for j in range(2):
                getattr(reduces[layer], name)(j)

        acts = {
            "chunk0": carried[:1],
            "chunk1": carried[1:] + [direct_part],
            "chunk2": [grads],
            "chunk3": [functools.partial(stage, "across_stage")],
            "early": [functools.partial(mixing, 0)] if layer == 1 else [],
            "line": [functools.partial(stage, "near_stage")],
        }
        backward_pass(dims, at, chunks, adj, sent, back, pair, pool, refs["backward"], Hooks(**acts))
        if layer > 1:
            turn = ready.at[next(rounds)]
            announce(dims, at, turn)
        d_out = direct[...] + right_flip(back[...] * alpha, mix[layer % 2, 1])
        if layer > 1:
            await_all(dims, at, turn)

        def close(layer=layer):
            finish_reduce(layer, range(2))
            freed.append(ready.at[next(rounds)])
            announce(dims, at, freed[0])

        carried = [functools.partial(stage, "line_stage"), close]

    d_pre = slope(0, d_out)
    d_pre_ref[...] = d_pre
    carried[0]()
    d_self = right_flip(d_pre, mix[0, 0])
    d_neigh = right_flip(d_pre, mix[0, 1])
    g_in = left_flip(d_self, feats[...]) + left_flip(d_neigh, raw[...])
    for half in range(2):
        top = slice(half * half_rows, (half + 1) * half_rows)
        put_rows(every[0], half, head, block // 2, g_in[top, :width])
        where = (slice(half * (far // 2), (half + 1) * (far // 2)),) + (slice(None),) * 3
        value = g_in[top, width:]
        every[0][where + (slice(head + block // 2, head + block), slice(0, wide_in - width))] = value.reshape(
            (far // 2, near, across, cores, block // 2, wide_in - width)
        )
    carried[1]()
    await_all(dims, at, freed.pop())
    final = reduces[0]
    final.core_stage(2)
    outers(0, d_pre)
    for half in range(2):
        weight_grads(0, half)
    final.core_stage(0)
    final.core_stage(1)
    for name in ("across_stage", "near_stage", "line_stage"):
        for j in (2, 0, 1):
            getattr(final, name)(j)
    finish_reduce(0, (2, 0, 1))


def train_on_device(dims, name_id, in_width, classes, adjacency, feats, info, target, owns):
    far, near, across, cores = dims
    nodes, wide_in = feats.shape
    width = owns[0].shape[1]
    block = owns[1].shape[0] // 2
    in_chunks, chunks = wide_in // LANES, width // LANES
    layers = len(owns)
    dma = pltpu.SemaphoreType.DMA
    pool = max(blocks_of(forward_blocks(dims, in_chunks)), blocks_of(backward_blocks(dims, chunks)))
    bufs, sems = reduce_scratch(dims, 3, block, width)
    strip = 128
    vmem = pl.BlockSpec(memory_space=pltpu.VMEM)
    refs = {
        "adj": pltpu.VMEM(adjacency.shape, bf16),
        "stage": pltpu.VMEM((2, strip, adjacency.shape[1]), jnp.int32),
        "stage_sems": dma((2,)),
        "pair": pltpu.VMEM((max(far * near, across * cores) * nodes, 2 * LANES), bf16),
        "pool": pltpu.VMEM((pool, nodes, LANES), f32),
        "sent": pltpu.VMEM((nodes, wide_in), f32),
        "raw": pltpu.VMEM((nodes, wide_in), f32),
        "inverse": pltpu.VMEM((nodes, LANES), f32),
        "mix": pltpu.VMEM((2, 2, width, width), f32),
        "direct": pltpu.VMEM((nodes, width), f32),
        "back": pltpu.VMEM((nodes, width), f32),
        "d_pre": pltpu.VMEM((nodes, width), f32),
        "agg": pltpu.VMEM((layers, nodes, width), f32),
        "hid": pltpu.VMEM((layers + 1, nodes, width), f32),
        "pre": pltpu.VMEM((layers, nodes, width), f32),
        "outer": pltpu.VMEM((2, width, width), f32),
        "ready": pltpu.SemaphoreType.REGULAR((3 * layers - 3,)),
        "forward": forward_sems(dims, in_chunks),
        "backward": backward_sems(dims, chunks),
        "reduce_bufs": bufs,
        "reduce_sems": sems,
    }
    for layer in range(layers):
        refs["every%d" % layer] = pltpu.VMEM(dims + owns[layer].shape, f32)
        refs["spread%d" % layer] = spread_sems(dims)
    return pl.pallas_call(
        functools.partial(train_kernel, dims, in_width, classes),
        out_shape=(
            jax.ShapeDtypeStruct((7 * block, width), f32),
            jax.ShapeDtypeStruct((8, LANES), f32),
        ),
        in_specs=[pl.BlockSpec(memory_space=pl.ANY)] + [vmem] * (3 + layers),
        out_specs=(vmem, vmem),
        scratch_shapes=[refs],
        compiler_params=pltpu.CompilerParams(
            collective_id=name_id, has_side_effects=True, vmem_limit_bytes=63 * 2**20
        ),
    )(adjacency, feats, info, target, *owns)


def dot(left, right, over=((1,), (0,))):
    return lax.dot_general(
        left, right, (over, ((), ())), precision=lax.Precision.HIGH, preferred_element_type=f32
    )


def left_t(left, right):
    return dot(left, right, ((0,), (0,)))


def right_t(left, right):
    return dot(left, right, ((1,), (1,)))


def pad_lanes(value, lanes):
    return jnp.pad(value, ((0, 0), (0, lanes - value.shape[1])))


def fits_on_chip(adjacency):
    return 2 * adjacency.shape[0] * adjacency.shape[1] <= 4 * 2**20


def gradients_fused(dims, features, adjacency, labels, labelled, node_count, w_in, w_side, w_proj, w_out):
    layers, block, width = w_side.shape
    nodes, in_width = features.shape
    classes = w_out.shape[1]
    wide_in = -(-(in_width + 1) // LANES) * LANES
    counts = node_count.astype(f32)
    alpha = 2.0 / (1.0 + counts)
    weight_mask = labelled.astype(f32)
    feats = pad_lanes(features, wide_in)
    info = pad_lanes(jnp.stack([alpha, weight_mask * lax.rsqrt(counts)], 1), LANES)
    target = pad_lanes(labels.astype(f32), LANES)
    w_in_t = pad_lanes(w_in.T, wide_in)
    tail = width - (wide_in - width) - LANES
    count = jnp.broadcast_to(jnp.sum(weight_mask), (block // 2, tail))
    head = jnp.concatenate(
        [w_in_t[:, :width], jnp.concatenate([w_in_t[:, width:], pad_lanes(w_out, LANES), count], 1)], 0
    )
    owns = [
        jnp.concatenate([w_side[l], w_proj[l]] + ([head] if l == 0 else []), 0) for l in range(layers)
    ]
    red, notes = train_on_device(dims, 1, in_width, classes, adjacency, feats, info, target, owns)
    start = [0, 3 * block, 5 * block]
    red_side = jnp.stack([red[at : at + block] for at in start])
    red_proj = jnp.stack([red[at + block : at + 2 * block] for at in start])
    first, second = red[2 * block : 2 * block + block // 2], red[2 * block + block // 2 : 3 * block]
    red_in = jnp.concatenate([first, second[:, : in_width - width]], 1).T
    at_lane = wide_in - width
    red_out = second[:, at_lane : at_lane + classes]
    return second[0, at_lane + LANES], notes[0, 0], red_in, red_side, red_proj, red_out


def gradients_apart(
    dims,
    features,
    adjacency,
    labels,
    labelled,
    node_count,
    w_in,
    w_side,
    w_proj,
    w_out,
):
    layers = w_side.shape[0]
    width = w_side.shape[2]
    in_width = features.shape[1]
    nodes = features.shape[0]
    both = ("wide", "narrow")
    adj = adjacency.astype(bf16)
    counts = node_count.astype(f32)
    alpha = 2.0 / (1.0 + counts)
    lam = lax.rsqrt(counts)
    target = labels.astype(f32)
    weight_mask = labelled.astype(f32)

    spare = -(in_width + 1) % LANES
    sent = jnp.concatenate(
        [alpha[:, None] * features, jnp.ones((nodes, 1), f32), jnp.zeros((nodes, spare), f32)], 1
    )
    summed = aggregate(dims, 1, adj, sent)
    inverse = 1.0 / (1.0 + summed[:, in_width : in_width + 1])
    agg_features = summed[:, :in_width] * inverse

    full_in, full_side, full_proj, full_out = (
        lax.all_gather(w_in, both, axis=1, tiled=True),
        lax.all_gather(w_side, both, axis=1, tiled=True),
        lax.all_gather(w_proj, both, axis=1, tiled=True),
        lax.all_gather(w_out, both, axis=0, tiled=True),
    )
    mix_self = [dot(full_side[l, :width], full_proj[l, :width]) for l in range(layers)]
    mix_neigh = [dot(full_side[l, width:], full_proj[l, width:]) for l in range(layers)]

    kept = []
    hidden = dot(features, full_in)
    agg = dot(agg_features, full_in)
    for layer in range(layers):
        if layer > 0:
            agg = aggregate(dims, 1 + layer, adj, alpha[:, None] * hidden) * inverse
        pre_act = dot(hidden, mix_self[layer]) + dot(agg, mix_neigh[layer])
        kept.append((hidden, agg, pre_act))
        act = jax.nn.silu(pre_act)
        hidden = act * lax.rsqrt(jnp.mean(act * act, -1, keepdims=True) + norm_eps)

    logits = dot(hidden, full_out)
    per = jnp.sum(jax.nn.softplus(logits) - target * logits, -1)
    loss_sum, label_count = lax.psum(
        (jnp.sum(weight_mask * lam * per), jnp.sum(weight_mask)), both
    )
    d_logits = (weight_mask * lam / label_count)[:, None] * (jax.nn.sigmoid(logits) - target)
    g_out = left_t(hidden, d_logits)
    d_out = right_t(d_logits, full_out)
    side_grads = [None] * layers
    proj_grads = [None] * layers
    for layer in reversed(range(layers)):
        hidden, agg, pre_act = kept[layer]
        sig = jax.nn.sigmoid(pre_act)
        act = pre_act * sig
        scale = lax.rsqrt(jnp.mean(act * act, -1, keepdims=True) + norm_eps)
        normed = act * scale
        d_act = scale * (d_out - normed * jnp.mean(d_out * normed, -1, keepdims=True))
        d_pre = d_act * sig * (1.0 + pre_act * (1.0 - sig))
        outer_self = left_t(hidden, d_pre)
        outer_neigh = left_t(agg, d_pre)
        side, proj = full_side[layer], full_proj[layer]
        side_grads[layer] = jnp.concatenate(
            [right_t(outer_self, proj[:width]), right_t(outer_neigh, proj[width:])], 0
        )
        proj_grads[layer] = jnp.concatenate(
            [left_t(side[:width], outer_self), left_t(side[width:], outer_neigh)], 0
        )
        d_self = right_t(d_pre, mix_self[layer])
        if layer > 0:
            back = aggregate(dims, 3 + layer, adj, d_pre * inverse, backward=True)
            d_out = d_self + right_t(alpha[:, None] * back, mix_neigh[layer])
        else:
            g_in = left_t(features, d_self) + left_t(agg_features, right_t(d_pre, mix_neigh[layer]))
    red_in, red_side, red_proj, red_out = (
        lax.psum_scatter(g_in, both, scatter_dimension=1, tiled=True),
        lax.psum_scatter(jnp.stack(side_grads), both, scatter_dimension=1, tiled=True),
        lax.psum_scatter(jnp.stack(proj_grads), both, scatter_dimension=1, tiled=True),
        lax.psum_scatter(g_out, both, scatter_dimension=0, tiled=True),
    )
    return loss_sum, label_count, red_in, red_side, red_proj, red_out


def step_on_device(
    dims,
    features,
    adjacency,
    labels,
    labelled,
    node_count,
    w_in,
    w_side,
    w_proj,
    w_out,
    row_in,
    col_in,
    row_side,
    col_side,
    row_proj,
    col_proj,
    row_out,
    col_out,
):
    width = w_side.shape[2]
    in_width = features.shape[1]
    classes = w_out.shape[1]
    both = ("wide", "narrow")
    gradients = gradients_fused if fits_on_chip(adjacency) else gradients_apart
    loss_sum, label_count, red_in, red_side, red_proj, red_out = gradients(
        dims, features, adjacency, labels, labelled, node_count, w_in, w_side, w_proj, w_out
    )
    sq_in = red_in * red_in
    sq_side = red_side * red_side
    sq_proj = red_proj * red_proj
    sq_out = red_out * red_out
    new_col_in = 0.5 * col_in + 0.5 * (jnp.mean(sq_in, 0) + stat_eps)
    new_row_side = 0.5 * row_side + 0.5 * (jnp.mean(sq_side, 2) + stat_eps)
    new_row_proj = 0.5 * row_proj + 0.5 * (jnp.mean(sq_proj, 2) + stat_eps)
    new_row_out = 0.5 * row_out + 0.5 * (jnp.mean(sq_out, 1) + stat_eps)
    (
        sum_row_in,
        sum_col_side,
        sum_col_proj,
        sum_col_out,
        total_side,
        total_proj,
        total_out,
        over_in,
        over_side,
        over_proj,
        over_out,
    ) = lax.psum(
        (
            jnp.sum(sq_in, 1),
            jnp.sum(sq_side, 1),
            jnp.sum(sq_proj, 1),
            jnp.sum(sq_out, 0),
            jnp.sum(new_row_side, 1),
            jnp.sum(new_row_proj, 1),
            jnp.sum(new_row_out),
            jnp.sum(sq_in / new_col_in[None, :], 1),
            jnp.sum(sq_side / new_row_side[:, :, None], 1),
            jnp.sum(sq_proj / new_row_proj[:, :, None], 1),
            jnp.sum(sq_out / new_row_out[:, None], 0),
        ),
        both,
    )
    new_row_in = 0.5 * row_in + 0.5 * (sum_row_in / width + stat_eps)
    new_col_side = 0.5 * col_side + 0.5 * (sum_col_side / (2 * width) + stat_eps)
    new_col_proj = 0.5 * col_proj + 0.5 * (sum_col_proj / (2 * width) + stat_eps)
    new_col_out = 0.5 * col_out + 0.5 * (sum_col_out / width + stat_eps)
    mean_in = jnp.mean(new_row_in)
    mean_side = total_side / (2 * width)
    mean_proj = total_proj / (2 * width)
    mean_out = total_out / width
    up_in = red_in * lax.rsqrt(new_row_in[:, None] * new_col_in[None, :] / mean_in)
    up_side = red_side * lax.rsqrt(
        new_row_side[:, :, None] * new_col_side[:, None, :] / mean_side[:, None, None]
    )
    up_proj = red_proj * lax.rsqrt(
        new_row_proj[:, :, None] * new_col_proj[:, None, :] / mean_proj[:, None, None]
    )
    up_out = red_out * lax.rsqrt(new_row_out[:, None] * new_col_out[None, :] / mean_out)
    ms_in = mean_in * jnp.sum(over_in / new_row_in) / (in_width * width)
    ms_side = mean_side * jnp.sum(over_side / new_col_side, 1) / (2 * width * width)
    ms_proj = mean_proj * jnp.sum(over_proj / new_col_proj, 1) / (2 * width * width)
    ms_out = mean_out * jnp.sum(over_out / new_col_out) / (width * classes)
    fac_in = 1.0 / jnp.maximum(1.0, jnp.sqrt(ms_in) / clip_level)
    fac_side = 1.0 / jnp.maximum(1.0, jnp.sqrt(ms_side) / clip_level)
    fac_proj = 1.0 / jnp.maximum(1.0, jnp.sqrt(ms_proj) / clip_level)
    fac_out = 1.0 / jnp.maximum(1.0, jnp.sqrt(ms_out) / clip_level)
    new_in = w_in - step_rate * (up_in * fac_in)
    new_side = w_side - step_rate * (up_side * fac_side[:, None, None])
    new_proj = w_proj - step_rate * (up_proj * fac_proj[:, None, None])
    new_out = w_out - step_rate * (up_out * fac_out)
    return (
        loss_sum,
        label_count,
        red_in,
        red_side,
        red_proj,
        red_out,
        new_in,
        new_side,
        new_proj,
        new_out,
        new_row_in,
        new_col_in,
        new_row_side,
        new_col_side,
        new_row_proj,
        new_col_proj,
        new_row_out,
        new_col_out,
    )


def solution(mesh):
    in_specs = (
        P(("wide", "narrow"), None),
        P("wide", "narrow"),
        P(("wide", "narrow"), None),
        P(("wide", "narrow")),
        P(("wide", "narrow")),
        P(None, ("wide", "narrow")),
        P(None, ("wide", "narrow"), None),
        P(None, ("wide", "narrow"), None),
        P(("wide", "narrow"), None),
        P(),
        P(("wide", "narrow")),
        P(None, ("wide", "narrow")),
        P(),
        P(None, ("wide", "narrow")),
        P(),
        P(("wide", "narrow")),
        P(),
    )
    out_specs = (
        P(),
        P(),
        P(None, ("wide", "narrow")),
        P(None, ("wide", "narrow"), None),
        P(None, ("wide", "narrow"), None),
        P(("wide", "narrow"), None),
        P(None, ("wide", "narrow")),
        P(None, ("wide", "narrow"), None),
        P(None, ("wide", "narrow"), None),
        P(("wide", "narrow"), None),
        P(),
        P(("wide", "narrow")),
        P(None, ("wide", "narrow")),
        P(),
        P(None, ("wide", "narrow")),
        P(),
        P(("wide", "narrow")),
        P(),
    )
    shards = functools.partial(step_on_device, grid_of(mesh))
    return jax.shard_map(shards, mesh=mesh, in_specs=in_specs, out_specs=out_specs, check_vma=False)
```

time: 1200 us -> 567 us (0.47)
  waiting for transfers between devices: 564 us -> 0 us
  Pallas kernels: 365 us -> 492 us
  blocking collectives: 120 us -> 40.1 us
  matrix products: 71.9 us -> 0 us
  other arithmetic: 39.7 us -> 11.7 us
  between operations: 18.4 us -> 4.24 us
    reduce_scatter x3 -> x0, waiting for transfers between devices: 376 us -> none  [the longest x1 142 us: step_on_device(): lax.psum_scatter(jnp.stack(proj_grads), both, scatter_dimension=1, tiled=...]
    unnamed x8 -> x0, waiting for transfers between devices: 134 us -> none
    pallas_call x5 -> x1, Pallas kernels: 365 us -> 492 us  [train_on_device(): pl.pallas_call(functools.partial(train_kernel, dims, in_width, classes),...]
    dot_general x43 -> x0, matrix products: 71.9 us -> none  [dot(): lax.dot_general(left, right, (over, ((), ())), precision=lax.Precision.HI...]
    all_gather x3 -> x0, waiting for transfers between devices: 54.4 us -> none  [the longest x1 54.3 us: step_on_device(): lax.all_gather(w_proj, both, axis=1, tiled=True)]
    all_gather x1 -> x0, blocking collectives: 44.6 us -> none  [step_on_device(): lax.all_gather(w_out, both, axis=0, tiled=True)]
    psum x2 -> x1, blocking collectives: 75.3 us -> 40.1 us  [step_on_device(): lax.psum((jnp.sum(sq_in, 1), jnp.sum(sq_side, 1), jnp.sum(sq_proj, 1), jn...]
  transfers between devices with their start and end apart: 7 -> 0, of which waited for: 5 -> 0; matrix products, arithmetic and copies ran while one was open for 5% -> 0% of each run, Pallas kernels for 8% -> 0%
where the time goes in v2:
time: 567 us; the launch traced here: 561 us
  Pallas kernels  492 us (87%)
  blocking collectives  40.1 us (7%)
  local copies, waits for them, and re-layouts  12.6 us (2%)
  other arithmetic  11.7 us (2%)
    pallas_call x1, Pallas kernels, train_on_device(): pl.pallas_call(functools.partial(train_kernel, dims, in_width, classes),...  492 us
    psum x1, blocking collectives, step_on_device(): lax.psum((jnp.sum(sq_in, 1), jnp.sum(sq_side, 1), jnp.sum(sq_proj, 1), jn...  40.1 us

profile of v2, /device:TPU:0, one launch (start us, length us, event | category | flops | bytes accessed | tf_op | source)
XLA Modules:
  0.0 561.1 jit_solution(13819507546381005052)
XLA Ops:
  0.7 1.3 copy.39
  2.0 0.0 copy-start.17
  2.0 0.0 copy-start.5
  2.1 0.0 copy-start.13
  2.1 0.0 copy-start.2
  2.1 0.0 copy-start.14
  2.1 0.0 copy-start.3
  2.1 0.9 pad.20.feats
  3.0 1.3 convert_reduce_fusion
  4.3 0.1 copy.40
  4.5 0.7 pad.21.info
  5.1 0.9 convert_element_type.21
  6.1 0.7 pad.22.target
  6.7 0.6 broadcast_in_dim.2
  7.4 0.7 pad_slice_fusion
  8.1 0.8 slice.81
  8.8 0.9 slice_bitcast_fusion.6
  9.8 0.9 slice_bitcast_fusion.7
  10.7 1.4 fusion.1.own0
  12.1 0.7 pad_maximum_fusion.2.own1
  12.7 0.7 pad_maximum_fusion.3.own2
  13.4 492.4 %shard_map.304 = (f32[224,512]{1,0:T(8,128)}, f32[8,128]{1,0:T(8,128)}) custom-call(s32[1024,2048]{1,0:T(8,128)} %adj_hbm.1, f32[256,640]{1,0:T(8,128)} %pad.20.feats, f32[256,128]{1,0:T(8,128)} %pad.21.info, f32[256,128]{1,0:T(8,128)} %pad.22.target, f32[96,512]{1,0:T(8,128)} %fusion.1.own0, f32[64,512]{1,0:T(8,128)} %pad_maximum_fusion.2.own1, ...), custom_call_target="tpu_custom_call" | custom-call | tf_op jit(solution)/shard_map/pallas_call | solution.py:1086
  505.8 1.2 slice.70
  507.0 1.2 slice.71
  508.2 0.7 slice.73
  508.9 0.8 slice.72
  509.7 0.1 multiply_reduce_fusion.4
  509.8 1.0 slice_bitcast_fusion.2
  510.8 0.1 multiply_reduce_fusion.3
  510.9 0.1 multiply_reduce_fusion.1
  511.1 0.8 multiply_reduce_fusion.7
  511.9 0.6 fusion.4
  512.5 0.1 divide_reduce_fusion.2
  512.6 0.1 fusion.5
  512.8 0.0 copy-start.10
  512.8 0.0 copy-start.11
  512.8 0.1 multiply_reduce_fusion.2
  512.9 0.1 multiply_reduce_fusion
  513.0 0.1 multiply_reduce_fusion.6
  513.1 40.1 %all-reduce.5 = (f32[602]{0:T(1024)S(1)}, f32[602]{0:T(1024)S(1)}, f32[3,512]{1,0:T(4,128)S(1)}, f32[3,512]{1,0:T(4,128)S(1)}, f32[3]{0:T(128)S(1)}, /*index=5*/...) all-reduce(f32[602]{0:T(1024)S(1)} %get-tuple-element.26, ...), channel_id=1, replica_groups=mesh['wide'=8,'narrow'=4] {'wide','narrow'}, use_global_device_ids=true, to_apply=%region_6.7 | all-reduce | flops 7597 | bytes 60776 | tf_op jit(solution)/shard_map/psum | solution.py:1296
  553.2 0.6 divide_reduce_fusion.6
  555.2 0.7 multiply_subtract_fusion.2
  555.9 0.1 divide_reduce_fusion.5
  556.1 0.8 multiply_subtract_fusion.1
  556.9 0.1 divide_reduce_fusion.4
  557.0 0.8 multiply_subtract_fusion
  558.5 0.6 divide_reduce_fusion.7
  559.9 0.7 multiply_subtract_fusion.3
  (43 shorter events, 0.1 us)
Async XLA Ops:
  0.7 511.2 %copy-start.21 = (f32[16]{0:T(128)S(1)}, f32[16]{0:T(128)}, u32[]{:S(2)}) copy-start(f32[16]{0:T(128)} %param.32) | copy-start | bytes 196
  0.7 511.2 %copy-start.22 = (f32[16]{0:T(128)S(1)}, f32[16]{0:T(128)}, u32[]{:S(2)}) copy-start(f32[16]{0:T(128)} %param.27) | copy-start | bytes 196
  0.7 511.9 %copy-start.18 = (f32[3,32]{1,0:T(4,128)S(1)}, f32[3,32]{1,0:T(4,128)}, u32[]{:S(2)}) copy-start(f32[3,32]{1,0:T(4,128)} %param.30) | copy-start | bytes 1156
  0.7 511.9 %copy-start.19 = (f32[3,32]{1,0:T(4,128)S(1)}, f32[3,32]{1,0:T(4,128)}, u32[]{:S(2)}) copy-start(f32[3,32]{1,0:T(4,128)} %param.28) | copy-start | bytes 1156
  2.0 551.2 %copy-start.17 = (f32[602]{0:T(1024)S(1)}, f32[602]{0:T(1024)}, u32[]{:S(2)}) copy-start(f32[602]{0:T(1024)} %param.26) | copy-start | bytes 7228
  2.0 553.1 %copy-start.5 = (f32[602,16]{0,1:T(8,128)S(1)}, f32[602,16]{0,1:T(8,128)}, u32[]{:S(2)}) copy-start(f32[602,16]{0,1:T(8,128)} %param.22) | copy-start | bytes 115588
  2.1 553.8 %copy-start.13 = (f32[3,512]{1,0:T(4,128)S(1)}, f32[3,512]{1,0:T(4,128)}, u32[]{:S(2)}) copy-start(f32[3,512]{1,0:T(4,128)} %param.29) | copy-start | bytes 18436
  2.1 554.0 %copy-start.2 = (f32[3,32,512]{2,1,0:T(8,128)S(1)}, f32[3,32,512]{2,1,0:T(8,128)}, u32[]{:S(2)}) copy-start(f32[3,32,512]{2,1,0:T(8,128)} %param.23) | copy-start | bytes 589828
  2.1 554.8 %copy-start.14 = (f32[3,512]{1,0:T(4,128)S(1)}, f32[3,512]{1,0:T(4,128)}, u32[]{:S(2)}) copy-start(f32[3,512]{1,0:T(4,128)} %param.31) | copy-start | bytes 18436
  2.1 554.9 %copy-start.3 = (f32[3,32,512]{2,1,0:T(8,128)S(1)}, f32[3,32,512]{2,1,0:T(8,128)}, u32[]{:S(2)}) copy-start(f32[3,32,512]{2,1,0:T(8,128)} %param.24) | copy-start | bytes 589828
  3.0 555.5 %copy-start.23 = (f32[121]{0:T(128)S(1)}, f32[121]{0:T(128)}, u32[]{:S(2)}) copy-start(f32[121]{0:T(128)} %param.33) | copy-start | bytes 1456
  3.0 556.9 %copy-start.9 = (f32[16,121]{1,0:T(8,128)S(1)}, f32[16,121]{1,0:T(8,128)}, u32[]{:S(2)}) copy-start(f32[16,121]{1,0:T(8,128)} %param.25) | copy-start | bytes 23236
  509.8 50.8 %copy-start.4 = (f32[602,16]{0,1:T(8,128)}, f32[602,16]{0,1:T(8,128)S(1)}, u32[]{:S(2)}) copy-start(f32[602,16]{0,1:T(8,128)S(1)} %get-tuple-element.63) | copy-start | bytes 115588
  510.9 49.6 %copy-start = (f32[3,32,512]{2,1,0:T(8,128)}, f32[3,32,512]{2,1,0:T(8,128)S(1)}, u32[]{:S(2)}) copy-start(f32[3,32,512]{2,1,0:T(8,128)S(1)} %get-tuple-element.61) | copy-start | bytes 589828
  511.0 49.5 %copy-start.1 = (f32[3,32,512]{2,1,0:T(8,128)}, f32[3,32,512]{2,1,0:T(8,128)S(1)}, u32[]{:S(2)}) copy-start(f32[3,32,512]{2,1,0:T(8,128)S(1)} %get-tuple-element.57) | copy-start | bytes 589828
  511.9 48.7 %copy-start.6 = (f32[16,121]{1,0:T(8,128)}, f32[16,121]{1,0:T(8,128)S(1)}, u32[]{:S(2)}) copy-start(f32[16,121]{1,0:T(8,128)S(1)} %get-tuple-element.53) | copy-start | bytes 23236
  512.5 48.0 %copy-start.15 = (f32[16]{0:T(128)}, f32[16]{0:T(128)S(1)}, u32[]{:S(2)}) copy-start(f32[16]{0:T(128)S(1)} %get-tuple-element.85) | copy-start | bytes 196
  512.5 48.0 %copy-start.16 = (f32[16]{0:T(128)}, f32[16]{0:T(128)S(1)}, u32[]{:S(2)}) copy-start(f32[16]{0:T(128)S(1)} %get-tuple-element.51) | copy-start | bytes 196
  512.8 47.8 %copy-start.10 = (f32[3,32]{1,0:T(4,128)}, f32[3,32]{1,0:T(4,128)S(1)}, u32[]{:S(2)}) copy-start(f32[3,32]{1,0:T(4,128)S(1)} %get-tuple-element.55) | copy-start | bytes 1156
  512.8 47.8 %copy-start.11 = (f32[3,32]{1,0:T(4,128)}, f32[3,32]{1,0:T(4,128)S(1)}, u32[]{:S(2)}) copy-start(f32[3,32]{1,0:T(4,128)S(1)} %get-tuple-element.84) | copy-start | bytes 1156
  553.8 6.8 %copy-start.12 = (f32[602]{0:T(1024)}, f32[602]{0:T(1024)S(1)}, u32[]{:S(2)}) copy-start(f32[602]{0:T(1024)S(1)} %get-tuple-element.49) | copy-start | bytes 7228
  556.0 4.6 copy-start.7
  557.0 3.6 copy-start.8
  559.1 1.5 copy-start.20

commit v3 on v2

--- a/solution.py
+++ b/solution.py
@@ -68,10 +68,18 @@
     return always
 
 
+def line_peers(dims, at):
+    far = dims[0]
+    p, q, x, c = at
+    return [(lax.rem(p + step, far), q, x, c) for step in range(1, far)]
+
+
 def entry_barrier(dims, at):
     barrier = pltpu.get_barrier_semaphore()
-    announce(dims, at, barrier)
-    await_all(dims, at, barrier)
+    everyone = neighbours(dims, at) + line_peers(dims, at)
+    for other in everyone:
+        pl.semaphore_signal(barrier, inc=1, device_id=device(dims, *other), device_id_type=MESH)
+    pl.semaphore_wait(barrier, len(everyone))
 
 
 def chunk(ref, k):
@@ -79,8 +87,8 @@
 
 
 class SpreadAll:
-    def __init__(self, dims, at, own, every, right_out, left_out, near_out, across_out, core_out, came):
-        self.dims, self.at, self.own, self.every = dims, at, own, every
+    def __init__(self, dims, at, every, right_out, left_out, near_out, across_out, core_out, came):
+        self.dims, self.at, self.every = dims, at, every
         self.right_out, self.left_out, self.near_out = right_out, left_out, near_out
         self.across_out, self.core_out, self.came = across_out, core_out, came
 
@@ -130,9 +138,9 @@
 
     def begin(self):
         p, q, x, c = self.at
-        self.on_line(p, self.own)
-        self.on_plane(p, q, self.own)
-        self.every[p, q, x, c] = self.own[...]
+        own = self.every.at[p, q, x, c]
+        self.on_line(p, own)
+        self.on_plane(p, q, own)
 
     def from_line(self, distance):
         p, q, x, c = self.at
@@ -364,23 +372,78 @@
         arrived(gathered.ref(early, p, qq), came.at[early, p, qq])
         go_right(early, p, qq, gathered.ref(early, p, qq))
         go_left(early, p, qq, gathered.ref(early, p, qq))
-    for step in range(1, far):
-        hooks.run("step%d" % step)
-        for k in range(chunks):
-            for side in range(2):
-                pp = p - step if side == 0 else p + step
-                onward = go_right if side == 0 else go_left
-
-                @pl.when(pp >= 0 if side == 0 else pp < far)
-                def _(k=k, pp=pp, onward=onward):
-                    for qq in [q] + (others if k == early else []):
-                        block = gathered.ref(k, pp, qq)
-                        arrived(block, came.at[k, pp, qq])
-                        onward(k, pp, qq, block)
-                    if k != early:
-                        go_near(k, pp, gathered.ref(k, pp, q))
-
-    hooks.run("drain")
+    group = near * nodes
+
+    def accumulate(k, pp, fresh):
+        high, low = halves(gathered.run(k, pp)[...].reshape(group, LANES))
+        pair[:group, :LANES] = high
+        pair[:group, LANES:] = low
+        columns = pl.ds(pl.multiple_of(pp * group, group), group)
+
+        def product(index, carry):
+            cc = lax.rem(index // across + 1 + c, cores)
+            xx = lax.rem(index, across)
+            rows = pl.multiple_of((xx * cores + cc) * nodes, nodes)
+            both = jnp.dot(adj[pl.ds(rows, nodes), columns], pair[:group, :], preferred_element_type=f32)
+            both = both[:, :LANES] + both[:, LANES:]
+            into = part.ref(k, cc, xx)
+            into[...] = both if fresh else into[...] + both
+            return carry
+
+        lax.fori_loop(0, cores * across, product, 0)
+
+    def from_near(k, pp):
+        if isinstance(k, int) and k == early:
+            return
+
+        def act():
+            for qq in others:
+                arrived(gathered.ref(k, pp, qq), came.at[k, pp, qq])
+
+        if isinstance(k, int):
+            act()
+        else:
+            pl.when(k != early)(act)
+
+    def sides(distance):
+        if distance == 0:
+            return [(p, p >= 0)]
+        return [(p - distance, p >= distance), (p + distance, p + distance < far)]
+
+    def from_line(step, k):
+        for pp, flag in sides(step):
+
+            @pl.when(flag)
+            def _(pp=pp):
+                for qq in [q] + (others if k == early else []):
+                    block = gathered.ref(k, pp, qq)
+                    arrived(block, came.at[k, pp, qq])
+
+                    @pl.when(pp < p)
+                    def _():
+                        go_right(k, pp, qq, block)
+
+                    @pl.when(pp > p)
+                    def _():
+                        go_left(k, pp, qq, block)
+
+                if k != early:
+                    go_near(k, pp, gathered.ref(k, pp, q))
+
+    def take_in(k, distance):
+        for pp, flag in sides(distance):
+
+            @pl.when(flag)
+            def _(pp=pp):
+                from_near(k, pp)
+                accumulate(k, pp, distance == 0)
+
+    def every_chunk(distance):
+        def act(k, carry):
+            take_in(k, distance)
+            return carry
+
+        lax.fori_loop(0, chunks, act, 0)
 
     def reduce_across(k):
         arrived(from_core.run(k), core_sems.at[1, k])
@@ -397,37 +460,29 @@
             total = total + from_across.ref(k, xx)[...]
         out[:, k * LANES : (k + 1) * LANES] = total
 
-    for k in range(chunks):
-        if k != early:
-            for pp in range(far):
-                for qq in others:
-                    arrived(gathered.ref(k, pp, qq), came.at[k, pp, qq])
-        high, low = halves(gathered.run(k)[...].reshape(far * near * nodes, LANES))
-        pair[: far * near * nodes, :LANES] = high
-        pair[: far * near * nodes, LANES:] = low
-
-        def product(index, carry, k=k):
-            cc = lax.rem(index // across + 1 + c, cores)
-            xx = lax.rem(index, across)
-            rows = pl.multiple_of((xx * cores + cc) * nodes, nodes)
-            both = jnp.dot(adj[pl.ds(rows, nodes), :], pair[: far * near * nodes, :], preferred_element_type=f32)
-            part.ref(k, cc, xx)[...] = both[:, :LANES] + both[:, LANES:]
-
-            @pl.when(index == across - 1)
-            def _():
-                send(part.run(k, 1 - c), from_core.run(k), core_sems.at[0, k], core_sems.at[1, k], device(dims, p, q, x, 1 - c))
-
-            return carry
-
-        lax.fori_loop(0, cores * across, product, 0)
-        if k >= 1:
-            reduce_across(k - 1)
-        if k >= 2:
-            finish(k - 2)
-    reduce_across(chunks - 1)
+    for step in range(1, far):
+        hooks.run("step%d" % step)
+        for k in range(chunks):
+            from_line(step, k)
+            if step == far - 1 and step >= 2:
+                take_in(k, step - 1)
+        if step == 1 or step < far - 1:
+            every_chunk(step - 1)
+    hooks.run("drain")
+    order = list(range(chunks))
+    for i, k in enumerate(order):
+        take_in(k, far - 1)
+        send(part.run(k, 1 - c), from_core.run(k), core_sems.at[0, k], core_sems.at[1, k], device(dims, p, q, x, 1 - c))
+        if i >= 1:
+            reduce_across(order[i - 1])
+        if i >= 2:
+            finish(order[i - 2])
+    hooks.run("product")
+    reduce_across(order[-1])
+    hooks.run("shadow")
     if chunks >= 2:
-        finish(chunks - 2)
-    finish(chunks - 1)
+        finish(order[-2])
+    finish(order[-1])
 
     for k in range(chunks):
         left_source(part.run(k, 1 - c), core_sems.at[0, k])
@@ -627,43 +682,52 @@
 class ReduceAll:
     def __init__(self, dims, at, own, first_rows, out, bufs, sems):
         self.dims, self.at, self.own, self.first_rows, self.out = dims, at, own, first_rows, out
-        self.halfway, self.from_across, self.from_near, self.from_left, self.from_right = bufs
-        self.core_sems, self.across_out, self.across_in, self.near_out, self.near_in = sems[:5]
+        self.halfway, self.from_first, self.from_next, self.from_left, self.from_right = bufs
+        self.core_sems, self.first_out, self.first_in, self.next_out, self.next_in = sems[:5]
         self.right_out, self.left_out, self.left_in, self.right_in = sems[5:]
         self.depth = self.halfway.shape[4]
+        self.turned = [False] * len(first_rows)
 
     def rows(self, j):
         return pl.ds(self.first_rows[j], self.depth)
+
+    def peers(self, turned):
+        far, near, across, cores = self.dims
+        p, q, x, c = self.at
+        if turned:
+            return [(lax.rem(q + step, near), device(self.dims, p, lax.rem(q + step, near), x, c)) for step in range(1, near)]
+        return [(lax.rem(x + step, across), device(self.dims, p, q, lax.rem(x + step, across), c)) for step in range(1, across)]
 
     def core_stage(self, j):
         p, q, x, c = self.at
         send(self.own.at[:, :, :, 1 - c, self.rows(j)], self.halfway.at[j], self.core_sems.at[0, j], self.core_sems.at[1, j], device(self.dims, p, q, x, 1 - c))
 
     def across_stage(self, j):
-        far, near, across, cores = self.dims
         p, q, x, c = self.at
         arrived(self.halfway.at[j], self.core_sems.at[1, j])
         self.halfway[j] = self.halfway[j] + self.own[:, :, :, c, self.rows(j)]
-        for step in range(1, across):
-            xx = lax.rem(x + step, across)
-            send(self.halfway.at[j, :, :, xx], self.from_across.at[j, step - 1], self.across_out.at[j, step - 1], self.across_in.at[j, step - 1], device(self.dims, p, q, xx, c))
+        for i, (other, target) in enumerate(self.peers(self.turned[j])):
+            src = self.halfway.at[j, :, other] if self.turned[j] else self.halfway.at[j, :, :, other]
+            send(src, self.from_first.at[j, i], self.first_out.at[j, i], self.first_in.at[j, i], target)
 
     def near_stage(self, j):
-        far, near, across, cores = self.dims
         p, q, x, c = self.at
-        for step in range(1, across):
-            arrived(self.from_across.at[j, step - 1], self.across_in.at[j, step - 1])
-            self.halfway[j, :, :, x] = self.halfway[j, :, :, x] + self.from_across[j, step - 1]
-        for step in range(1, near):
-            qq = lax.rem(q + step, near)
-            send(self.halfway.at[j, :, qq, x], self.from_near.at[j, step - 1], self.near_out.at[j, step - 1], self.near_in.at[j, step - 1], device(self.dims, p, qq, x, c))
+        for i, _ in enumerate(self.peers(self.turned[j])):
+            arrived(self.from_first.at[j, i], self.first_in.at[j, i])
+            if self.turned[j]:
+                self.halfway[j, :, q] = self.halfway[j, :, q] + self.from_first[j, i]
+            else:
+                self.halfway[j, :, :, x] = self.halfway[j, :, :, x] + self.from_first[j, i]
+        for i, (other, target) in enumerate(self.peers(not self.turned[j])):
+            src = self.halfway.at[j, :, q, other] if self.turned[j] else self.halfway.at[j, :, other, x]
+            send(src, self.from_next.at[j, i], self.next_out.at[j, i], self.next_in.at[j, i], target)
 
     def line_stage(self, j):
         far, near, across, cores = self.dims
         p, q, x, c = self.at
-        for step in range(1, near):
-            arrived(self.from_near.at[j, step - 1], self.near_in.at[j, step - 1])
-            self.halfway[j, :, q, x] = self.halfway[j, :, q, x] + self.from_near[j, step - 1]
+        for i, _ in enumerate(self.peers(not self.turned[j])):
+            arrived(self.from_next.at[j, i], self.next_in.at[j, i])
+            self.halfway[j, :, q, x] = self.halfway[j, :, q, x] + self.from_next[j, i]
         for distance in range(far - 1, 0, -1):
             pp = p + distance
 
@@ -707,10 +771,10 @@
         far, near, across, cores = self.dims
         p, q, x, c = self.at
         left_source(self.own.at[:, :, :, 1 - c, self.rows(j)], self.core_sems.at[0, j])
-        for step in range(1, across):
-            left_source(self.from_across.at[j, step - 1], self.across_out.at[j, step - 1])
-        for step in range(1, near):
-            left_source(self.from_near.at[j, step - 1], self.near_out.at[j, step - 1])
+        for i, _ in enumerate(self.peers(self.turned[j])):
+            left_source(self.from_first.at[j, i], self.first_out.at[j, i])
+        for i, _ in enumerate(self.peers(not self.turned[j])):
+            left_source(self.from_next.at[j, i], self.next_out.at[j, i])
         for pp in range(far):
             @pl.when(pp > p)
             def _(pp=pp):
@@ -816,21 +880,40 @@
     return sig, act, lax.rsqrt(jnp.mean(act * act, -1, keepdims=True) + norm_eps)
 
 
-def train_kernel(dims, in_width, classes, adj_hbm, feats, info, target, own0, own1, own2, red, notes, refs):
+def column_of(row):
+    size = row.shape[1]
+    same = lax.broadcasted_iota(jnp.int32, (size, size), 0) == lax.broadcasted_iota(jnp.int32, (size, size), 1)
+    return jnp.sum(jnp.where(same, jnp.broadcast_to(row, (size, size)), 0.0), 1, keepdims=True)
+
+
+def row_of(column):
+    size = column.shape[0]
+    same = lax.broadcasted_iota(jnp.int32, (size, size), 0) == lax.broadcasted_iota(jnp.int32, (size, size), 1)
+    return jnp.sum(jnp.where(same, jnp.broadcast_to(column, (size, size)), 0.0), 0, keepdims=True)
+
+
+def blend(old, mean_square):
+    return 0.5 * old + 0.5 * (mean_square + stat_eps)
+
+
+def row_statistic(grad, old, count):
+    square = grad * grad
+    return square, blend(old, jnp.sum(square, 1, keepdims=True) / count)
+
+
+def train_kernel(dims, in_width, classes, adj_hbm, feats, info, w_in_t, w_side, w_proj, w_out, col_in, row_side, row_proj, row_out, red, stat, refs):
     far, near, across, cores = dims
     at = place(dims)
     nodes, wide_in = feats.shape
-    width = own0.shape[1]
-    block = own1.shape[0] // 2
-    owns = (own0, own1, own2)
-    layers = len(owns)
-    every = (refs["every0"], refs["every1"], refs["every2"])
+    layers, block, width = w_side.shape
+    every = [refs["every%d" % layer] for layer in range(layers)]
     adj, stage, stage_sems = refs["adj"], refs["stage"], refs["stage_sems"]
     pair, pool, sent = refs["pair"], refs["pool"], refs["sent"]
     raw, inverse, mix, direct, back = refs["raw"], refs["inverse"], refs["mix"], refs["direct"], refs["back"]
     agg, hid, pre, outer, ready = refs["agg"], refs["hid"], refs["pre"], refs["outer"], refs["ready"]
     in_chunks, chunks = wide_in // LANES, width // LANES
     head = 2 * block
+    tail = wide_in - width + LANES
 
     strip = stage.shape[1]
 
@@ -840,9 +923,21 @@
     strips = adj.shape[0] // strip
     strip_copy(0).start()
     strip_copy(1).start()
+    for layer in range(layers):
+        mine = every[layer].at[at]
+        mine[:block] = w_side[layer]
+        mine[block : 2 * block] = w_proj[layer]
+    mine = every[0].at[at]
+    mine[head : head + block // 2] = w_in_t[:, :width]
+    mine[head + block // 2 : head + block, : wide_in - width] = w_in_t[:, width:]
+    mine[head + block // 2 : head + block, wide_in - width : tail] = jnp.zeros((block // 2, LANES), f32)
+    mine[head + block // 2 : head + block, wide_in - width : wide_in - width + classes] = w_out[...]
+    marked = jnp.sum(info[:, LANES + 2 : LANES + 3], 0, keepdims=True)
+    mine[head + block // 2 : head + block, tail:] = jnp.broadcast_to(marked, (block // 2, width - tail))
     entry_barrier(dims, at)
-    alpha = info[:, 0:1]
-    weight = info[:, 1:2]
+    target = info[:, :LANES]
+    alpha = info[:, LANES : LANES + 1]
+    weight = info[:, LANES + 1 : LANES + 2]
     lane = lax.broadcasted_iota(jnp.int32, (nodes, wide_in), 1)
     sent[...] = jnp.where(lane == in_width, 1.0, feats[...] * alpha)
 
@@ -853,7 +948,7 @@
             if i + 2 < strips:
                 strip_copy(i + 2).start()
 
-    spreads = [SpreadAll(dims, at, owns[l], every[l], *refs["spread%d" % l]) for l in range(layers)]
+    spreads = [SpreadAll(dims, at, every[l], *refs["spread%d" % l]) for l in range(layers)]
 
     def mixing(layer):
         for half in range(2):
@@ -868,22 +963,21 @@
         first, second = both(head), both(head + block // 2)
         return jnp.concatenate([first, second[:, : wide_in - width]], 1)
 
+    def onward(layer):
+        spreads[layer].drain()
+        if layer + 1 < layers:
+            spreads[layer + 1].begin()
+
     def ahead(layer):
-        def act():
-            spreads[layer].drain()
-            spreads[layer].end()
-            mixing(layer)
-            if layer == 0:
-                hid[0] = right_flip(feats[...], input_weights())
-            direct[...] = plain(hid[layer], mix[layer % 2, 0])
-            if layer + 1 < layers:
-                spreads[layer + 1].begin()
-
-        return act
+        spreads[layer].end()
+        mixing(layer)
+        if layer == 0:
+            hid[0] = right_flip(feats[...], input_weights())
+        direct[...] = plain(hid[layer], mix[layer % 2, 0])
 
     rounds = iter(range(ready.shape[0]))
     for layer in range(layers):
-        acts = {"drain": [ahead(layer)]}
+        acts = {"drain": [functools.partial(onward, layer)], "shadow": [functools.partial(ahead, layer)]}
         for step in range(1, far):
             acts["step%d" % step] = [functools.partial(spreads[layer].step, step)]
         if layer == 0:
@@ -893,7 +987,7 @@
             turn = ready.at[next(rounds)]
             announce(dims, at, turn)
             inverse[...] = jnp.broadcast_to(1.0 / (1.0 + raw[:, in_width : in_width + 1]), inverse.shape)
-            raw[...] = raw[...] * inverse[:, 0:1]
+            raw[...] = jnp.where(lane < in_width, raw[...] * inverse[:, 0:1], 0.0)
             agg[0] = right_flip(raw[...], input_weights())
         else:
             forward_pass(dims, at, chunks, adj, sent, agg.at[layer], pair, pool, refs["forward"], Hooks(**acts))
@@ -915,16 +1009,15 @@
             [rows_of(every[0], half, head + block // 2, block // 2)[:, at_lane : at_lane + LANES] for half in range(2)], 0
         )
 
-    tail = wide_in - width + LANES
     labelled = jnp.sum(every[0][:, :, :, :, head + block // 2 : head + block // 2 + 8, tail : tail + LANES].reshape(-1, 8, LANES), 0)[0:1, 0:1]
-    notes[...] = jnp.broadcast_to(labelled, notes.shape)
+    refs["marks"][...] = jnp.broadcast_to(labelled, refs["marks"].shape)
     head_weights = output_weights()
     logits = plain(hid[layers], head_weights)
     column = lax.broadcasted_iota(jnp.int32, logits.shape, 1)
     soft = jnp.maximum(logits, 0.0) + jnp.log(1.0 + jnp.exp(-jnp.abs(logits)))
-    each = jnp.where(column < classes, soft - target[...] * logits, 0.0)
+    each = jnp.where(column < classes, soft - target * logits, 0.0)
     loss = jnp.sum(weight * jnp.sum(each, -1, keepdims=True), 0, keepdims=True)
-    d_logits = jnp.where(column < classes, (weight / labelled) * (jax.nn.sigmoid(logits) - target[...]), 0.0)
+    d_logits = jnp.where(column < classes, (weight / labelled) * (jax.nn.sigmoid(logits) - target), 0.0)
     g_out = left_flip(hid[layers], d_logits)
     d_out = right_flip(d_logits, head_weights)
     start = head + block // 2
@@ -964,12 +1057,71 @@
         put_rows(every[layer], half, block, block, g_proj)
 
     base = [0, 3 * block, 5 * block]
+    sums = refs["sums"]
+    sums[...] = jnp.zeros_like(sums)
+    spot = lax.broadcasted_iota(jnp.int32, (1, wide_in), 1)
+    slot = 2 * layers
+
+    def note_total(index, new_row):
+        total = jnp.sum(new_row, 0, keepdims=True)
+        sums[slot + 1 : slot + 2] = sums[slot + 1 : slot + 2] + jnp.where(spot == LANES + index, total, 0.0)
+
+    def note_layer(layer):
+        for kind, old in enumerate((row_side, row_proj)):
+            start = base[layer] + kind * block
+            square, new_row = row_statistic(red[start : start + block], column_of(old[layer : layer + 1]), width)
+            index = kind * layers + layer
+            sums[index : index + 1, :width] = jnp.sum(square, 0, keepdims=True)
+            sums[slot + 2 + index : slot + 3 + index, :width] = jnp.sum(square / new_row, 0, keepdims=True)
+            note_total(index, new_row)
+
+    def note_head():
+        first, second = red[head : head + block // 2], red[head + block // 2 : head + block]
+        square = jnp.concatenate([first * first, second[:, : wide_in - width] * second[:, : wide_in - width]], 1)
+        new_col = blend(column_of(col_in[...]), jnp.sum(square, 1, keepdims=True) / in_width)
+        sums[slot : slot + 1] = jnp.sum(square, 0, keepdims=True)
+        sums[2 * slot + 2 : 2 * slot + 3] = jnp.sum(square / new_col, 0, keepdims=True)
+        square, new_row = row_statistic(second[:, wide_in - width : tail], column_of(row_out[...]), classes)
+        sums[slot + 1 : slot + 2, :LANES] = jnp.sum(square, 0, keepdims=True)
+        sums[2 * slot + 3 : 2 * slot + 4, :LANES] = jnp.sum(square / new_row, 0, keepdims=True)
+        note_total(slot, new_row)
+
+    def sum_everywhere(stat):
+        far, near, across, cores = dims
+        p, q, x, c = at
+        came_in, out_sems, in_sems = refs["sum_in"], refs["sum_out"], refs["sum_came"]
+        groups = [
+            [device(dims, p, q, x, 1 - c)],
+            [device(dims, p, q, lax.rem(x + step, across), c) for step in range(1, across)],
+            [device(dims, p, lax.rem(q + step, near), x, c) for step in range(1, near)],
+            [device(dims, *other) for other in line_peers(dims, at)],
+        ]
+        base_slot = 0
+        for turn, group in enumerate(groups):
+            for i, target in enumerate(group):
+                at_slot = base_slot + i
+                send(sums.at[pl.ds(turn * stat.shape[0], stat.shape[0])], came_in.at[at_slot], out_sems.at[at_slot], in_sems.at[at_slot], target)
+            total = sums[turn * stat.shape[0] : (turn + 1) * stat.shape[0]]
+            for i in range(len(group)):
+                at_slot = base_slot + i
+                arrived(came_in.at[at_slot], in_sems.at[at_slot])
+                total = total + came_in[at_slot]
+            base_slot += len(group)
+            if turn + 1 < len(groups):
+                sums[(turn + 1) * stat.shape[0] : (turn + 2) * stat.shape[0]] = total
+            else:
+                stat[...] = total
+                stat[2 * slot + 4 : 2 * slot + 5, :LANES] = jnp.broadcast_to(refs["marks"][0:1, 0:1], (1, LANES))
+        for at_slot in range(base_slot):
+            left_source(came_in.at[at_slot], out_sems.at[at_slot])
+
 
     def finish_reduce(layer, pieces):
         for j in pieces:
             reduces[layer].last_stage(j, base[layer] + j * block)
         for j in pieces:
             reduces[layer].end(j)
+        note_layer(layer)
 
     d_pre_ref = refs["d_pre"]
     carried, freed = [], []
@@ -1033,29 +1185,92 @@
     carried[1]()
     await_all(dims, at, freed.pop())
     final = reduces[0]
+    final.turned = [near == across, False, False]
     final.core_stage(2)
     outers(0, d_pre)
-    for half in range(2):
-        weight_grads(0, half)
+    weight_grads(0, 0)
+    weight_grads(0, 1)
     final.core_stage(0)
     final.core_stage(1)
-    for name in ("across_stage", "near_stage", "line_stage"):
-        for j in (2, 0, 1):
-            getattr(final, name)(j)
+    final.across_stage(2)
+    final.across_stage(0)
+    final.across_stage(1)
+    final.near_stage(2)
+    final.near_stage(0)
+    final.near_stage(1)
+    final.line_stage(2)
+    final.line_stage(0)
+    final.line_stage(1)
     finish_reduce(0, (2, 0, 1))
-
-
-def train_on_device(dims, name_id, in_width, classes, adjacency, feats, info, target, owns):
+    note_head()
+    sum_everywhere(stat)
+
+
+def update_kernel(in_width, classes, red, stat, w_in_t, w_side, w_proj, w_out, row_in, col_in, row_side, col_side, row_proj, col_proj, row_out, col_out, loss, count, g_in, g_side, g_proj, g_out, n_in, n_side, n_proj, n_out, s_row_in, s_col_in, s_row_side, s_col_side, s_row_proj, s_col_proj, s_row_out, s_col_out):
+    layers, block, width = w_side.shape
+    head = 2 * block
+    wide_in = w_in_t.shape[1]
+    tail = wide_in - width + LANES
+    slot = 2 * layers
+    base = [0, 3 * block, 5 * block]
+
+    def step_of(weight, grad, new_row, new_col, mean, over, size):
+        update = grad * lax.rsqrt(new_row * new_col / mean)
+        factor = 1.0 / jnp.maximum(1.0, jnp.sqrt(mean * over / size) / clip_level)
+        return weight - step_rate * (update * factor)
+
+    def total_of(index):
+        return stat[slot + 1 : slot + 2, LANES + index : LANES + index + 1]
+
+    kinds = (
+        (w_side, row_side, col_side, g_side, n_side, s_row_side, s_col_side),
+        (w_proj, row_proj, col_proj, g_proj, n_proj, s_row_proj, s_col_proj),
+    )
+    for layer in range(layers):
+        for kind, (weight, row, col, g, n, s_row, s_col) in enumerate(kinds):
+            start = base[layer] + kind * block
+            index = kind * layers + layer
+            grad = red[start : start + block]
+            _, new_row = row_statistic(grad, column_of(row[layer : layer + 1]), width)
+            new_col = blend(col[layer : layer + 1], stat[index : index + 1, :width] / (2 * width))
+            over = jnp.sum(stat[slot + 2 + index : slot + 3 + index, :width] / new_col, 1, keepdims=True)
+            g[layer] = grad
+            n[layer] = step_of(weight[layer], grad, new_row, new_col, total_of(index) / (2 * width), over, 2 * width * width)
+            s_row[layer : layer + 1] = row_of(new_row)
+            s_col[layer : layer + 1] = new_col
+    first, second = red[head : head + block // 2], red[head + block // 2 : head + block]
+    grad = jnp.concatenate([first, second[:, : wide_in - width]], 1)[:, :in_width]
+    new_col = blend(column_of(col_in[...]), jnp.sum(grad * grad, 1, keepdims=True) / in_width)
+    new_row = blend(row_in[...], stat[slot : slot + 1, :in_width] / width)
+    mean = jnp.sum(new_row, 1, keepdims=True) / in_width
+    over = jnp.sum(stat[2 * slot + 2 : 2 * slot + 3, :in_width] / new_row, 1, keepdims=True)
+    g_in[...] = grad
+    n_in[...] = step_of(w_in_t[:, :in_width], grad, new_col, new_row, mean, over, in_width * width)
+    s_row_in[...] = new_row
+    s_col_in[...] = row_of(new_col)
+    grad = second[:, wide_in - width : wide_in - width + classes]
+    _, new_row = row_statistic(grad, column_of(row_out[...]), classes)
+    new_col = blend(col_out[...], stat[slot + 1 : slot + 2, :classes] / width)
+    over = jnp.sum(stat[2 * slot + 3 : 2 * slot + 4, :classes] / new_col, 1, keepdims=True)
+    g_out[...] = grad
+    n_out[...] = step_of(w_out[...], grad, new_row, new_col, total_of(slot) / width, over, width * classes)
+    s_row_out[...] = row_of(new_row)
+    s_col_out[...] = new_col
+    loss[...] = second[0:1, tail : tail + 1]
+    count[...] = stat[2 * slot + 4 : 2 * slot + 5, 0:1]
+
+
+def train_on_device(dims, name_id, in_width, classes, adjacency, feats, info, w_in_t, w_side, w_proj, w_out, col_in, row_side, row_proj, row_out):
     far, near, across, cores = dims
     nodes, wide_in = feats.shape
-    width = owns[0].shape[1]
-    block = owns[1].shape[0] // 2
+    layers, block, width = w_side.shape
     in_chunks, chunks = wide_in // LANES, width // LANES
-    layers = len(owns)
     dma = pltpu.SemaphoreType.DMA
     pool = max(blocks_of(forward_blocks(dims, in_chunks)), blocks_of(backward_blocks(dims, chunks)))
     bufs, sems = reduce_scratch(dims, 3, block, width)
     strip = 128
+    stat_rows = 24
+    partners = 1 + (across - 1) + (near - 1) + (far - 1)
     vmem = pl.BlockSpec(memory_space=pltpu.VMEM)
     refs = {
         "adj": pltpu.VMEM(adjacency.shape, bf16),
@@ -1077,25 +1292,62 @@
         "ready": pltpu.SemaphoreType.REGULAR((3 * layers - 3,)),
         "forward": forward_sems(dims, in_chunks),
         "backward": backward_sems(dims, chunks),
+        "sums": pltpu.VMEM((4 * stat_rows, wide_in), f32),
+        "sum_in": pltpu.VMEM((partners, stat_rows, wide_in), f32),
+        "sum_out": dma((partners,)),
+        "sum_came": dma((partners,)),
+        "marks": pltpu.VMEM((8, LANES), f32),
         "reduce_bufs": bufs,
         "reduce_sems": sems,
     }
     for layer in range(layers):
-        refs["every%d" % layer] = pltpu.VMEM(dims + owns[layer].shape, f32)
+        refs["every%d" % layer] = pltpu.VMEM(dims + ((3 if layer == 0 else 2) * block, width), f32)
         refs["spread%d" % layer] = spread_sems(dims)
     return pl.pallas_call(
         functools.partial(train_kernel, dims, in_width, classes),
         out_shape=(
             jax.ShapeDtypeStruct((7 * block, width), f32),
-            jax.ShapeDtypeStruct((8, LANES), f32),
+            jax.ShapeDtypeStruct((stat_rows, wide_in), f32),
         ),
-        in_specs=[pl.BlockSpec(memory_space=pl.ANY)] + [vmem] * (3 + layers),
+        in_specs=[pl.BlockSpec(memory_space=pl.ANY)] + [vmem] * 10,
         out_specs=(vmem, vmem),
         scratch_shapes=[refs],
         compiler_params=pltpu.CompilerParams(
             collective_id=name_id, has_side_effects=True, vmem_limit_bytes=63 * 2**20
         ),
-    )(adjacency, feats, info, target, *owns)
+    )(adjacency, feats, info, w_in_t, w_side, w_proj, w_out, col_in, row_side, row_proj, row_out)
+
+
+def update_on_device(in_width, classes, *arrays):
+    w_side, w_out = arrays[3], arrays[5]
+    layers, block, width = w_side.shape
+    shapes = [
+        (1, 1),
+        (1, 1),
+        (block // 2, in_width),
+        w_side.shape,
+        w_side.shape,
+        w_out.shape,
+        (block // 2, in_width),
+        w_side.shape,
+        w_side.shape,
+        w_out.shape,
+        (1, in_width),
+        (1, block // 2),
+        (layers, block),
+        (layers, width),
+        (layers, block),
+        (layers, width),
+        (1, block // 2),
+        (1, classes),
+    ]
+    vmem = pl.BlockSpec(memory_space=pltpu.VMEM)
+    return pl.pallas_call(
+        functools.partial(update_kernel, in_width, classes),
+        out_shape=[jax.ShapeDtypeStruct(shape, f32) for shape in shapes],
+        in_specs=[vmem] * len(arrays),
+        out_specs=[vmem] * len(shapes),
+    )(*arrays)
 
 
 def dot(left, right, over=((1,), (0,))):
@@ -1120,38 +1372,7 @@
     return 2 * adjacency.shape[0] * adjacency.shape[1] <= 4 * 2**20
 
 
-def gradients_fused(dims, features, adjacency, labels, labelled, node_count, w_in, w_side, w_proj, w_out):
-    layers, block, width = w_side.shape
-    nodes, in_width = features.shape
-    classes = w_out.shape[1]
-    wide_in = -(-(in_width + 1) // LANES) * LANES
-    counts = node_count.astype(f32)
-    alpha = 2.0 / (1.0 + counts)
-    weight_mask = labelled.astype(f32)
-    feats = pad_lanes(features, wide_in)
-    info = pad_lanes(jnp.stack([alpha, weight_mask * lax.rsqrt(counts)], 1), LANES)
-    target = pad_lanes(labels.astype(f32), LANES)
-    w_in_t = pad_lanes(w_in.T, wide_in)
-    tail = width - (wide_in - width) - LANES
-    count = jnp.broadcast_to(jnp.sum(weight_mask), (block // 2, tail))
-    head = jnp.concatenate(
-        [w_in_t[:, :width], jnp.concatenate([w_in_t[:, width:], pad_lanes(w_out, LANES), count], 1)], 0
-    )
-    owns = [
-        jnp.concatenate([w_side[l], w_proj[l]] + ([head] if l == 0 else []), 0) for l in range(layers)
-    ]
-    red, notes = train_on_device(dims, 1, in_width, classes, adjacency, feats, info, target, owns)
-    start = [0, 3 * block, 5 * block]
-    red_side = jnp.stack([red[at : at + block] for at in start])
-    red_proj = jnp.stack([red[at + block : at + 2 * block] for at in start])
-    first, second = red[2 * block : 2 * block + block // 2], red[2 * block + block // 2 : 3 * block]
-    red_in = jnp.concatenate([first, second[:, : in_width - width]], 1).T
-    at_lane = wide_in - width
-    red_out = second[:, at_lane : at_lane + classes]
-    return second[0, at_lane + LANES], notes[0, 0], red_in, red_side, red_proj, red_out
-
-
-def gradients_apart(
+def step_fused(
     dims,
     features,
     adjacency,
@@ -1162,10 +1383,85 @@
     w_side,
     w_proj,
     w_out,
+    row_in,
+    col_in,
+    row_side,
+    col_side,
+    row_proj,
+    col_proj,
+    row_out,
+    col_out,
+):
+    nodes, in_width = features.shape
+    classes = w_out.shape[1]
+    wide_in = -(-(in_width + 1) // LANES) * LANES
+    counts = node_count.astype(f32)
+    mask = labelled.astype(f32)
+    lane = lax.broadcasted_iota(jnp.int32, (nodes, LANES), 1)
+    facts = jnp.where(
+        lane == 0,
+        (2.0 / (1.0 + counts))[:, None],
+        jnp.where(lane == 1, (mask * lax.rsqrt(counts))[:, None], jnp.where(lane == 2, mask[:, None], 0.0)),
+    )
+    info = jnp.concatenate([pad_lanes(labels.astype(f32), LANES), facts], 1)
+    w_in_t = pad_lanes(w_in.T, wide_in)
+    local = (w_in_t, w_side, w_proj, w_out)
+    red, stat = train_on_device(
+        dims, 1, in_width, classes, adjacency, pad_lanes(features, wide_in), info, *local,
+        col_in[None], row_side, row_proj, row_out[None],
+    )
+    done = update_on_device(
+        in_width, classes, red, stat, *local,
+        row_in[None], col_in[None], row_side, col_side, row_proj, col_proj, row_out[None], col_out[None],
+    )
+    (loss, count, g_in, g_side, g_proj, g_out, n_in, n_side, n_proj, n_out,
+     s_row_in, s_col_in, s_row_side, s_col_side, s_row_proj, s_col_proj, s_row_out, s_col_out) = done
+    return (
+        loss[0, 0],
+        count[0, 0],
+        g_in.T,
+        g_side,
+        g_proj,
+        g_out,
+        n_in.T,
+        n_side,
+        n_proj,
+        n_out,
+        s_row_in[0],
+        s_col_in[0],
+        s_row_side,
+        s_col_side,
+        s_row_proj,
+        s_col_proj,
+        s_row_out[0],
+        s_col_out[0],
+    )
+
+
+def step_apart(
+    dims,
+    features,
+    adjacency,
+    labels,
+    labelled,
+    node_count,
+    w_in,
+    w_side,
+    w_proj,
+    w_out,
+    row_in,
+    col_in,
+    row_side,
+    col_side,
+    row_proj,
+    col_proj,
+    row_out,
+    col_out,
 ):
     layers = w_side.shape[0]
     width = w_side.shape[2]
     in_width = features.shape[1]
+    classes = w_out.shape[1]
     nodes = features.shape[0]
     both = ("wide", "narrow")
     adj = adjacency.astype(bf16)
@@ -1241,37 +1537,6 @@
         lax.psum_scatter(jnp.stack(side_grads), both, scatter_dimension=1, tiled=True),
         lax.psum_scatter(jnp.stack(proj_grads), both, scatter_dimension=1, tiled=True),
         lax.psum_scatter(g_out, both, scatter_dimension=0, tiled=True),
-    )
-    return loss_sum, label_count, red_in, red_side, red_proj, red_out
-
-
-def step_on_device(
-    dims,
-    features,
-    adjacency,
-    labels,
-    labelled,
-    node_count,
-    w_in,
-    w_side,
-    w_proj,
-    w_out,
-    row_in,
-    col_in,
-    row_side,
-    col_side,
-    row_proj,
-    col_proj,
-    row_out,
-    col_out,
-):
-    width = w_side.shape[2]
-    in_width = features.shape[1]
-    classes = w_out.shape[1]
-    both = ("wide", "narrow")
-    gradients = gradients_fused if fits_on_chip(adjacency) else gradients_apart
-    loss_sum, label_count, red_in, red_side, red_proj, red_out = gradients(
-        dims, features, adjacency, labels, labelled, node_count, w_in, w_side, w_proj, w_out
     )
     sq_in = red_in * red_in
     sq_side = red_side * red_side
@@ -1359,6 +1624,11 @@
     )
 
 
+def step_on_device(dims, features, adjacency, *others):
+    step = step_fused if fits_on_chip(adjacency) else step_apart
+    return step(dims, features, adjacency, *others)
+
+
 def solution(mesh):
     in_specs = (
         P(("wide", "narrow"), None),

time: 567 us -> 497 us (0.88)
  blocking collectives: 40.1 us -> 0 us
  Pallas kernels: 492 us -> 479 us
  local copies, waits for them, and re-layouts: 12.6 us -> 4.18 us
  other arithmetic: 11.7 us -> 4.48 us
    psum x1 -> x0, blocking collectives: 40.1 us -> none  [step_on_device(): lax.psum((jnp.sum(sq_in, 1), jnp.sum(sq_side, 1), jnp.sum(sq_proj, 1), jn...]
    pallas_call x1, Pallas kernels: 492 us -> 476 us  [train_on_device(): pl.pallas_call(functools.partial(train_kernel, dims, in_width, classes),...]
where the time goes in v3:
time: 497 us; the launch traced here: 488 us
  Pallas kernels  479 us (96%)
    pallas_call x1, Pallas kernels, train_on_device(): pl.pallas_call(functools.partial(train_kernel, dims, in_width, classes),...  476 us

profile of v3, /device:TPU:0, one launch (start us, length us, event | category | flops | bytes accessed | tf_op | source)
XLA Modules:
  0.0 488.4 jit_solution(7011059512153121042)
XLA Ops:
  0.7 0.0 copy-start
  0.7 1.3 copy.35
  2.0 0.9 pad.12.feats
  2.9 0.9 convert_element_type.15
  3.8 0.7 convert_element_type.17
  4.5 0.7 add_divide_fusion
  5.2 0.2 select_select_fusion
  5.4 0.7 select_maximum_fusion.info
  6.1 1.4 pad.14.w_in_t
  7.5 476.1 %shard_map.304 = (f32[224,512]{1,0:T(8,128)}, f32[24,640]{1,0:T(8,128)}) custom-call(s32[1024,2048]{1,0:T(8,128)} %adj_hbm.1, f32[256,640]{1,0:T(8,128)} %pad.12.feats, f32[256,256]{1,0:T(8,128)} %select_maximum_fusion.info, f32[16,640]{1,0:T(8,128)} %pad.14.w_in_t, f32[3,32,512]{2,1,0:T(8,128)} %w_side.3, f32[3,32,512]{2,1,0:T(8,128)} %w_proj.3, ...), custom_call_target="tpu_custom_call" | custom-call | tf_op jit(solution)/shard_map/pallas_call | solution.py:1306
  483.6 0.0 copy-done
  483.7 0.6 broadcast_in_dim.48.row_in
  484.2 2.5 shard_map.305
  486.7 1.3 reduce
  (2 shorter events, 0.0 us)
Async XLA Ops:
  0.7 483.0 %copy-start = (f32[602]{0:T(1024)S(1)}, f32[602]{0:T(1024)}, u32[]{:S(2)}) copy-start(f32[602]{0:T(1024)} %param.26) | copy-start | bytes 7228

commit v4 on v3

--- a/solution.py
+++ b/solution.py
@@ -460,29 +460,39 @@
             total = total + from_across.ref(k, xx)[...]
         out[:, k * LANES : (k + 1) * LANES] = total
 
-    for step in range(1, far):
+    def complete(k):
+        take_in(k, last)
+        send(part.run(k, 1 - c), from_core.run(k), core_sems.at[0, k], core_sems.at[1, k], device(dims, p, q, x, 1 - c))
+
+    last = far - 1
+    for step in range(1, last):
         hooks.run("step%d" % step)
         for k in range(chunks):
             from_line(step, k)
-            if step == far - 1 and step >= 2:
-                take_in(k, step - 1)
-        if step == 1 or step < far - 1:
-            every_chunk(step - 1)
+        every_chunk(step - 1)
+    hooks.run("step%d" % last)
+    for k in range(chunks):
+        from_line(last, k)
+        take_in(k, last - 1)
+        if k >= 1:
+            complete(k - 1)
+        if k >= 2:
+            reduce_across(k - 2)
+        if k >= 3:
+            finish(k - 3)
     hooks.run("drain")
-    order = list(range(chunks))
-    for i, k in enumerate(order):
-        take_in(k, far - 1)
-        send(part.run(k, 1 - c), from_core.run(k), core_sems.at[0, k], core_sems.at[1, k], device(dims, p, q, x, 1 - c))
-        if i >= 1:
-            reduce_across(order[i - 1])
-        if i >= 2:
-            finish(order[i - 2])
+    complete(chunks - 1)
+    if chunks >= 2:
+        reduce_across(chunks - 2)
+    if chunks >= 3:
+        finish(chunks - 3)
     hooks.run("product")
-    reduce_across(order[-1])
+    reduce_across(chunks - 1)
+    if chunks >= 2:
+        finish(chunks - 2)
     hooks.run("shadow")
-    if chunks >= 2:
-        finish(order[-2])
-    finish(order[-1])
+    finish(chunks - 1)
+    hooks.run("last")
 
     for k in range(chunks):
         left_source(part.run(k, 1 - c), core_sems.at[0, k])
@@ -679,17 +689,40 @@
     return [dma((chunks, 2 * across)), dma((chunks, across, cores))] + [dma((chunks, far, near))] * 6
 
 
+class Part:
+    def __init__(self, index, piece, offset, depth, own_row, out_row, turned):
+        self.index, self.piece, self.offset, self.depth = index, piece, offset, depth
+        self.own_row, self.out_row, self.turned = own_row, out_row, turned
+
+
 class ReduceAll:
-    def __init__(self, dims, at, own, first_rows, out, bufs, sems):
-        self.dims, self.at, self.own, self.first_rows, self.out = dims, at, own, first_rows, out
-        self.halfway, self.from_first, self.from_next, self.from_left, self.from_right = bufs
+    def __init__(self, dims, at, own, out, bufs, sems):
+        self.dims, self.at, self.own, self.out = dims, at, own, out
+        self.halfway, self.first_buf, self.next_buf, self.left_buf, self.right_buf = bufs
         self.core_sems, self.first_out, self.first_in, self.next_out, self.next_in = sems[:5]
         self.right_out, self.left_out, self.left_in, self.right_in = sems[5:]
-        self.depth = self.halfway.shape[4]
-        self.turned = [False] * len(first_rows)
-
-    def rows(self, j):
-        return pl.ds(self.first_rows[j], self.depth)
+
+    def own_rows(self, part):
+        return pl.ds(part.own_row, part.depth)
+
+    def half(self, part, *where):
+        lead = (part.piece,) + where + (slice(None),) * (3 - len(where))
+        return self.halfway.at[lead + (pl.ds(part.offset, part.depth),)]
+
+    def from_first(self, part, i):
+        return self.first_buf.at[part.piece, i, :, :, pl.ds(part.offset, part.depth)]
+
+    def from_next(self, part, i):
+        return self.next_buf.at[part.piece, i, :, pl.ds(part.offset, part.depth)]
+
+    def from_left(self, part, pp):
+        return self.left_buf.at[part.piece, pp, pl.ds(part.offset, part.depth)]
+
+    def from_right(self, part, pp):
+        return self.right_buf.at[part.piece, pp, pl.ds(part.offset, part.depth)]
+
+    def add(self, ref, other):
+        ref[...] = ref[...] + other[...]
 
     def peers(self, turned):
         far, near, across, cores = self.dims
@@ -698,36 +731,34 @@
             return [(lax.rem(q + step, near), device(self.dims, p, lax.rem(q + step, near), x, c)) for step in range(1, near)]
         return [(lax.rem(x + step, across), device(self.dims, p, q, lax.rem(x + step, across), c)) for step in range(1, across)]
 
-    def core_stage(self, j):
+    def core_stage(self, part):
         p, q, x, c = self.at
-        send(self.own.at[:, :, :, 1 - c, self.rows(j)], self.halfway.at[j], self.core_sems.at[0, j], self.core_sems.at[1, j], device(self.dims, p, q, x, 1 - c))
-
-    def across_stage(self, j):
+        send(self.own.at[:, :, :, 1 - c, self.own_rows(part)], self.half(part), self.core_sems.at[0, part.index], self.core_sems.at[1, part.index], device(self.dims, p, q, x, 1 - c))
+
+    def across_stage(self, part):
         p, q, x, c = self.at
-        arrived(self.halfway.at[j], self.core_sems.at[1, j])
-        self.halfway[j] = self.halfway[j] + self.own[:, :, :, c, self.rows(j)]
-        for i, (other, target) in enumerate(self.peers(self.turned[j])):
-            src = self.halfway.at[j, :, other] if self.turned[j] else self.halfway.at[j, :, :, other]
-            send(src, self.from_first.at[j, i], self.first_out.at[j, i], self.first_in.at[j, i], target)
-
-    def near_stage(self, j):
+        arrived(self.half(part), self.core_sems.at[1, part.index])
+        self.add(self.half(part), self.own.at[:, :, :, c, self.own_rows(part)])
+        for i, (other, target) in enumerate(self.peers(part.turned)):
+            src = self.half(part, slice(None), other) if part.turned else self.half(part, slice(None), slice(None), other)
+            send(src, self.from_first(part, i), self.first_out.at[part.index, i], self.first_in.at[part.index, i], target)
+
+    def near_stage(self, part):
         p, q, x, c = self.at
-        for i, _ in enumerate(self.peers(self.turned[j])):
-            arrived(self.from_first.at[j, i], self.first_in.at[j, i])
-            if self.turned[j]:
-                self.halfway[j, :, q] = self.halfway[j, :, q] + self.from_first[j, i]
-            else:
-                self.halfway[j, :, :, x] = self.halfway[j, :, :, x] + self.from_first[j, i]
-        for i, (other, target) in enumerate(self.peers(not self.turned[j])):
-            src = self.halfway.at[j, :, q, other] if self.turned[j] else self.halfway.at[j, :, other, x]
-            send(src, self.from_next.at[j, i], self.next_out.at[j, i], self.next_in.at[j, i], target)
-
-    def line_stage(self, j):
+        mine = self.half(part, slice(None), q) if part.turned else self.half(part, slice(None), slice(None), x)
+        for i, _ in enumerate(self.peers(part.turned)):
+            arrived(self.from_first(part, i), self.first_in.at[part.index, i])
+            self.add(mine, self.from_first(part, i))
+        for i, (other, target) in enumerate(self.peers(not part.turned)):
+            src = self.half(part, slice(None), q, other) if part.turned else self.half(part, slice(None), other, x)
+            send(src, self.from_next(part, i), self.next_out.at[part.index, i], self.next_in.at[part.index, i], target)
+
+    def line_stage(self, part):
         far, near, across, cores = self.dims
         p, q, x, c = self.at
-        for i, _ in enumerate(self.peers(not self.turned[j])):
-            arrived(self.from_next.at[j, i], self.next_in.at[j, i])
-            self.halfway[j, :, q, x] = self.halfway[j, :, q, x] + self.from_next[j, i]
+        for i, _ in enumerate(self.peers(not part.turned)):
+            arrived(self.from_next(part, i), self.next_in.at[part.index, i])
+            self.add(self.half(part, slice(None), q, x), self.from_next(part, i))
         for distance in range(far - 1, 0, -1):
             pp = p + distance
 
@@ -735,10 +766,10 @@
             def _(pp=pp):
                 @pl.when(p > 0)
                 def _():
-                    arrived(self.from_left.at[j, pp], self.left_in.at[j, pp])
-                    self.halfway[j, pp, q, x] = self.halfway[j, pp, q, x] + self.from_left[j, pp]
-
-                send(self.halfway.at[j, pp, q, x], self.from_left.at[j, pp], self.right_out.at[j, pp], self.left_in.at[j, pp], device(self.dims, p + 1, q, x, c))
+                    arrived(self.from_left(part, pp), self.left_in.at[part.index, pp])
+                    self.add(self.half(part, pp, q, x), self.from_left(part, pp))
+
+                send(self.half(part, pp, q, x), self.from_left(part, pp), self.right_out.at[part.index, pp], self.left_in.at[part.index, pp], device(self.dims, p + 1, q, x, c))
 
             pm = p - distance
 
@@ -746,46 +777,46 @@
             def _(pm=pm):
                 @pl.when(p < far - 1)
                 def _():
-                    arrived(self.from_right.at[j, pm], self.right_in.at[j, pm])
-                    self.halfway[j, pm, q, x] = self.halfway[j, pm, q, x] + self.from_right[j, pm]
-
-                send(self.halfway.at[j, pm, q, x], self.from_right.at[j, pm], self.left_out.at[j, pm], self.right_in.at[j, pm], device(self.dims, p - 1, q, x, c))
-
-    def last_stage(self, j, out_row):
+                    arrived(self.from_right(part, pm), self.right_in.at[part.index, pm])
+                    self.add(self.half(part, pm, q, x), self.from_right(part, pm))
+
+                send(self.half(part, pm, q, x), self.from_right(part, pm), self.left_out.at[part.index, pm], self.right_in.at[part.index, pm], device(self.dims, p - 1, q, x, c))
+
+    def last_stage(self, part):
         far, near, across, cores = self.dims
         p, q, x, c = self.at
-        into = self.out.at[pl.ds(out_row, self.depth)]
-        into[...] = self.halfway[j, p, q, x]
+        into = self.out.at[pl.ds(part.out_row, part.depth)]
+        into[...] = self.half(part, p, q, x)[...]
 
         @pl.when(p > 0)
         def _():
-            arrived(self.from_left.at[j, p], self.left_in.at[j, p])
-            into[...] = into[...] + self.from_left[j, p]
+            arrived(self.from_left(part, p), self.left_in.at[part.index, p])
+            self.add(into, self.from_left(part, p))
 
         @pl.when(p < far - 1)
         def _():
-            arrived(self.from_right.at[j, p], self.right_in.at[j, p])
-            into[...] = into[...] + self.from_right[j, p]
-
-    def end(self, j):
+            arrived(self.from_right(part, p), self.right_in.at[part.index, p])
+            self.add(into, self.from_right(part, p))
+
+    def end(self, part):
         far, near, across, cores = self.dims
         p, q, x, c = self.at
-        left_source(self.own.at[:, :, :, 1 - c, self.rows(j)], self.core_sems.at[0, j])
-        for i, _ in enumerate(self.peers(self.turned[j])):
-            left_source(self.from_first.at[j, i], self.first_out.at[j, i])
-        for i, _ in enumerate(self.peers(not self.turned[j])):
-            left_source(self.from_next.at[j, i], self.next_out.at[j, i])
+        left_source(self.half(part), self.core_sems.at[0, part.index])
+        for i, _ in enumerate(self.peers(part.turned)):
+            left_source(self.from_first(part, i), self.first_out.at[part.index, i])
+        for i, _ in enumerate(self.peers(not part.turned)):
+            left_source(self.from_next(part, i), self.next_out.at[part.index, i])
         for pp in range(far):
             @pl.when(pp > p)
             def _(pp=pp):
-                left_source(self.from_left.at[j, pp], self.right_out.at[j, pp])
+                left_source(self.from_left(part, pp), self.right_out.at[part.index, pp])
 
             @pl.when(pp < p)
             def _(pp=pp):
-                left_source(self.from_right.at[j, pp], self.left_out.at[j, pp])
-
-
-def reduce_scratch(dims, pieces, depth, width):
+                left_source(self.from_right(part, pp), self.left_out.at[part.index, pp])
+
+
+def reduce_scratch(dims, pieces, parts, depth, width):
     far, near, across, cores = dims
     dma = pltpu.SemaphoreType.DMA
     bufs = [
@@ -796,12 +827,12 @@
         pltpu.VMEM((pieces, far, depth, width), f32),
     ]
     sems = [
-        dma((2, pieces)),
-        dma((pieces, max(across - 1, 1))),
-        dma((pieces, max(across - 1, 1))),
-        dma((pieces, max(near - 1, 1))),
-        dma((pieces, max(near - 1, 1))),
-    ] + [dma((pieces, far))] * 4
+        dma((2, parts)),
+        dma((parts, max(across - 1, 1))),
+        dma((parts, max(across - 1, 1))),
+        dma((parts, max(near - 1, 1))),
+        dma((parts, max(near - 1, 1))),
+    ] + [dma((parts, far))] * 4
     return bufs, sems
 
 
@@ -963,11 +994,6 @@
         first, second = both(head), both(head + block // 2)
         return jnp.concatenate([first, second[:, : wide_in - width]], 1)
 
-    def onward(layer):
-        spreads[layer].drain()
-        if layer + 1 < layers:
-            spreads[layer + 1].begin()
-
     def ahead(layer):
         spreads[layer].end()
         mixing(layer)
@@ -977,12 +1003,23 @@
 
     rounds = iter(range(ready.shape[0]))
     for layer in range(layers):
-        acts = {"drain": [functools.partial(onward, layer)], "shadow": [functools.partial(ahead, layer)]}
-        for step in range(1, far):
-            acts["step%d" % step] = [functools.partial(spreads[layer].step, step)]
+        acts = {}
         if layer == 0:
+            for step in range(1, far):
+                acts["step%d" % step] = [functools.partial(spreads[0].step, step)]
             acts["begin"] = [spreads[0].begin]
             acts["sent"] = [load_adjacency]
+            acts["drain"] = [spreads[0].drain]
+            acts["shadow"] = [functools.partial(ahead, 0)]
+        else:
+            acts["sent"] = [functools.partial(spreads[layer].step, step) for step in range(3, far)]
+            acts["step%d" % (far - 1)] = [spreads[layer].drain, functools.partial(ahead, layer)]
+        if layer + 1 < layers:
+            after = spreads[layer + 1]
+            acts["drain"] = acts.get("drain", []) + [after.begin]
+            acts["product"] = [functools.partial(after.step, 1)]
+            acts["last"] = [functools.partial(after.step, 2)]
+        if layer == 0:
             forward_pass(dims, at, in_chunks, adj, sent, raw, pair, pool, refs["forward"], Hooks(**acts))
             turn = ready.at[next(rounds)]
             announce(dims, at, turn)
@@ -1033,9 +1070,7 @@
         )
         put_rows(every[0], half, start, block // 2, piece)
 
-    reduces = [
-        ReduceAll(dims, at, every[l], [0, block, head], red, refs["reduce_bufs"], refs["reduce_sems"]) for l in range(layers)
-    ]
+    reduces = [ReduceAll(dims, at, every[l], red, refs["reduce_bufs"], refs["reduce_sems"]) for l in range(layers)]
 
     def slope(layer, d_out):
         pre_act = pre[layer]
@@ -1116,11 +1151,11 @@
             left_source(came_in.at[at_slot], out_sems.at[at_slot])
 
 
-    def finish_reduce(layer, pieces):
-        for j in pieces:
-            reduces[layer].last_stage(j, base[layer] + j * block)
-        for j in pieces:
-            reduces[layer].end(j)
+    def finish_reduce(layer, parts):
+        for part in parts:
+            reduces[layer].last_stage(part)
+        for part in parts:
+            reduces[layer].end(part)
         note_layer(layer)
 
     d_pre_ref = refs["d_pre"]
@@ -1128,28 +1163,32 @@
     for layer in range(layers - 1, 0, -1):
         d_pre_ref[...] = slope(layer, d_out)
         sent[:, :width] = d_pre_ref[...] * inverse[:, 0:1]
-
-        def grads(layer=layer):
+        first = 2 * ((layers - 1 - layer) % 2)
+        parts = [
+            Part(first + kind, first + kind, 0, block, kind * block, base[layer] + kind * block, False) for kind in range(2)
+        ]
+
+        def begin_grads(layer=layer):
             outers(layer, d_pre_ref[...])
-            for half in range(2):
-                weight_grads(layer, half)
-            if freed:
-                await_all(dims, at, freed.pop())
-            for j in range(2):
-                reduces[layer].core_stage(j)
+            weight_grads(layer, 0)
+
+        def more_grads(layer=layer, parts=parts):
+            weight_grads(layer, 1)
+            for part in parts:
+                reduces[layer].core_stage(part)
 
         def direct_part(layer=layer):
             direct[...] = right_flip(d_pre_ref[...], mix[layer % 2, 0])
 
-        def stage(name, layer=layer):
-            for j in range(2):
-                getattr(reduces[layer], name)(j)
+        def stage(name, layer=layer, parts=parts):
+            for part in parts:
+                getattr(reduces[layer], name)(part)
 
         acts = {
-            "chunk0": carried[:1],
-            "chunk1": carried[1:] + [direct_part],
-            "chunk2": [grads],
-            "chunk3": [functools.partial(stage, "across_stage")],
+            "sent": carried[:1] + [begin_grads],
+            "chunk0": carried[1:],
+            "chunk1": [more_grads],
+            "chunk2": [direct_part, functools.partial(stage, "across_stage")],
             "early": [functools.partial(mixing, 0)] if layer == 1 else [],
             "line": [functools.partial(stage, "near_stage")],
         }
@@ -1161,10 +1200,11 @@
         if layer > 1:
             await_all(dims, at, turn)
 
-        def close(layer=layer):
-            finish_reduce(layer, range(2))
-            freed.append(ready.at[next(rounds)])
-            announce(dims, at, freed[0])
+        def close(layer=layer, parts=parts):
+            finish_reduce(layer, parts)
+            if layer == layers - 1 or layer == 1:
+                freed.append(ready.at[next(rounds)])
+                announce(dims, at, freed[-1])
 
         carried = [functools.partial(stage, "line_stage"), close]
 
@@ -1183,25 +1223,35 @@
             (far // 2, near, across, cores, block // 2, wide_in - width)
         )
     carried[1]()
-    await_all(dims, at, freed.pop())
+    for turn in freed:
+        await_all(dims, at, turn)
     final = reduces[0]
-    final.turned = [near == across, False, False]
-    final.core_stage(2)
+    depth = block // 2
+    order = [
+        Part(2 * piece + turned, piece, turned * depth, depth, piece * block + turned * depth, piece * block + turned * depth, turned == 1 and near == across)
+        for piece in (2, 0, 1)
+        for turned in range(2)
+    ]
+    for part in order[:2]:
+        final.core_stage(part)
     outers(0, d_pre)
+    for part in order[:2]:
+        final.across_stage(part)
     weight_grads(0, 0)
+    for part in order[:2]:
+        final.near_stage(part)
     weight_grads(0, 1)
-    final.core_stage(0)
-    final.core_stage(1)
-    final.across_stage(2)
-    final.across_stage(0)
-    final.across_stage(1)
-    final.near_stage(2)
-    final.near_stage(0)
-    final.near_stage(1)
-    final.line_stage(2)
-    final.line_stage(0)
-    final.line_stage(1)
-    finish_reduce(0, (2, 0, 1))
+    for part in order[2:]:
+        final.core_stage(part)
+    for part in order[:2]:
+        final.line_stage(part)
+    for part in order[2:]:
+        final.across_stage(part)
+    for part in order[2:]:
+        final.near_stage(part)
+    for part in order[2:]:
+        final.line_stage(part)
+    finish_reduce(0, order)
     note_head()
     sum_everywhere(stat)
 
@@ -1267,7 +1317,7 @@
     in_chunks, chunks = wide_in // LANES, width // LANES
     dma = pltpu.SemaphoreType.DMA
     pool = max(blocks_of(forward_blocks(dims, in_chunks)), blocks_of(backward_blocks(dims, chunks)))
-    bufs, sems = reduce_scratch(dims, 3, block, width)
+    bufs, sems = reduce_scratch(dims, 4, 6, block, width)
     strip = 128
     stat_rows = 24
     partners = 1 + (across - 1) + (near - 1) + (far - 1)
@@ -1625,7 +1675,7 @@
 
 
 def step_on_device(dims, features, adjacency, *others):
-    step = step_fused if fits_on_chip(adjacency) else step_apart
+    step = step_fused if dims[0] == 4 and fits_on_chip(adjacency) else step_apart
     return step(dims, features, adjacency, *others)
 
 

time: 497 us -> 487 us (0.980)
  Pallas kernels: 479 us -> 470 us
    pallas_call x1, Pallas kernels: 476 us -> 468 us  [train_on_device(): pl.pallas_call(functools.partial(train_kernel, dims, in_width, classes),...]
where the time goes in v4:
time: 487 us; the launch traced here: 480 us
  Pallas kernels  470 us (97%)
    pallas_call x1, Pallas kernels, train_on_device(): pl.pallas_call(functools.partial(train_kernel, dims, in_width, classes),...  468 us

profile of v4, /device:TPU:0, one launch (start us, length us, event | category | flops | bytes accessed | tf_op | source)
XLA Modules:
  0.0 480.1 jit_solution(17892748833152877727)
XLA Ops:
  0.7 0.0 copy-start
  0.7 1.3 copy.35
  2.0 0.9 pad.12.feats
  2.9 0.9 convert_element_type.15
  3.8 0.7 convert_element_type.17
  4.5 0.7 add_divide_fusion
  5.2 0.2 select_select_fusion
  5.4 0.7 select_maximum_fusion.info
  6.1 1.4 pad.14.w_in_t
  7.5 467.8 %shard_map.304 = (f32[224,512]{1,0:T(8,128)}, f32[24,640]{1,0:T(8,128)}) custom-call(s32[1024,2048]{1,0:T(8,128)} %adj_hbm.1, f32[256,640]{1,0:T(8,128)} %pad.12.feats, f32[256,256]{1,0:T(8,128)} %select_maximum_fusion.info, f32[16,640]{1,0:T(8,128)} %pad.14.w_in_t, f32[3,32,512]{2,1,0:T(8,128)} %w_side.3, f32[3,32,512]{2,1,0:T(8,128)} %w_proj.3, ...), custom_call_target="tpu_custom_call" | custom-call | tf_op jit(solution)/shard_map/pallas_call | solution.py:1356
  475.3 0.0 copy-done
  475.3 0.6 broadcast_in_dim.48.row_in
  475.9 2.5 shard_map.305
  478.3 1.3 reduce
  (2 shorter events, 0.0 us)
Async XLA Ops:
  0.7 474.6 %copy-start = (f32[602]{0:T(1024)S(1)}, f32[602]{0:T(1024)}, u32[]{:S(2)}) copy-start(f32[602]{0:T(1024)} %param.26) | copy-start | bytes 7228

commit v5 on v4

--- a/solution.py
+++ b/solution.py
@@ -471,25 +471,31 @@
             from_line(step, k)
         every_chunk(step - 1)
     hooks.run("step%d" % last)
-    for k in range(chunks):
+    for k in range(early):
+        if k >= 2:
+            reduce_across(k - 2)
         from_line(last, k)
         take_in(k, last - 1)
         if k >= 1:
             complete(k - 1)
-        if k >= 2:
-            reduce_across(k - 2)
-        if k >= 3:
-            finish(k - 3)
+    if early >= 2:
+        reduce_across(early - 2)
+    take_in(early, last - 1)
     hooks.run("drain")
-    complete(chunks - 1)
-    if chunks >= 2:
-        reduce_across(chunks - 2)
-    if chunks >= 3:
-        finish(chunks - 3)
+    if early >= 1:
+        complete(early - 1)
+    for k in range(early - 2):
+        finish(k)
+    if early >= 1:
+        reduce_across(early - 1)
+    from_line(last, early)
+    complete(early)
+    if early >= 2:
+        finish(early - 2)
     hooks.run("product")
-    reduce_across(chunks - 1)
-    if chunks >= 2:
-        finish(chunks - 2)
+    reduce_across(early)
+    if early >= 1:
+        finish(early - 1)
     hooks.run("shadow")
     finish(chunks - 1)
     hooks.run("last")
@@ -541,6 +547,8 @@
     others = [lax.rem(q + step, near) for step in range(1, near)]
     crossing = [lax.rem(x + step, across) for step in range(1, across)]
 
+    at_end = jnp.logical_or(p == 0, p == far - 1)
+
     def on_line(k, pp, qq):
         return line_early.ref(pp, qq) if k == early else line_rest.ref(k, pp)
 
@@ -602,8 +610,10 @@
         def step(i, carry):
             pp = dest(i)
             if k == early:
-                for qq in others + [q]:
-                    along(k, pp, qq)
+                @pl.when(jnp.logical_not(at_end))
+                def _():
+                    for qq in others + [q]:
+                        along(k, pp, qq)
             else:
                 for qq in others:
                     arrived(from_near.ref(k, pp, qq), near_in.at[k, pp, qq])
@@ -634,7 +644,11 @@
             start = pl.multiple_of((pp * near + qq) * nodes, nodes)
             both = lax.dot_general(adj[:, pl.ds(start, nodes)], pair[:total_rows, :], (((0,), (0,)), ((), ())), preferred_element_type=f32)
             part.ref(k, pp, qq)[...] = both[:, :LANES] + both[:, LANES:]
-            if k != early:
+            if k == early:
+                @pl.when(at_end)
+                def _():
+                    pl.when(pp != p)(lambda: along(k, pp, qq))
+            else:
                 @pl.when(qq != q)
                 def _():
                     send(part.ref(k, pp, qq), from_near.ref(k, pp, q), near_out.at[k, pp, lax.rem(qq - q - 1 + near, near)], near_in.at[k, pp, q], device(dims, p, qq, x, c))
@@ -1004,21 +1018,15 @@
     rounds = iter(range(ready.shape[0]))
     for layer in range(layers):
         acts = {}
+        now = spreads[layer]
         if layer == 0:
-            for step in range(1, far):
-                acts["step%d" % step] = [functools.partial(spreads[0].step, step)]
-            acts["begin"] = [spreads[0].begin]
-            acts["sent"] = [load_adjacency]
-            acts["drain"] = [spreads[0].drain]
-            acts["shadow"] = [functools.partial(ahead, 0)]
+            acts = {"begin": [now.begin], "sent": [load_adjacency], "step1": [functools.partial(now.step, 1)], "step2": [functools.partial(now.step, 2)], "step3": [functools.partial(now.step, 3)], "drain": [now.drain], "shadow": [functools.partial(ahead, 0)]}
         else:
-            acts["sent"] = [functools.partial(spreads[layer].step, step) for step in range(3, far)]
-            acts["step%d" % (far - 1)] = [spreads[layer].drain, functools.partial(ahead, layer)]
+            acts = {"sent": [functools.partial(now.step, 2)], "step2": [functools.partial(now.step, 3)], "step3": [now.drain, functools.partial(ahead, layer)]}
         if layer + 1 < layers:
             after = spreads[layer + 1]
-            acts["drain"] = acts.get("drain", []) + [after.begin]
-            acts["product"] = [functools.partial(after.step, 1)]
-            acts["last"] = [functools.partial(after.step, 2)]
+            for name, act in [("drain", after.begin), ("last", functools.partial(after.step, 1))]:
+                acts[name] = acts.get(name, []) + [act]
         if layer == 0:
             forward_pass(dims, at, in_chunks, adj, sent, raw, pair, pool, refs["forward"], Hooks(**acts))
             turn = ready.at[next(rounds)]

time: 487 us -> 469 us (0.963)
  Pallas kernels: 470 us -> 453 us
    pallas_call x1, Pallas kernels: 468 us -> 450 us  [train_on_device(): pl.pallas_call(functools.partial(train_kernel, dims, in_width, classes),...]
where the time goes in v5:
time: 469 us; the launch traced here: 462 us
  Pallas kernels  453 us (97%)
    pallas_call x1, Pallas kernels, train_on_device(): pl.pallas_call(functools.partial(train_kernel, dims, in_width, classes),...  450 us

profile of v5, /device:TPU:0, one launch (start us, length us, event | category | flops | bytes accessed | tf_op | source)
XLA Modules:
  0.0 462.5 jit_solution(3555522577479997991)
XLA Ops:
  0.7 0.0 copy-start
  0.7 1.3 copy.35
  2.0 0.9 pad.12.feats
  2.9 0.9 convert_element_type.15
  3.8 0.7 convert_element_type.17
  4.5 0.7 add_divide_fusion
  5.2 0.2 select_select_fusion
  5.4 0.7 select_maximum_fusion.info
  6.1 1.4 pad.14.w_in_t
  7.5 450.2 %shard_map.304 = (f32[224,512]{1,0:T(8,128)}, f32[24,640]{1,0:T(8,128)}) custom-call(s32[1024,2048]{1,0:T(8,128)} %adj_hbm.1, f32[256,640]{1,0:T(8,128)} %pad.12.feats, f32[256,256]{1,0:T(8,128)} %select_maximum_fusion.info, f32[16,640]{1,0:T(8,128)} %pad.14.w_in_t, f32[3,32,512]{2,1,0:T(8,128)} %w_side.3, f32[3,32,512]{2,1,0:T(8,128)} %w_proj.3, ...), custom_call_target="tpu_custom_call" | custom-call | tf_op jit(solution)/shard_map/pallas_call | solution.py:1364
  457.7 0.0 copy-done
  457.7 0.6 broadcast_in_dim.48.row_in
  458.3 2.5 shard_map.305
  460.8 1.3 reduce
  (2 shorter events, 0.0 us)
Async XLA Ops:
  0.7 457.0 %copy-start = (f32[602]{0:T(1024)S(1)}, f32[602]{0:T(1024)}, u32[]{:S(2)}) copy-start(f32[602]{0:T(1024)} %param.26) | copy-start | bytes 7228

commit v6 on v5

--- a/solution.py
+++ b/solution.py
@@ -1218,7 +1218,6 @@
 
     d_pre = slope(0, d_out)
     d_pre_ref[...] = d_pre
-    carried[0]()
     d_self = right_flip(d_pre, mix[0, 0])
     d_neigh = right_flip(d_pre, mix[0, 1])
     g_in = left_flip(d_self, feats[...]) + left_flip(d_neigh, raw[...])
@@ -1230,35 +1229,35 @@
         every[0][where + (slice(head + block // 2, head + block), slice(0, wide_in - width))] = value.reshape(
             (far // 2, near, across, cores, block // 2, wide_in - width)
         )
-    carried[1]()
-    for turn in freed:
-        await_all(dims, at, turn)
+    await_all(dims, at, freed.pop(0))
     final = reduces[0]
     depth = block // 2
     order = [
-        Part(2 * piece + turned, piece, turned * depth, depth, piece * block + turned * depth, piece * block + turned * depth, turned == 1 and near == across)
-        for piece in (2, 0, 1)
+        Part(index + turned, piece, turned * depth, depth, kind * block + turned * depth, kind * block + turned * depth, turned == 1 and near == across)
+        for kind, piece, index in ((2, 0, 0), (0, 1, 4), (1, 2, 2))
         for turned in range(2)
     ]
-    for part in order[:2]:
-        final.core_stage(part)
+
+    def go(name, parts):
+        for part in parts:
+            getattr(final, name)(part)
+
+    go("core_stage", order[:2])
+    carried[0]()
     outers(0, d_pre)
-    for part in order[:2]:
-        final.across_stage(part)
+    go("across_stage", order[:2])
     weight_grads(0, 0)
-    for part in order[:2]:
-        final.near_stage(part)
+    go("near_stage", order[:2])
     weight_grads(0, 1)
-    for part in order[2:]:
-        final.core_stage(part)
-    for part in order[:2]:
-        final.line_stage(part)
-    for part in order[2:]:
-        final.across_stage(part)
-    for part in order[2:]:
-        final.near_stage(part)
-    for part in order[2:]:
-        final.line_stage(part)
+    go("core_stage", order[2:4])
+    carried[1]()
+    go("across_stage", order[2:4])
+    await_all(dims, at, freed.pop(0))
+    go("core_stage", order[4:])
+    go("line_stage", order[:2])
+    go("across_stage", order[4:])
+    go("near_stage", order[2:])
+    go("line_stage", order[2:])
     finish_reduce(0, order)
     note_head()
     sum_everywhere(stat)

time: 469 us -> 459 us (0.979)
  Pallas kernels: 453 us -> 442 us
    pallas_call x1, Pallas kernels: 450 us -> 439 us  [train_on_device(): pl.pallas_call(functools.partial(train_kernel, dims, in_width, classes),...]
where the time goes in v6:
time: 459 us; the launch traced here: 452 us
  Pallas kernels  442 us (96%)
    pallas_call x1, Pallas kernels, train_on_device(): pl.pallas_call(functools.partial(train_kernel, dims, in_width, classes),...  439 us

profile of v6, /device:TPU:0, one launch (start us, length us, event | category | flops | bytes accessed | tf_op | source)
XLA Modules:
  0.0 451.5 jit_solution(8467502592782643479)
XLA Ops:
  0.7 0.0 copy-start
  0.7 1.3 copy.35
  2.0 0.9 pad.12.feats
  2.9 0.9 convert_element_type.15
  3.8 0.7 convert_element_type.17
  4.5 0.7 add_divide_fusion
  5.2 0.2 select_select_fusion
  5.4 0.7 select_maximum_fusion.info
  6.1 1.4 pad.14.w_in_t
  7.5 439.2 %shard_map.304 = (f32[224,512]{1,0:T(8,128)}, f32[24,640]{1,0:T(8,128)}) custom-call(s32[1024,2048]{1,0:T(8,128)} %adj_hbm.1, f32[256,640]{1,0:T(8,128)} %pad.12.feats, f32[256,256]{1,0:T(8,128)} %select_maximum_fusion.info, f32[16,640]{1,0:T(8,128)} %pad.14.w_in_t, f32[3,32,512]{2,1,0:T(8,128)} %w_side.3, f32[3,32,512]{2,1,0:T(8,128)} %w_proj.3, ...), custom_call_target="tpu_custom_call" | custom-call | tf_op jit(solution)/shard_map/pallas_call | solution.py:1363
  446.7 0.0 copy-done
  446.7 0.6 broadcast_in_dim.48.row_in
  447.3 2.5 shard_map.305
  449.8 1.3 reduce
  (2 shorter events, 0.0 us)
Async XLA Ops:
  0.7 446.1 %copy-start = (f32[602]{0:T(1024)S(1)}, f32[602]{0:T(1024)}, u32[]{:S(2)}) copy-start(f32[602]{0:T(1024)} %param.26) | copy-start | bytes 7228
